TPU v7x, 32 devices: a whole 2x2x4 slice. The times are simulated.
32 devices in a mesh: dom: 4 (over y, x), orb: 8 (over z, core).
Axes of the slice: x: 2, y: 2, z: 4, core: 2. Of those that a mesh axis runs over, the one named last changes fastest.
Arguments:
- orbitals: float32 [128, 32, 16, 128], P('orb', 'dom'), may hold values from -6 to 6
- potential: float32 [32, 16, 128], P('dom'), may hold values from 0.2 to 17, as said below
- rotation: float32 [128, 128], P('orb'), may hold values from -0.6 to 0.6
- block: int32 [1], replicated, may hold values from 0 to 7
- owner: int32 [1], replicated, may hold values from 0 to 7
Outputs:
- gradient: float32 [16, 32, 16, 128], P(None, 'dom')
- updated: float32 [128, 32, 16, 128], P('orb', 'dom')
Inputs may be any that keep to these rules, and one draw needn't show every extreme that they name: A positive local potential.
All inputs are finite; a program needn't handle non-finite values.
Results may differ from a plain program's by a relative error of at most 0.00017.
Values sent between devices are 32-bit elements; how exact they have to be, the bound alone decides.
No kernel may reach another device: no remote copies, remote signals or barrier semaphores. Data moves between devices by JAX's collectives and lax.ppermute only.
A program may use at most 128 MiB of HBM per device.

v0:
```python
import functools

import jax
import jax.numpy as jnp
import numpy as np
from jax import lax
from jax.experimental import pallas as pl
from jax.experimental.pallas import tpu as pltpu
from jax.sharding import PartitionSpec as P

CENTER = -5369.0 / 1800.0
SIDES = (12.0 / 7.0, -15.0 / 56.0, 10.0 / 189.0, -1.0 / 112.0, 2.0 / 1925.0, -1.0 / 16632.0)
WIDTH = 6
CHUNKS = 4
MIX = 8
BF16 = jnp.bfloat16
VMEM = pl.BlockSpec(memory_space=pltpu.VMEM)
HBM = pl.BlockSpec(memory_space=pltpu.HBM)
SMEM = pl.BlockSpec(memory_space=pltpu.SMEM)


def params():
    return pltpu.CompilerParams(vmem_limit_bytes=32 * 1024 * 1024)


def plane_weights(planes, rows_y):
    cells = planes * rows_y
    table = np.zeros((3 * cells, cells), np.float64)
    skipped = (planes - WIDTH) * rows_y
    for x in range(planes):
        for y in range(rows_y):
            out = x * rows_y + y
            for k, weight in enumerate(SIDES, 1):
                for step in (k, -k):
                    table[2 * cells + x * rows_y + (y + step) % rows_y, out] += weight
                    row = (x + step) * rows_y + y
                    if row < 0:
                        table[cells + row - skipped, out] += weight
                    elif row >= cells:
                        table[row, out] += weight
                    else:
                        table[2 * cells + row, out] += weight
    table = -0.5 * table
    high = table.astype(BF16)
    return high, (table - high.astype(np.float64)).astype(BF16)


def split(value):
    high = value.astype(BF16)
    return high, (value - high.astype(jnp.float32)).astype(BF16)


def dot3(left, right, contract):
    dot = lambda x, y: lax.dot_general(x, y, (contract, ((), ())), preferred_element_type=jnp.float32)
    rows = left[0].shape[0]
    both = dot(jnp.concatenate(left, axis=0), right[0])
    return both[:rows] + (both[rows:] + dot(left[0], right[1]))


def pack_kernel(blocks, x_hbm, *refs):
    *t_refs, turned, x_ref, sems = refs
    count, _, rows_z = x_ref.shape
    chunks = sems.shape[0]
    per = count // chunks
    copies = [
        pltpu.make_async_copy(x_hbm.at[pl.ds(i * per, per)], x_ref.at[pl.ds(i * per, per)], sems.at[i])
        for i in range(chunks)
    ]
    for copy in copies:
        copy.start()
    for i, copy in enumerate(copies):
        copy.wait()
        for a in range(i * per, (i + 1) * per):
            turned[pl.ds(a, rows_z, stride=count), :] = x_ref[a].T
    rows = rows_z // blocks * count
    rank = lax.axis_index("orb")
    for m, t_ref in enumerate(t_refs):
        for core in range(2):
            start = pl.multiple_of((rank ^ (2 * m + core)) * rows, rows)
            t_ref[core] = turned[pl.ds(start, rows), :].reshape(t_ref.shape[1:])


def hand_kernel(block_ref, owner_ref, pair_ref, other_ref):
    other_ref[...] = pair_ref[1]


def by_block(refs):
    refs = refs[::-1]
    half = len(refs) // 2 - 1
    return [refs[half + k // 2] if k % 2 else refs[k // 2].at[0] for k in range(2 * half)] + list(refs[2 * half :])


def squeeze(value):
    rows, wide = value.shape
    quarter, free = rows // 4, wide // 4
    lane = lax.broadcasted_iota(jnp.int32, (quarter, wide), 1)
    rest = value[3 * quarter :]
    parts = []
    for j in range(3):
        moved = pltpu.roll(rest, (3 - j) * free, 1)
        parts.append(jnp.where(lane < 3 * free, value[j * quarter : (j + 1) * quarter], moved))
    return jnp.concatenate(parts, axis=0)


def expand(value):
    rows, wide = value.shape
    quarter, free = rows // 3, wide // 4
    lane = lax.broadcasted_iota(jnp.int32, (quarter, wide), 1)
    rest = value[:quarter]
    for j in range(3):
        moved = pltpu.roll(value[j * quarter : (j + 1) * quarter], (j + 1) * free, 1)
        rest = jnp.where((lane >= j * free) & (lane < (j + 1) * free), moved, rest)
    return jnp.concatenate([value, rest], axis=0)


def pick_kernel(block_ref, *refs):
    x_refs, (act_ref, near_ref, far_ref, first_ref, last_ref) = by_block(refs[:-5]), refs[-5:]
    slab, nb, cells = act_ref.shape
    rank = lax.axis_index("orb")
    for k, x_ref in enumerate(x_refs):
        @pl.when((rank ^ block_ref[0]) == k)
        def _(x_ref=x_ref):
            act_ref[...] = x_ref[...]
    odd = rank % 2
    near_ref[...] = act_ref[pl.ds((1 - odd) * (slab - WIDTH), WIDTH)]
    far_ref[...] = act_ref[pl.ds(odd * (slab - WIDTH), WIDTH)]
    flat = act_ref[...].reshape(slab * nb, cells)
    first_ref[...] = squeeze(flat)
    last_ref[...] = squeeze(pltpu.roll(flat, 3 * (cells // 4), 1))


def split_kernel(blocks, act_ref, v_ref, wh_ref, wl_ref, *refs):
    x_refs, (high_ref, low_ref, inner_ref, turned) = by_block(refs[:-4]), refs[-4:]
    slab, nb, cells = act_ref.shape
    rank = lax.axis_index("orb")
    for k, x_ref in enumerate(x_refs):
        rows = pl.ds(pl.multiple_of((rank ^ k) * nb, nb), nb)
        for z in range(slab):
            high, low = split(x_ref[z])
            high_ref[rows, z * cells : (z + 1) * cells] = high
            low_ref[rows, z * cells : (z + 1) * cells] = low
    turned[...] = v_ref[...].T
    mine = pl.ds(pl.multiple_of(rank * slab, slab), slab)
    act = act_ref[...]
    middle = slice(2 * cells, 3 * cells)
    inner = dot3(split(act.reshape(slab * nb, cells)), (wh_ref[middle], wl_ref[middle]), ((1,), (0,)))
    inner = inner.reshape(slab, nb, cells) + (turned[mine, :][:, None, :] - 1.5 * CENTER) * act
    edge = jnp.zeros((WIDTH, nb, cells), jnp.float32)
    tall = jnp.concatenate([edge, act, edge], axis=0)
    for k, weight in enumerate(SIDES, 1):
        upper = tall[WIDTH + k : WIDTH + k + slab]
        lower = tall[WIDTH - k : WIDTH - k + slab]
        inner = inner + (-0.5 * weight) * (upper + lower)
    inner_ref[...] = inner


def project_kernel(
    volume, owner_ref, rot_ref, xh_ref, xl_ref, inner_ref, near_ref, far_ref, xb_ref, xa_ref, wh_ref, wl_ref,
    a_ref, p_ref, around,
):
    slab, nb, cells = inner_ref.shape
    rank = lax.axis_index("orb")
    odd = rank % 2
    around[1 - odd] = near_ref[...]
    around[odd] = far_ref[...]
    beside = slice(0, 2 * cells)
    wide = jnp.concatenate([expand(xb_ref[...]), expand(xa_ref[...])], axis=1)
    applied = dot3(split(wide), (wh_ref[beside], wl_ref[beside]), ((1,), (0,)))
    a_ref[...] = inner_ref[...] + applied.reshape(slab, nb, cells)
    for z in range(WIDTH):
        below, above = a_ref[z], a_ref[slab - 1 - z]
        for k in range(z + 1, WIDTH + 1):
            below = below + (-0.5 * SIDES[k - 1]) * around[0, WIDTH + z - k]
            above = above + (-0.5 * SIDES[k - 1]) * around[1, k - 1 - z]
        a_ref[z] = below
        a_ref[slab - 1 - z] = above
    flat = jnp.concatenate([a_ref[z] for z in range(slab)], axis=1)
    total = dot3(split(flat), (xh_ref[...], xl_ref[...]), ((1,), (1,)))
    p_ref[:nb] = total * volume
    p_ref[nb:] = jnp.where(rank == owner_ref[0], rot_ref[...], 0.0)


def remove_kernel(xh_ref, xl_ref, a_ref, *refs):
    *p_refs, g_ref = refs
    slab, nb, cells = a_ref.shape
    removed = dot3(split(total(p_refs, 0, nb)), (xh_ref[...], xl_ref[...]), ((1,), (0,)))
    for z in range(slab):
        g_ref[z] = a_ref[z] - removed[:, z * cells : (z + 1) * cells]


def mixing_kernel(nb, *refs):
    *p_refs, high_ref, low_ref = refs
    size, wide = high_ref.shape[0], p_refs[0].shape[1]
    row, col = (lax.broadcasted_iota(jnp.int32, (size, wide), axis) for axis in (0, 1))
    mine = jnp.where(col == lax.axis_index("orb") * nb + row % nb, 1.0, 0.0).astype(BF16)
    orbital, col = (lax.broadcasted_iota(jnp.int32, (nb, size), axis) for axis in (0, 1))
    repeat = jnp.where(orbital == col % nb, 1.0, 0.0).astype(BF16)
    row, col = (lax.broadcasted_iota(jnp.int32, (size, size), axis) for axis in (0, 1))
    same = row // nb == col // nb
    dot = lambda x, y, axes: lax.dot_general(x, y, (axes, ((), ())), preferred_element_type=jnp.float32)
    for part, ref in zip(split(total(p_refs, nb, nb)), (high_ref, low_ref)):
        block = dot(mine, part, ((1,), (1,))).astype(BF16)
        ref[...] = jnp.where(same, dot(block, repeat, ((1,), (0,))), 0.0).astype(BF16)


def update_kernel(blocks, sequence, wh_ref, wl_ref, x_ref, *refs):
    g_refs, (grad_hbm, out_hbm, whole, grad, mixed, added, out, sems) = refs[:blocks], refs[blocks:]
    nb, cells, rows_z = x_ref.shape
    rank = lax.axis_index("orb")
    share = rows_z // blocks * nb
    for k, g_ref in zip(sequence, g_refs):
        at = pl.ds(pl.multiple_of((rank ^ k) * share, share), share)
        whole[at, :] = g_ref[...].reshape(share, cells)
    per = nb // CHUNKS
    copies = []
    for i in range(CHUNKS):
        for c in range(i * per, (i + 1) * per):
            plane = whole[pl.ds(c, rows_z, stride=nb), :].T
            grad[c] = plane
            mixed[pl.ds(c, cells, stride=nb), :] = plane
        part = pl.ds(i * per, per)
        copies.append(pltpu.make_async_copy(grad.at[part], grad_hbm.at[part], sems.at[0, i]))
        copies[-1].start()
    size = wh_ref.shape[0]
    mix = (wh_ref[...], wl_ref[...])
    rows = cells // CHUNKS
    tall = rows * nb
    for i in range(CHUNKS):
        parts = split(mixed[i * tall : (i + 1) * tall])
        sides = [jnp.concatenate([p[j : j + size] for j in range(0, tall, size)], axis=1) for p in parts]
        result = dot3(mix, sides, ((1,), (0,)))
        for j in range(tall // size):
            added[i * tall + j * size : i * tall + (j + 1) * size] = result[:, j * rows_z : (j + 1) * rows_z]
        some = pl.ds(i * rows, rows)
        for a in range(nb):
            out[a, some] = x_ref[a, some] + added[pl.ds(i * tall + a, rows, stride=nb), :]
        copies.append(pltpu.make_async_copy(out.at[:, some], out_hbm.at[:, some], sems.at[1, i]))
        copies[-1].start()
    for copy in copies:
        copy.wait()


def swap(value, axis, k):
    count = lax.axis_size(axis)
    return lax.ppermute(value, axis, [(i, i ^ k) for i in range(count)])


def dom_kernel(value_ref, *refs):
    *other_refs, out_ref = refs
    nb = other_refs[0].shape[0]
    out_ref[:nb] = value_ref[:nb] + sum(ref[...] for ref in other_refs)
    out_ref[nb:] = value_ref[nb:]


def total(refs, first, count):
    rows = slice(first, first + count)
    return sum(ref[rows] for ref in refs)


def per_device(orbitals, potential, rotation, block, owner):
    nb, planes, rows_y, rows_z = orbitals.shape
    blocks, doms = lax.axis_size("orb"), lax.axis_size("dom")
    cells = planes * rows_y
    slab = rows_z // blocks
    volume = 1.0 / (cells * doms * rows_z)
    f32 = jnp.float32
    shape = lambda *dims: jax.ShapeDtypeStruct(dims, f32)
    piece, edge = shape(slab, nb, cells), shape(WIDTH, nb, cells)

    flat = orbitals.reshape(nb, cells, rows_z)
    held = pltpu.with_memory_space_constraint(flat, pltpu.HBM)
    chips = half = blocks // 2
    pieces = pl.pallas_call(
        functools.partial(pack_kernel, blocks),
        out_shape=[shape(2, slab, nb, cells)] * chips,
        in_specs=[HBM],
        out_specs=[VMEM] * chips,
        scratch_shapes=[
            pltpu.VMEM(((rows_z + 1) * nb, cells), f32),
            pltpu.VMEM((nb, cells, rows_z), f32),
            pltpu.SemaphoreType.DMA((CHUNKS,)),
        ],
        compiler_params=params(),
        name="pack",
    )(held)
    last = 2 * (chips - 1)
    pairs = [swap(value, "orb", 2 * m) if m else value for m, value in enumerate(pieces[:-1])]
    direct = [swap(pieces[-1][core], "orb", last + core) for core in range(2)]
    nearest = pl.pallas_call(
        hand_kernel,
        out_shape=piece,
        in_specs=[SMEM, SMEM, VMEM],
        out_specs=VMEM,
        compiler_params=params(),
        name="hand",
    )(block, owner, pairs[1])
    others = [nearest if m == 1 else value[1] for m, value in enumerate(pairs)]
    spread = (pairs + [swap(value, "orb", 1) for value in others] + direct)[::-1]

    side = shape(3 * slab * nb // 4, cells)
    active, near, far, first, last = pl.pallas_call(
        pick_kernel,
        out_shape=(piece, edge, edge, side, side),
        in_specs=[SMEM] + [VMEM] * len(spread),
        out_specs=[VMEM] * 5,
        compiler_params=params(),
        name="pick",
    )(block, *spread)

    up = lambda count: [(i, (i + 1) % count) for i in range(count)]
    down = lambda count: [(i, (i - 1) % count) for i in range(count)]
    x_before = lax.ppermute(last, "dom", up(doms))
    x_after = lax.ppermute(first, "dom", down(doms))
    z_near = swap(near, "orb", 1)
    z_far = lax.ppermute(far, "orb", [(o, (o + 2 * (o % 2) - 1) % blocks) for o in range(blocks)])

    halves = jax.ShapeDtypeStruct((blocks * nb, slab * cells), BF16)
    weights = [jnp.asarray(w) for w in plane_weights(planes, rows_y)]
    *parts, inner = pl.pallas_call(
        functools.partial(split_kernel, blocks),
        out_shape=(halves, halves, piece),
        in_specs=[VMEM] * (len(spread) + 4),
        out_specs=(VMEM, VMEM, VMEM),
        scratch_shapes=[pltpu.VMEM((rows_z, cells), f32)],
        compiler_params=params(),
        cost_estimate=pl.CostEstimate(flops=3 * blocks * nb * slab * cells, bytes_accessed=0, transcendentals=0),
        name="split",
    )(active, potential.reshape(cells, rows_z), *weights, *spread)

    applied, part = pl.pallas_call(
        functools.partial(project_kernel, volume),
        out_shape=(piece, shape(2 * nb, blocks * nb)),
        in_specs=[SMEM] + [VMEM] * 10,
        out_specs=(VMEM, VMEM),
        scratch_shapes=[pltpu.VMEM((2, WIDTH, nb, cells), f32)],
        compiler_params=params(),
        name="project",
    )(owner, rotation, *parts, inner, z_near, z_far, x_before, x_after, *weights)

    part = part + swap(part, "orb", 1)
    part = pl.pallas_call(
        dom_kernel,
        out_shape=shape(2 * nb, blocks * nb),
        in_specs=[VMEM] * doms,
        out_specs=VMEM,
        compiler_params=params(),
        name="dom",
    )(part, *[swap(part[:nb], "dom", k) for k in range(1, doms)])
    sums = [part] + [swap(part, "orb", k) for k in range(2, blocks, 2)]

    own = pl.pallas_call(
        remove_kernel,
        out_shape=piece,
        in_specs=[VMEM] * (3 + chips),
        out_specs=VMEM,
        compiler_params=params(),
        name="remove",
    )(*parts, applied, *sums)

    gathered = [own] + [None] * (blocks - 1)
    for k in range(2, blocks, 2):
        gathered[k] = swap(own, "orb", k)
    for k in range(0, blocks, 2):
        gathered[k + 1] = swap(gathered[k], "orb", 1)

    square = jax.ShapeDtypeStruct((MIX * nb, MIX * nb), BF16)
    mixing = pl.pallas_call(
        functools.partial(mixing_kernel, nb),
        out_shape=(square, square),
        in_specs=[VMEM] * chips,
        out_specs=(VMEM, VMEM),
        compiler_params=params(),
        name="mixing",
    )(*sums)

    sequence = sorted(range(blocks), key=lambda k: (k >= half, -k if k >= half else k))
    gradient, updated = pl.pallas_call(
        functools.partial(update_kernel, blocks, sequence),
        out_shape=(shape(nb, cells, rows_z), shape(nb, cells, rows_z)),
        in_specs=[VMEM] * (3 + blocks),
        out_specs=(HBM, HBM),
        scratch_shapes=[
            pltpu.VMEM(((rows_z + 1) * nb, cells), f32),
            pltpu.VMEM((nb, cells, rows_z), f32),
            pltpu.VMEM(((cells + 1) * nb, rows_z), f32),
            pltpu.VMEM(((cells + 1) * nb, rows_z), f32),
            pltpu.VMEM((nb, cells, rows_z), f32),
            pltpu.SemaphoreType.DMA((2, CHUNKS)),
        ],
        compiler_params=params(),
        name="update",
    )(*mixing, flat, *[gathered[k] for k in sequence])
    return gradient.reshape(orbitals.shape), updated.reshape(orbitals.shape)


def solution(mesh):
    in_specs = (P("orb", "dom", None, None), P("dom", None, None), P("orb", None), P(), P())
    out_specs = (P(None, "dom", None, None), P("orb", "dom", None, None))
    return jax.shard_map(
        per_device, mesh=mesh, in_specs=in_specs, out_specs=out_specs, check_vma=False
    )
```

profile of v0, /device:TPU:0, one launch (start us, length us, event | category | flops | bytes accessed | tf_op | source)
XLA Modules:
  0.0 67.4 jit_solution(4831491500707630678)
XLA Ops:
  0.6 1.7 %pack.1 = (f32[2,16,16,128]{3,2,1,0:T(8,128)S(1)}, f32[2,16,16,128]{3,2,1,0:T(8,128)S(1)}, f32[2,16,16,128]{3,2,1,0:T(8,128)S(1)}, f32[2,16,16,128]{3,2,1,0:T(8,128)S(1)}) custom-call(f32[16,128,128]{2,1,0:T(8,128)} %bitcast.12), custom_call_target="tpu_custom_call" | custom-call | tf_op jit(solution)/shard_map/pack/pallas_call | solution.py:273
  2.3 4.1 %collective-permute-start.2 = (f32[2,16,16,128]{3,2,1,0:T(8,128)S(1)}, f32[2,16,16,128]{3,2,1,0:T(8,128)S(1)}, u32[]{:S(2)}, u32[]{:S(2)}) collective-permute-start(f32[2,16,16,128]{3,2,1,0:T(8,128)S(1)} %get-tuple-element.21), channel_id=1, source_target_pairs={{0,4},{1,5},{2,6},{3,7},{4,0},{5,1},{6,2},{7,3},{8,12},{9,13},{10,... | collective-permute-start | bytes 786440 | tf_op jit(solution)/shard_map/ppermute | solution.py:245
  6.5 1.6 %collective-permute-start.4 = (f32[2,16,16,128]{3,2,1,0:T(8,128)S(1)}, f32[2,16,16,128]{3,2,1,0:T(8,128)S(1)}, u32[]{:S(2)}, u32[]{:S(2)}) collective-permute-start(f32[2,16,16,128]{3,2,1,0:T(8,128)S(1)} %get-tuple-element.22), channel_id=1, source_target_pairs={{0,2},{1,3},{2,0},{3,1},{4,6},{5,7},{6,4},{7,5},{8,10},{9,11},{10,... | collective-permute-start | bytes 786440 | tf_op jit(solution)/shard_map/ppermute | solution.py:245
  8.2 3.3 %collective-permute-start = (f32[16,16,128]{2,1,0:T(8,128)S(1)}, f32[16,16,128]{2,1,0:T(8,128)S(1)}, u32[]{:S(2)}, u32[]{:S(2)}) collective-permute-start(f32[16,16,128]{2,1,0:T(8,128)S(1)} %get-tuple-element.39), channel_id=1, source_target_pairs={{0,7},{1,6},{2,5},{3,4},{4,3},{5,2},{6,1},{7,0},{8,15},{9,14},{10,... | collective-permute-start | bytes 393224 | tf_op jit(solution)/shard_map/ppermute | solution.py:245
  12.8 7.2 %collective-permute-done.2.refs_5_ = f32[2,16,16,128]{3,2,1,0:T(8,128)S(1)} collective-permute-done((f32[2,16,16,128]{3,2,1,0:T(8,128)S(1)}, f32[2,16,16,128]{3,2,1,0:T(8,128)S(1)}, u32[]{:S(2)}, u32[]{:S(2)}) %collective-permute-start.2) | collective-permute-done | bytes 262176 | tf_op jit(solution)/shard_map/ppermute | solution.py:245
  20.1 5.1 %collective-permute-done.4.pair_ref.refs_6_ = f32[2,16,16,128]{3,2,1,0:T(8,128)S(1)} collective-permute-done((f32[2,16,16,128]{3,2,1,0:T(8,128)S(1)}, f32[2,16,16,128]{3,2,1,0:T(8,128)S(1)}, u32[]{:S(2)}, u32[]{:S(2)}) %collective-permute-start.4) | collective-permute-done | bytes 262176 | tf_op jit(solution)/shard_map/ppermute | solution.py:245
  25.4 1.3 %collective-permute-done.5.refs_3_ = f32[16,16,128]{2,1,0:T(8,128)S(1)} collective-permute-done((f32[16,16,128]{2,1,0:T(8,128)S(1)}, f32[16,16,128]{2,1,0:T(8,128)S(1)}, u32[]{:S(2)}, u32[]{:S(2)}) %collective-permute-start.5) | collective-permute-done | bytes 131104 | tf_op jit(solution)/shard_map/ppermute | solution.py:245
  27.0 1.7 %collective-permute-start.9 = (f32[192,128]{1,0:T(8,128)S(1)}, f32[192,128]{1,0:T(8,128)S(1)}, u32[]{:S(2)}, u32[]{:S(2)}) collective-permute-start(f32[192,128]{1,0:T(8,128)S(1)} %get-tuple-element.30), channel_id=1, source_target_pairs={{0,8},{8,16},{16,24},{24,0},{1,9},{9,17},{17,25},{25,1},{2,10},{10... | collective-permute-start | bytes 294920 | tf_op jit(solution)/shard_map/ppermute | solution.py:312
  28.7 1.3 %collective-permute-start.10 = (f32[192,128]{1,0:T(8,128)S(1)}, f32[192,128]{1,0:T(8,128)S(1)}, u32[]{:S(2)}, u32[]{:S(2)}) collective-permute-start(f32[192,128]{1,0:T(8,128)S(1)} %get-tuple-element.31), channel_id=1, source_target_pairs={{0,24},{8,0},{16,8},{24,16},{1,25},{9,1},{17,9},{25,17},{2,26},{10... | collective-permute-start | bytes 294920 | tf_op jit(solution)/shard_map/ppermute | solution.py:313
  29.9 2.6 %collective-permute-start.8 = (f32[6,16,128]{2,1,0:T(8,128)S(1)}, f32[6,16,128]{2,1,0:T(8,128)S(1)}, u32[]{:S(2)}, u32[]{:S(2)}) collective-permute-start(f32[6,16,128]{2,1,0:T(8,128)S(1)} %get-tuple-element.29), channel_id=1, source_target_pairs={{0,7},{1,2},{2,1},{3,4},{4,3},{5,6},{6,5},{7,0},{8,15},{9,10},{10,... | collective-permute-start | bytes 147464 | tf_op jit(solution)/shard_map/ppermute | solution.py:315
  32.5 0.4 split.1
  33.0 2.3 %collective-permute-done.8.far_ref = f32[6,16,128]{2,1,0:T(8,128)S(1)} collective-permute-done((f32[6,16,128]{2,1,0:T(8,128)S(1)}, f32[6,16,128]{2,1,0:T(8,128)S(1)}, u32[]{:S(2)}, u32[]{:S(2)}) %collective-permute-start.8) | collective-permute-done | bytes 49184 | tf_op jit(solution)/shard_map/ppermute | solution.py:315
  35.3 0.8 %project.1 = (f32[16,16,128]{2,1,0:T(8,128)S(1)}, f32[32,128]{1,0:T(8,128)S(1)}) custom-call(s32[1]{0:T(128)S(6)} %copy.10.owner_ref, f32[16,128]{1,0:T(8,128)S(1)} %copy-done.4, bf16[128,2048]{1,0:T(8,128)(2,1)S(1)} %get-tuple-element.25.xh_ref, bf16[128,2048]{1,0:T(8,128)(2,1)S(1)} %get-tuple-element.26.xl_ref, ...), custom_call_target="tpu_custom_call" | custom-call | tf_op jit(solution)/shard_map/project/pallas_call | solution.py:330
  36.4 0.9 %collective-permute-done.11 = f32[32,128]{1,0:T(8,128)S(1)} collective-permute-done((f32[32,128]{1,0:T(8,128)S(1)}, f32[32,128]{1,0:T(8,128)S(1)}, u32[]{:S(2)}, u32[]{:S(2)}) %collective-permute-start.11) | collective-permute-done | bytes 16416 | tf_op jit(solution)/shard_map/ppermute | solution.py:245
  37.3 1.7 %collective-permute-start.14 = (f32[16,128]{1,0:T(8,128)S(1)}, f32[16,128]{1,0:T(8,128)S(1)}, u32[]{:S(2)}, u32[]{:S(2)}) collective-permute-start(f32[16,128]{1,0:T(8,128)S(1)} %slice.23), channel_id=1, source_target_pairs={{0,24},{8,16},{16,8},{24,0},{1,25},{9,17},{17,9},{25,1},{2,26},{10... | collective-permute-start | bytes 24584 | tf_op jit(solution)/shard_map/ppermute | solution.py:245
  39.0 1.2 %collective-permute-start.13 = (f32[16,128]{1,0:T(8,128)S(1)}, f32[16,128]{1,0:T(8,128)S(1)}, u32[]{:S(2)}, u32[]{:S(2)}) collective-permute-start(f32[16,128]{1,0:T(8,128)S(1)} %slice.23), channel_id=1, source_target_pairs={{0,16},{8,24},{16,0},{24,8},{1,17},{9,25},{17,1},{25,9},{2,18},{10... | collective-permute-start | bytes 24584 | tf_op jit(solution)/shard_map/ppermute | solution.py:245
  40.3 0.5 collective-permute-start.12
  40.8 1.1 %collective-permute-done.14.refs_2_ = f32[16,128]{1,0:T(8,128)S(1)} collective-permute-done((f32[16,128]{1,0:T(8,128)S(1)}, f32[16,128]{1,0:T(8,128)S(1)}, u32[]{:S(2)}, u32[]{:S(2)}) %collective-permute-start.14) | collective-permute-done | bytes 8224 | tf_op jit(solution)/shard_map/ppermute | solution.py:245
  41.9 0.8 %collective-permute-done.13.refs_1_ = f32[16,128]{1,0:T(8,128)S(1)} collective-permute-done((f32[16,128]{1,0:T(8,128)S(1)}, f32[16,128]{1,0:T(8,128)S(1)}, u32[]{:S(2)}, u32[]{:S(2)}) %collective-permute-start.13) | collective-permute-done | bytes 8224 | tf_op jit(solution)/shard_map/ppermute | solution.py:245
  42.7 1.2 %collective-permute-done.12.refs_0_ = f32[16,128]{1,0:T(8,128)S(1)} collective-permute-done((f32[16,128]{1,0:T(8,128)S(1)}, f32[16,128]{1,0:T(8,128)S(1)}, u32[]{:S(2)}, u32[]{:S(2)}) %collective-permute-start.12) | collective-permute-done | bytes 8224 | tf_op jit(solution)/shard_map/ppermute | solution.py:245
  43.9 2.8 %collective-permute-start.17 = (f32[32,128]{1,0:T(8,128)S(1)}, f32[32,128]{1,0:T(8,128)S(1)}, u32[]{:S(2)}, u32[]{:S(2)}) collective-permute-start(f32[32,128]{1,0:T(8,128)S(1)} %dom.1.refs_0_), channel_id=1, source_target_pairs={{0,6},{1,7},{2,4},{3,5},{4,2},{5,3},{6,0},{7,1},{8,14},{9,15},{10,... | collective-permute-start | bytes 49160 | tf_op jit(solution)/shard_map/ppermute | solution.py:245
  46.7 2.3 %collective-permute-start.16 = (f32[32,128]{1,0:T(8,128)S(1)}, f32[32,128]{1,0:T(8,128)S(1)}, u32[]{:S(2)}, u32[]{:S(2)}) collective-permute-start(f32[32,128]{1,0:T(8,128)S(1)} %dom.1.refs_0_), channel_id=1, source_target_pairs={{0,4},{1,5},{2,6},{3,7},{4,0},{5,1},{6,2},{7,3},{8,12},{9,13},{10,... | collective-permute-start | bytes 49160 | tf_op jit(solution)/shard_map/ppermute | solution.py:245
  49.0 0.5 collective-permute-start.15
  49.5 1.9 %collective-permute-done.16.refs_2_ = f32[32,128]{1,0:T(8,128)S(1)} collective-permute-done((f32[32,128]{1,0:T(8,128)S(1)}, f32[32,128]{1,0:T(8,128)S(1)}, u32[]{:S(2)}, u32[]{:S(2)}) %collective-permute-start.16) | collective-permute-done | bytes 16416 | tf_op jit(solution)/shard_map/ppermute | solution.py:245
  51.3 1.4 %collective-permute-done.15.refs_1_ = f32[32,128]{1,0:T(8,128)S(1)} collective-permute-done((f32[32,128]{1,0:T(8,128)S(1)}, f32[32,128]{1,0:T(8,128)S(1)}, u32[]{:S(2)}, u32[]{:S(2)}) %collective-permute-start.15) | collective-permute-done | bytes 16416 | tf_op jit(solution)/shard_map/ppermute | solution.py:245
  52.9 1.6 %collective-permute-start.23 = (f32[16,16,128]{2,1,0:T(8,128)S(1)}, f32[16,16,128]{2,1,0:T(8,128)S(1)}, u32[]{:S(2)}, u32[]{:S(2)}) collective-permute-start(f32[16,16,128]{2,1,0:T(8,128)S(1)} %remove.1.refs_0_), channel_id=1, source_target_pairs={{0,4},{1,5},{2,6},{3,7},{4,0},{5,1},{6,2},{7,3},{8,12},{9,13},{10,... | collective-permute-start | bytes 393224 | tf_op jit(solution)/shard_map/ppermute | solution.py:245
  54.6 2.2 %collective-permute-start.21 = (f32[16,16,128]{2,1,0:T(8,128)S(1)}, f32[16,16,128]{2,1,0:T(8,128)S(1)}, u32[]{:S(2)}, u32[]{:S(2)}) collective-permute-start(f32[16,16,128]{2,1,0:T(8,128)S(1)} %remove.1.refs_0_), channel_id=1, source_target_pairs={{0,6},{1,7},{2,4},{3,5},{4,2},{5,3},{6,0},{7,1},{8,14},{9,15},{10,... | collective-permute-start | bytes 393224 | tf_op jit(solution)/shard_map/ppermute | solution.py:245
  56.8 6.4 %collective-permute-done.23.refs_7_ = f32[16,16,128]{2,1,0:T(8,128)S(1)} collective-permute-done((f32[16,16,128]{2,1,0:T(8,128)S(1)}, f32[16,16,128]{2,1,0:T(8,128)S(1)}, u32[]{:S(2)}, u32[]{:S(2)}) %collective-permute-start.23) | collective-permute-done | bytes 131104 | tf_op jit(solution)/shard_map/ppermute | solution.py:245
  63.2 0.5 collective-permute-start.22
  63.8 0.4 mixing.1
  64.7 0.5 collective-permute-done.20.refs_3_
  65.2 2.3 %update.1 = (f32[16,128,128]{2,1,0:T(8,128)}, f32[16,128,128]{2,1,0:T(8,128)}) custom-call(bf16[128,128]{1,0:T(8,128)(2,1)S(1)} %get-tuple-element.33.wh_ref, bf16[128,128]{1,0:T(8,128)(2,1)S(1)} %get-tuple-element.34.wl_ref, f32[16,128,128]{2,1,0:T(8,128)S(1)} %bitcast.13, f32[16,16,128]{2,1,0:T(8,128)S(1)} %remove.1.refs_0_, ...), custom_call_target="tpu_custom_call" | custom-call | tf_op jit(solution)/shard_map/update/pallas_call | solution.py:377
  (42 shorter events, 1.8 us)
Async XLA Ops:
  2.3 17.8 %collective-permute-start.2 = (f32[2,16,16,128]{3,2,1,0:T(8,128)S(1)}, f32[2,16,16,128]{3,2,1,0:T(8,128)S(1)}, u32[]{:S(2)}, u32[]{:S(2)}) collective-permute-start(f32[2,16,16,128]{3,2,1,0:T(8,128)S(1)} %get-tuple-element.21), channel_id=1, source_target_pairs={{0,4},{1,5},{2,6},{3,7},{4,0},{5,1},{6,2},{7,3},{8,12},{9,13},{10,... | collective-permute-start | bytes 786440 | tf_op jit(solution)/shard_map/ppermute | solution.py:245
  6.4 19.0 %collective-permute-start.6 = (f32[16,16,128]{2,1,0:T(8,128)S(1)}, f32[16,16,128]{2,1,0:T(8,128)S(1)}, u32[]{:S(2)}, u32[]{:S(2)}) collective-permute-start(f32[16,16,128]{2,1,0:T(8,128)S(1)} %slice_bitcast_fusion.1), channel_id=1, source_target_pairs={{0,1},{1,0},{2,3},{3,2},{4,5},{5,4},{6,7},{7,6},{8,9},{9,8},{10,11... | collective-permute-start | bytes 393224 | tf_op jit(solution)/shard_map/ppermute | solution.py:245
  6.5 18.8 %collective-permute-start.4 = (f32[2,16,16,128]{3,2,1,0:T(8,128)S(1)}, f32[2,16,16,128]{3,2,1,0:T(8,128)S(1)}, u32[]{:S(2)}, u32[]{:S(2)}) collective-permute-start(f32[2,16,16,128]{3,2,1,0:T(8,128)S(1)} %get-tuple-element.22), channel_id=1, source_target_pairs={{0,2},{1,3},{2,0},{3,1},{4,6},{5,7},{6,4},{7,5},{8,10},{9,11},{10,... | collective-permute-start | bytes 786440 | tf_op jit(solution)/shard_map/ppermute | solution.py:245
  8.1 17.3 %collective-permute-start.1 = (f32[16,16,128]{2,1,0:T(8,128)S(1)}, f32[16,16,128]{2,1,0:T(8,128)S(1)}, u32[]{:S(2)}, u32[]{:S(2)}) collective-permute-start(f32[16,16,128]{2,1,0:T(8,128)S(1)} %get-tuple-element.38), channel_id=1, source_target_pairs={{0,6},{1,7},{2,4},{3,5},{4,2},{5,3},{6,0},{7,1},{8,14},{9,15},{10,... | collective-permute-start | bytes 393224 | tf_op jit(solution)/shard_map/ppermute | solution.py:245
  8.2 17.2 %collective-permute-start = (f32[16,16,128]{2,1,0:T(8,128)S(1)}, f32[16,16,128]{2,1,0:T(8,128)S(1)}, u32[]{:S(2)}, u32[]{:S(2)}) collective-permute-start(f32[16,16,128]{2,1,0:T(8,128)S(1)} %get-tuple-element.39), channel_id=1, source_target_pairs={{0,7},{1,6},{2,5},{3,4},{4,3},{5,2},{6,1},{7,0},{8,15},{9,14},{10,... | collective-permute-start | bytes 393224 | tf_op jit(solution)/shard_map/ppermute | solution.py:245
  20.1 5.4 %collective-permute-start.3 = (f32[16,16,128]{2,1,0:T(8,128)S(1)}, f32[16,16,128]{2,1,0:T(8,128)S(1)}, u32[]{:S(2)}, u32[]{:S(2)}) collective-permute-start(f32[16,16,128]{2,1,0:T(8,128)S(1)} %slice_bitcast_fusion), channel_id=1, source_target_pairs={{0,1},{1,0},{2,3},{3,2},{4,5},{5,4},{6,7},{7,6},{8,9},{9,8},{10,11... | collective-permute-start | bytes 393224 | tf_op jit(solution)/shard_map/ppermute | solution.py:245
  25.3 7.2 %copy-start.1 = (bf16[384,128]{1,0:T(8,128)(2,1)S(1)}, bf16[384,128]{1,0:T(8,128)(2,1)}, u32[]{:S(2)}) copy-start(bf16[384,128]{1,0:T(8,128)(2,1)} %constant.5.clone.wl_ref) | copy-start | bytes 294916
  25.3 7.2 %copy-start.2 = (bf16[384,128]{1,0:T(8,128)(2,1)S(1)}, bf16[384,128]{1,0:T(8,128)(2,1)}, u32[]{:S(2)}) copy-start(bf16[384,128]{1,0:T(8,128)(2,1)} %constant.4.clone.wh_ref) | copy-start | bytes 294916
  25.3 7.2 %copy-start.3 = (f32[8,16,128]{2,1,0:T(8,128)S(1)}, f32[8,16,128]{2,1,0:T(8,128)}, u32[]{:S(2)}) copy-start(f32[8,16,128]{2,1,0:T(8,128)} %param.8) | copy-start | bytes 196612
  25.3 1.4 %collective-permute-start.5 = (f32[16,16,128]{2,1,0:T(8,128)S(1)}, f32[16,16,128]{2,1,0:T(8,128)S(1)}, u32[]{:S(2)}, u32[]{:S(2)}) collective-permute-start(f32[16,16,128]{2,1,0:T(8,128)S(1)} %hand.1), channel_id=1, source_target_pairs={{0,1},{1,0},{2,3},{3,2},{4,5},{5,4},{6,7},{7,6},{8,9},{9,8},{10,11... | collective-permute-start | bytes 393224 | tf_op jit(solution)/shard_map/ppermute | solution.py:245
  27.0 8.3 %collective-permute-start.9 = (f32[192,128]{1,0:T(8,128)S(1)}, f32[192,128]{1,0:T(8,128)S(1)}, u32[]{:S(2)}, u32[]{:S(2)}) collective-permute-start(f32[192,128]{1,0:T(8,128)S(1)} %get-tuple-element.30), channel_id=1, source_target_pairs={{0,8},{8,16},{16,24},{24,0},{1,9},{9,17},{17,25},{25,1},{2,10},{10... | collective-permute-start | bytes 294920 | tf_op jit(solution)/shard_map/ppermute | solution.py:312
  28.7 6.6 %collective-permute-start.10 = (f32[192,128]{1,0:T(8,128)S(1)}, f32[192,128]{1,0:T(8,128)S(1)}, u32[]{:S(2)}, u32[]{:S(2)}) collective-permute-start(f32[192,128]{1,0:T(8,128)S(1)} %get-tuple-element.31), channel_id=1, source_target_pairs={{0,24},{8,0},{16,8},{24,16},{1,25},{9,1},{17,9},{25,17},{2,26},{10... | collective-permute-start | bytes 294920 | tf_op jit(solution)/shard_map/ppermute | solution.py:313
  29.9 3.0 %collective-permute-start.7 = (f32[6,16,128]{2,1,0:T(8,128)S(1)}, f32[6,16,128]{2,1,0:T(8,128)S(1)}, u32[]{:S(2)}, u32[]{:S(2)}) collective-permute-start(f32[6,16,128]{2,1,0:T(8,128)S(1)} %get-tuple-element.28), channel_id=1, source_target_pairs={{0,1},{1,0},{2,3},{3,2},{4,5},{5,4},{6,7},{7,6},{8,9},{9,8},{10,11... | collective-permute-start | bytes 147464 | tf_op jit(solution)/shard_map/ppermute | solution.py:245
  29.9 5.3 %collective-permute-start.8 = (f32[6,16,128]{2,1,0:T(8,128)S(1)}, f32[6,16,128]{2,1,0:T(8,128)S(1)}, u32[]{:S(2)}, u32[]{:S(2)}) collective-permute-start(f32[6,16,128]{2,1,0:T(8,128)S(1)} %get-tuple-element.29), channel_id=1, source_target_pairs={{0,7},{1,2},{2,1},{3,4},{4,3},{5,6},{6,5},{7,0},{8,15},{9,10},{10,... | collective-permute-start | bytes 147464 | tf_op jit(solution)/shard_map/ppermute | solution.py:315
  32.5 2.7 %copy-start.4 = (f32[16,128]{1,0:T(8,128)S(1)}, f32[16,128]{1,0:T(8,128)}, u32[]{:S(2)}) copy-start(f32[16,128]{1,0:T(8,128)} %rot_ref.1) | copy-start | bytes 24580
  36.1 29.1 %copy-start = (f32[16,8,16,128]{3,2,1,0:T(8,128)S(1)}, f32[16,8,16,128]{3,2,1,0:T(8,128)}, u32[]{:S(2)}) copy-start(f32[16,8,16,128]{3,2,1,0:T(8,128)} %param.7) | copy-start | bytes 3145732
  36.1 1.2 %collective-permute-start.11 = (f32[32,128]{1,0:T(8,128)S(1)}, f32[32,128]{1,0:T(8,128)S(1)}, u32[]{:S(2)}, u32[]{:S(2)}) collective-permute-start(f32[32,128]{1,0:T(8,128)S(1)} %get-tuple-element.32), channel_id=1, source_target_pairs={{0,1},{1,0},{2,3},{3,2},{4,5},{5,4},{6,7},{7,6},{8,9},{9,8},{10,11... | collective-permute-start | bytes 49160 | tf_op jit(solution)/shard_map/ppermute | solution.py:245
  37.3 4.5 %collective-permute-start.14 = (f32[16,128]{1,0:T(8,128)S(1)}, f32[16,128]{1,0:T(8,128)S(1)}, u32[]{:S(2)}, u32[]{:S(2)}) collective-permute-start(f32[16,128]{1,0:T(8,128)S(1)} %slice.23), channel_id=1, source_target_pairs={{0,24},{8,16},{16,8},{24,0},{1,25},{9,17},{17,9},{25,1},{2,26},{10... | collective-permute-start | bytes 24584 | tf_op jit(solution)/shard_map/ppermute | solution.py:245
  39.0 3.7 %collective-permute-start.13 = (f32[16,128]{1,0:T(8,128)S(1)}, f32[16,128]{1,0:T(8,128)S(1)}, u32[]{:S(2)}, u32[]{:S(2)}) collective-permute-start(f32[16,128]{1,0:T(8,128)S(1)} %slice.23), channel_id=1, source_target_pairs={{0,16},{8,24},{16,0},{24,8},{1,17},{9,25},{17,1},{25,9},{2,18},{10... | collective-permute-start | bytes 24584 | tf_op jit(solution)/shard_map/ppermute | solution.py:245
  40.3 3.7 %collective-permute-start.12 = (f32[16,128]{1,0:T(8,128)S(1)}, f32[16,128]{1,0:T(8,128)S(1)}, u32[]{:S(2)}, u32[]{:S(2)}) collective-permute-start(f32[16,128]{1,0:T(8,128)S(1)} %slice.23), channel_id=1, source_target_pairs={{0,8},{8,0},{16,24},{24,16},{1,9},{9,1},{17,25},{25,17},{2,10},{10... | collective-permute-start | bytes 24584 | tf_op jit(solution)/shard_map/ppermute | solution.py:245
  43.9 5.5 %collective-permute-start.17 = (f32[32,128]{1,0:T(8,128)S(1)}, f32[32,128]{1,0:T(8,128)S(1)}, u32[]{:S(2)}, u32[]{:S(2)}) collective-permute-start(f32[32,128]{1,0:T(8,128)S(1)} %dom.1.refs_0_), channel_id=1, source_target_pairs={{0,6},{1,7},{2,4},{3,5},{4,2},{5,3},{6,0},{7,1},{8,14},{9,15},{10,... | collective-permute-start | bytes 49160 | tf_op jit(solution)/shard_map/ppermute | solution.py:245
  46.7 4.6 %collective-permute-start.16 = (f32[32,128]{1,0:T(8,128)S(1)}, f32[32,128]{1,0:T(8,128)S(1)}, u32[]{:S(2)}, u32[]{:S(2)}) collective-permute-start(f32[32,128]{1,0:T(8,128)S(1)} %dom.1.refs_0_), channel_id=1, source_target_pairs={{0,4},{1,5},{2,6},{3,7},{4,0},{5,1},{6,2},{7,3},{8,12},{9,13},{10,... | collective-permute-start | bytes 49160 | tf_op jit(solution)/shard_map/ppermute | solution.py:245
  49.0 3.7 %collective-permute-start.15 = (f32[32,128]{1,0:T(8,128)S(1)}, f32[32,128]{1,0:T(8,128)S(1)}, u32[]{:S(2)}, u32[]{:S(2)}) collective-permute-start(f32[32,128]{1,0:T(8,128)S(1)} %dom.1.refs_0_), channel_id=1, source_target_pairs={{0,2},{1,3},{2,0},{3,1},{4,6},{5,7},{6,4},{7,5},{8,10},{9,11},{10,... | collective-permute-start | bytes 49160 | tf_op jit(solution)/shard_map/ppermute | solution.py:245
  52.9 10.2 %collective-permute-start.23 = (f32[16,16,128]{2,1,0:T(8,128)S(1)}, f32[16,16,128]{2,1,0:T(8,128)S(1)}, u32[]{:S(2)}, u32[]{:S(2)}) collective-permute-start(f32[16,16,128]{2,1,0:T(8,128)S(1)} %remove.1.refs_0_), channel_id=1, source_target_pairs={{0,4},{1,5},{2,6},{3,7},{4,0},{5,1},{6,2},{7,3},{8,12},{9,13},{10,... | collective-permute-start | bytes 393224 | tf_op jit(solution)/shard_map/ppermute | solution.py:245
  54.6 8.6 %collective-permute-start.21 = (f32[16,16,128]{2,1,0:T(8,128)S(1)}, f32[16,16,128]{2,1,0:T(8,128)S(1)}, u32[]{:S(2)}, u32[]{:S(2)}) collective-permute-start(f32[16,16,128]{2,1,0:T(8,128)S(1)} %remove.1.refs_0_), channel_id=1, source_target_pairs={{0,6},{1,7},{2,4},{3,5},{4,2},{5,3},{6,0},{7,1},{8,14},{9,15},{10,... | collective-permute-start | bytes 393224 | tf_op jit(solution)/shard_map/ppermute | solution.py:245
  56.8 7.0 %collective-permute-start.19 = (f32[16,16,128]{2,1,0:T(8,128)S(1)}, f32[16,16,128]{2,1,0:T(8,128)S(1)}, u32[]{:S(2)}, u32[]{:S(2)}) collective-permute-start(f32[16,16,128]{2,1,0:T(8,128)S(1)} %remove.1.refs_0_), channel_id=1, source_target_pairs={{0,2},{1,3},{2,0},{3,1},{4,6},{5,7},{6,4},{7,5},{8,10},{9,11},{10,... | collective-permute-start | bytes 393224 | tf_op jit(solution)/shard_map/ppermute | solution.py:245
  56.8 7.4 %collective-permute-start.18 = (f32[16,16,128]{2,1,0:T(8,128)S(1)}, f32[16,16,128]{2,1,0:T(8,128)S(1)}, u32[]{:S(2)}, u32[]{:S(2)}) collective-permute-start(f32[16,16,128]{2,1,0:T(8,128)S(1)} %remove.1.refs_0_), channel_id=1, source_target_pairs={{0,1},{1,0},{2,3},{3,2},{4,5},{5,4},{6,7},{7,6},{8,9},{9,8},{10,11... | collective-permute-start | bytes 393224 | tf_op jit(solution)/shard_map/ppermute | solution.py:245
  63.1 1.3 %collective-permute-start.24 = (f32[16,16,128]{2,1,0:T(8,128)S(1)}, f32[16,16,128]{2,1,0:T(8,128)S(1)}, u32[]{:S(2)}, u32[]{:S(2)}) collective-permute-start(f32[16,16,128]{2,1,0:T(8,128)S(1)} %collective-permute-done.23.refs_7_), channel_id=1, source_target_pairs={{0,1},{1,0},{2,3},{3,2},{4,5},{5,4},{6,7},{7,6},{8,9},{9,8},{10,11... | collective-permute-start | bytes 393224 | tf_op jit(solution)/shard_map/ppermute | solution.py:245
  63.2 1.5 %collective-permute-start.22 = (f32[16,16,128]{2,1,0:T(8,128)S(1)}, f32[16,16,128]{2,1,0:T(8,128)S(1)}, u32[]{:S(2)}, u32[]{:S(2)}) collective-permute-start(f32[16,16,128]{2,1,0:T(8,128)S(1)} %collective-permute-done.21.refs_5_), channel_id=1, source_target_pairs={{0,1},{1,0},{2,3},{3,2},{4,5},{5,4},{6,7},{7,6},{8,9},{9,8},{10,11... | collective-permute-start | bytes 393224 | tf_op jit(solution)/shard_map/ppermute | solution.py:245
  63.8 1.3 %collective-permute-start.20 = (f32[16,16,128]{2,1,0:T(8,128)S(1)}, f32[16,16,128]{2,1,0:T(8,128)S(1)}, u32[]{:S(2)}, u32[]{:S(2)}) collective-permute-start(f32[16,16,128]{2,1,0:T(8,128)S(1)} %collective-permute-done.19.refs_2_), channel_id=1, source_target_pairs={{0,1},{1,0},{2,3},{3,2},{4,5},{5,4},{6,7},{7,6},{8,9},{9,8},{10,11... | collective-permute-start | bytes 393224 | tf_op jit(solution)/shard_map/ppermute | solution.py:245
where the time goes:
time: 67.6 us; the launch traced here: 67.4 us
  waiting for transfers between devices  30.6 us (45%)
  starting transfers between devices  28.6 us (42%)
  Pallas kernels  5.98 us (9%)
  between operations  2.11 us (3%)
    ppermute x22, waiting for transfers between devices, swap(): return lax.ppermute(value, axis, [(i, i ^ k) for i in range(count)])  28.3 us
    ppermute x22, starting transfers between devices, swap(): return lax.ppermute(value, axis, [(i, i ^ k) for i in range(count)])  23.1 us
    ppermute x1, starting transfers between devices, per_device(): lax.ppermute(far, 'orb', [(o, (o + 2 * (o % 2) - 1) % blocks) for o in ra...  2.59 us
    ppermute x1, waiting for transfers between devices, per_device(): lax.ppermute(far, 'orb', [(o, (o + 2 * (o % 2) - 1) % blocks) for o in ra...  2.3 us
    pallas_call x1, Pallas kernels, per_device(): pl.pallas_call(functools.partial(update_kernel, blocks, sequence), out_sh...  2.26 us
    ppermute x1, starting transfers between devices, per_device(): x_before = lax.ppermute(last, 'dom', up(doms))  1.7 us
    pallas_call x1, Pallas kernels, per_device(): pl.pallas_call(functools.partial(pack_kernel, blocks), out_shape=[shape(2...  1.65 us
  transfers between devices with their start and end apart: 25, of which 15 were waited for; matrix products, arithmetic and copies ran while one was open for 0% of the time, Pallas kernels for 1%

commit v1 on v0

--- a/solution.py
+++ b/solution.py
@@ -155,7 +155,7 @@
 
 
 def project_kernel(
-    volume, owner_ref, rot_ref, xh_ref, xl_ref, inner_ref, near_ref, far_ref, xb_ref, xa_ref, wh_ref, wl_ref,
+    volume, owner_ref, rot_ref, xh_ref, xl_ref, inner_ref, far_ref, near_ref, xb_ref, xa_ref, wh_ref, wl_ref,
     a_ref, p_ref, around,
 ):
     slab, nb, cells = inner_ref.shape
@@ -192,11 +192,11 @@
     *p_refs, high_ref, low_ref = refs
     size, wide = high_ref.shape[0], p_refs[0].shape[1]
     row, col = (lax.broadcasted_iota(jnp.int32, (size, wide), axis) for axis in (0, 1))
-    mine = jnp.where(col == lax.axis_index("orb") * nb + row % nb, 1.0, 0.0).astype(BF16)
+    mine = jnp.where(col == lax.axis_index("orb") * nb + row // MIX, 1.0, 0.0).astype(BF16)
     orbital, col = (lax.broadcasted_iota(jnp.int32, (nb, size), axis) for axis in (0, 1))
-    repeat = jnp.where(orbital == col % nb, 1.0, 0.0).astype(BF16)
+    repeat = jnp.where(orbital == col // MIX, 1.0, 0.0).astype(BF16)
     row, col = (lax.broadcasted_iota(jnp.int32, (size, size), axis) for axis in (0, 1))
-    same = row // nb == col // nb
+    same = row % MIX == col % MIX
     dot = lambda x, y, axes: lax.dot_general(x, y, (axes, ((), ())), preferred_element_type=jnp.float32)
     for part, ref in zip(split(total(p_refs, nb, nb)), (high_ref, low_ref)):
         block = dot(mine, part, ((1,), (1,))).astype(BF16)
@@ -204,7 +204,7 @@
 
 
 def update_kernel(blocks, sequence, wh_ref, wl_ref, x_ref, *refs):
-    g_refs, (grad_hbm, out_hbm, whole, grad, mixed, added, out, sems) = refs[:blocks], refs[blocks:]
+    g_refs, (grad_hbm, out_hbm, whole, grad, out, sems) = refs[:blocks], refs[blocks:]
     nb, cells, rows_z = x_ref.shape
     rank = lax.axis_index("orb")
     share = rows_z // blocks * nb
@@ -215,25 +215,20 @@
     copies = []
     for i in range(CHUNKS):
         for c in range(i * per, (i + 1) * per):
-            plane = whole[pl.ds(c, rows_z, stride=nb), :].T
-            grad[c] = plane
-            mixed[pl.ds(c, cells, stride=nb), :] = plane
+            grad[c] = whole[pl.ds(c, rows_z, stride=nb), :].T
         part = pl.ds(i * per, per)
         copies.append(pltpu.make_async_copy(grad.at[part], grad_hbm.at[part], sems.at[0, i]))
         copies[-1].start()
-    size = wh_ref.shape[0]
     mix = (wh_ref[...], wl_ref[...])
     rows = cells // CHUNKS
-    tall = rows * nb
     for i in range(CHUNKS):
-        parts = split(mixed[i * tall : (i + 1) * tall])
-        sides = [jnp.concatenate([p[j : j + size] for j in range(0, tall, size)], axis=1) for p in parts]
-        result = dot3(mix, sides, ((1,), (0,)))
-        for j in range(tall // size):
-            added[i * tall + j * size : i * tall + (j + 1) * size] = result[:, j * rows_z : (j + 1) * rows_z]
         some = pl.ds(i * rows, rows)
-        for a in range(nb):
-            out[a, some] = x_ref[a, some] + added[pl.ds(i * tall + a, rows, stride=nb), :]
+        places = [pl.ds(start, MIX) for start in range(i * rows, (i + 1) * rows, MIX)]
+        sides = [jnp.concatenate([grad[c, at] for c in range(nb)], axis=0) for at in places]
+        result = dot3(mix, split(jnp.concatenate(sides, axis=1)), ((1,), (0,)))
+        for j, at in enumerate(places):
+            for a in range(nb):
+                out[a, at] = x_ref[a, at] + result[a * MIX : (a + 1) * MIX, j * rows_z : (j + 1) * rows_z]
         copies.append(pltpu.make_async_copy(out.at[:, some], out_hbm.at[:, some], sems.at[1, i]))
         copies[-1].start()
     for copy in copies:
@@ -335,7 +330,7 @@
         scratch_shapes=[pltpu.VMEM((2, WIDTH, nb, cells), f32)],
         compiler_params=params(),
         name="project",
-    )(owner, rotation, *parts, inner, z_near, z_far, x_before, x_after, *weights)
+    )(owner, rotation, *parts, inner, z_far, z_near, x_before, x_after, *weights)
 
     part = part + swap(part, "orb", 1)
     part = pl.pallas_call(
@@ -382,8 +377,6 @@
         scratch_shapes=[
             pltpu.VMEM(((rows_z + 1) * nb, cells), f32),
             pltpu.VMEM((nb, cells, rows_z), f32),
-            pltpu.VMEM(((cells + 1) * nb, rows_z), f32),
-            pltpu.VMEM(((cells + 1) * nb, rows_z), f32),
             pltpu.VMEM((nb, cells, rows_z), f32),
             pltpu.SemaphoreType.DMA((2, CHUNKS)),
         ],

time: 67.6 us -> 67.2 us (level)
  starting transfers between devices: 28.6 us -> 29.8 us
  waiting for transfers between devices: 30.6 us -> 29.6 us
    ppermute x22, starting transfers between devices: 23.1 us -> 25.1 us  [swap(): return lax.ppermute(value, axis, [(i, i ^ k) for i in range(count)])]
    ppermute x1, waiting for transfers between devices: 2.3 us -> 1.22 us  [per_device(): lax.ppermute(far, 'orb', [(o, (o + 2 * (o % 2) - 1) % blocks) for o in ra...]
    ppermute x1, starting transfers between devices: 2.59 us -> 1.7 us  [per_device(): lax.ppermute(far, 'orb', [(o, (o + 2 * (o % 2) - 1) % blocks) for o in ra...]
where the time goes in v1:
time: 67.2 us; the launch traced here: 67 us
  starting transfers between devices  29.8 us (44%)
  waiting for transfers between devices  29.6 us (44%)
  Pallas kernels  5.47 us (8%)
  between operations  2.11 us (3%)
    ppermute x22, waiting for transfers between devices, swap(): return lax.ppermute(value, axis, [(i, i ^ k) for i in range(count)])  28.4 us
    ppermute x22, starting transfers between devices, swap(): return lax.ppermute(value, axis, [(i, i ^ k) for i in range(count)])  25.1 us
    pallas_call x1, Pallas kernels, per_device(): pl.pallas_call(functools.partial(update_kernel, blocks, sequence), out_sh...  1.77 us
    ppermute x1, starting transfers between devices, per_device(): x_before = lax.ppermute(last, 'dom', up(doms))  1.7 us
    ppermute x1, starting transfers between devices, per_device(): lax.ppermute(far, 'orb', [(o, (o + 2 * (o % 2) - 1) % blocks) for o in ra...  1.7 us
    pallas_call x1, Pallas kernels, per_device(): pl.pallas_call(functools.partial(pack_kernel, blocks), out_shape=[shape(2...  1.65 us
  transfers between devices with their start and end apart: 25, of which 15 were waited for; matrix products, arithmetic and copies ran while one was open for 0% of the time, Pallas kernels for 1%

profile of v1, /device:TPU:0, one launch (start us, length us, event | category | flops | bytes accessed | tf_op | source)
XLA Modules:
  0.0 67.0 jit_solution(13333697502945125604)
XLA Ops:
  0.6 1.7 %pack.1 = (f32[2,16,16,128]{3,2,1,0:T(8,128)S(1)}, f32[2,16,16,128]{3,2,1,0:T(8,128)S(1)}, f32[2,16,16,128]{3,2,1,0:T(8,128)S(1)}, f32[2,16,16,128]{3,2,1,0:T(8,128)S(1)}) custom-call(f32[16,128,128]{2,1,0:T(8,128)} %bitcast.12), custom_call_target="tpu_custom_call" | custom-call | tf_op jit(solution)/shard_map/pack/pallas_call | solution.py:268
  2.3 4.1 %collective-permute-start.2 = (f32[2,16,16,128]{3,2,1,0:T(8,128)S(1)}, f32[2,16,16,128]{3,2,1,0:T(8,128)S(1)}, u32[]{:S(2)}, u32[]{:S(2)}) collective-permute-start(f32[2,16,16,128]{3,2,1,0:T(8,128)S(1)} %get-tuple-element.21), channel_id=1, source_target_pairs={{0,4},{1,5},{2,6},{3,7},{4,0},{5,1},{6,2},{7,3},{8,12},{9,13},{10,... | collective-permute-start | bytes 786440 | tf_op jit(solution)/shard_map/ppermute | solution.py:240
  6.5 1.6 %collective-permute-start.4 = (f32[2,16,16,128]{3,2,1,0:T(8,128)S(1)}, f32[2,16,16,128]{3,2,1,0:T(8,128)S(1)}, u32[]{:S(2)}, u32[]{:S(2)}) collective-permute-start(f32[2,16,16,128]{3,2,1,0:T(8,128)S(1)} %get-tuple-element.22), channel_id=1, source_target_pairs={{0,2},{1,3},{2,0},{3,1},{4,6},{5,7},{6,4},{7,5},{8,10},{9,11},{10,... | collective-permute-start | bytes 786440 | tf_op jit(solution)/shard_map/ppermute | solution.py:240
  8.2 3.3 %collective-permute-start = (f32[16,16,128]{2,1,0:T(8,128)S(1)}, f32[16,16,128]{2,1,0:T(8,128)S(1)}, u32[]{:S(2)}, u32[]{:S(2)}) collective-permute-start(f32[16,16,128]{2,1,0:T(8,128)S(1)} %get-tuple-element.39), channel_id=1, source_target_pairs={{0,7},{1,6},{2,5},{3,4},{4,3},{5,2},{6,1},{7,0},{8,15},{9,14},{10,... | collective-permute-start | bytes 393224 | tf_op jit(solution)/shard_map/ppermute | solution.py:240
  12.8 7.2 %collective-permute-done.2.refs_5_ = f32[2,16,16,128]{3,2,1,0:T(8,128)S(1)} collective-permute-done((f32[2,16,16,128]{3,2,1,0:T(8,128)S(1)}, f32[2,16,16,128]{3,2,1,0:T(8,128)S(1)}, u32[]{:S(2)}, u32[]{:S(2)}) %collective-permute-start.2) | collective-permute-done | bytes 262176 | tf_op jit(solution)/shard_map/ppermute | solution.py:240
  20.1 5.1 %collective-permute-done.4.pair_ref.refs_6_ = f32[2,16,16,128]{3,2,1,0:T(8,128)S(1)} collective-permute-done((f32[2,16,16,128]{3,2,1,0:T(8,128)S(1)}, f32[2,16,16,128]{3,2,1,0:T(8,128)S(1)}, u32[]{:S(2)}, u32[]{:S(2)}) %collective-permute-start.4) | collective-permute-done | bytes 262176 | tf_op jit(solution)/shard_map/ppermute | solution.py:240
  25.4 1.3 %collective-permute-done.5.refs_3_ = f32[16,16,128]{2,1,0:T(8,128)S(1)} collective-permute-done((f32[16,16,128]{2,1,0:T(8,128)S(1)}, f32[16,16,128]{2,1,0:T(8,128)S(1)}, u32[]{:S(2)}, u32[]{:S(2)}) %collective-permute-start.5) | collective-permute-done | bytes 131104 | tf_op jit(solution)/shard_map/ppermute | solution.py:240
  26.9 1.7 %collective-permute-start.9 = (f32[192,128]{1,0:T(8,128)S(1)}, f32[192,128]{1,0:T(8,128)S(1)}, u32[]{:S(2)}, u32[]{:S(2)}) collective-permute-start(f32[192,128]{1,0:T(8,128)S(1)} %get-tuple-element.30), channel_id=1, source_target_pairs={{0,8},{8,16},{16,24},{24,0},{1,9},{9,17},{17,25},{25,1},{2,10},{10... | collective-permute-start | bytes 294920 | tf_op jit(solution)/shard_map/ppermute | solution.py:307
  28.6 1.3 %collective-permute-start.10 = (f32[192,128]{1,0:T(8,128)S(1)}, f32[192,128]{1,0:T(8,128)S(1)}, u32[]{:S(2)}, u32[]{:S(2)}) collective-permute-start(f32[192,128]{1,0:T(8,128)S(1)} %get-tuple-element.31), channel_id=1, source_target_pairs={{0,24},{8,0},{16,8},{24,16},{1,25},{9,1},{17,9},{25,17},{2,26},{10... | collective-permute-start | bytes 294920 | tf_op jit(solution)/shard_map/ppermute | solution.py:308
  29.9 1.7 %collective-permute-start.7 = (f32[6,16,128]{2,1,0:T(8,128)S(1)}, f32[6,16,128]{2,1,0:T(8,128)S(1)}, u32[]{:S(2)}, u32[]{:S(2)}) collective-permute-start(f32[6,16,128]{2,1,0:T(8,128)S(1)} %get-tuple-element.28), channel_id=1, source_target_pairs={{0,7},{1,2},{2,1},{3,4},{4,3},{5,6},{6,5},{7,0},{8,15},{9,10},{10,... | collective-permute-start | bytes 147464 | tf_op jit(solution)/shard_map/ppermute | solution.py:310
  31.6 2.0 %collective-permute-start.8 = (f32[6,16,128]{2,1,0:T(8,128)S(1)}, f32[6,16,128]{2,1,0:T(8,128)S(1)}, u32[]{:S(2)}, u32[]{:S(2)}) collective-permute-start(f32[6,16,128]{2,1,0:T(8,128)S(1)} %get-tuple-element.29), channel_id=1, source_target_pairs={{0,1},{1,0},{2,3},{3,2},{4,5},{5,4},{6,7},{7,6},{8,9},{9,8},{10,11... | collective-permute-start | bytes 147464 | tf_op jit(solution)/shard_map/ppermute | solution.py:240
  33.6 0.4 split.1
  34.0 1.2 %collective-permute-done.7.far_ref = f32[6,16,128]{2,1,0:T(8,128)S(1)} collective-permute-done((f32[6,16,128]{2,1,0:T(8,128)S(1)}, f32[6,16,128]{2,1,0:T(8,128)S(1)}, u32[]{:S(2)}, u32[]{:S(2)}) %collective-permute-start.7) | collective-permute-done | bytes 49184 | tf_op jit(solution)/shard_map/ppermute | solution.py:310
  35.3 0.8 %project.1 = (f32[16,16,128]{2,1,0:T(8,128)S(1)}, f32[32,128]{1,0:T(8,128)S(1)}) custom-call(s32[1]{0:T(128)S(6)} %copy.10.owner_ref, f32[16,128]{1,0:T(8,128)S(1)} %copy-done.4, bf16[128,2048]{1,0:T(8,128)(2,1)S(1)} %get-tuple-element.25.xh_ref, bf16[128,2048]{1,0:T(8,128)(2,1)S(1)} %get-tuple-element.26.xl_ref, ...), custom_call_target="tpu_custom_call" | custom-call | tf_op jit(solution)/shard_map/project/pallas_call | solution.py:325
  36.4 0.9 %collective-permute-done.11 = f32[32,128]{1,0:T(8,128)S(1)} collective-permute-done((f32[32,128]{1,0:T(8,128)S(1)}, f32[32,128]{1,0:T(8,128)S(1)}, u32[]{:S(2)}, u32[]{:S(2)}) %collective-permute-start.11) | collective-permute-done | bytes 16416 | tf_op jit(solution)/shard_map/ppermute | solution.py:240
  37.3 1.7 %collective-permute-start.14 = (f32[16,128]{1,0:T(8,128)S(1)}, f32[16,128]{1,0:T(8,128)S(1)}, u32[]{:S(2)}, u32[]{:S(2)}) collective-permute-start(f32[16,128]{1,0:T(8,128)S(1)} %slice.23), channel_id=1, source_target_pairs={{0,24},{8,16},{16,8},{24,0},{1,25},{9,17},{17,9},{25,1},{2,26},{10... | collective-permute-start | bytes 24584 | tf_op jit(solution)/shard_map/ppermute | solution.py:240
  39.0 1.2 %collective-permute-start.13 = (f32[16,128]{1,0:T(8,128)S(1)}, f32[16,128]{1,0:T(8,128)S(1)}, u32[]{:S(2)}, u32[]{:S(2)}) collective-permute-start(f32[16,128]{1,0:T(8,128)S(1)} %slice.23), channel_id=1, source_target_pairs={{0,16},{8,24},{16,0},{24,8},{1,17},{9,25},{17,1},{25,9},{2,18},{10... | collective-permute-start | bytes 24584 | tf_op jit(solution)/shard_map/ppermute | solution.py:240
  40.2 0.5 collective-permute-start.12
  40.8 1.1 %collective-permute-done.14.refs_2_ = f32[16,128]{1,0:T(8,128)S(1)} collective-permute-done((f32[16,128]{1,0:T(8,128)S(1)}, f32[16,128]{1,0:T(8,128)S(1)}, u32[]{:S(2)}, u32[]{:S(2)}) %collective-permute-start.14) | collective-permute-done | bytes 8224 | tf_op jit(solution)/shard_map/ppermute | solution.py:240
  41.8 0.8 %collective-permute-done.13.refs_1_ = f32[16,128]{1,0:T(8,128)S(1)} collective-permute-done((f32[16,128]{1,0:T(8,128)S(1)}, f32[16,128]{1,0:T(8,128)S(1)}, u32[]{:S(2)}, u32[]{:S(2)}) %collective-permute-start.13) | collective-permute-done | bytes 8224 | tf_op jit(solution)/shard_map/ppermute | solution.py:240
  42.7 1.2 %collective-permute-done.12.refs_0_ = f32[16,128]{1,0:T(8,128)S(1)} collective-permute-done((f32[16,128]{1,0:T(8,128)S(1)}, f32[16,128]{1,0:T(8,128)S(1)}, u32[]{:S(2)}, u32[]{:S(2)}) %collective-permute-start.12) | collective-permute-done | bytes 8224 | tf_op jit(solution)/shard_map/ppermute | solution.py:240
  43.9 2.1 %collective-permute-start.17 = (f32[32,128]{1,0:T(8,128)S(1)}, f32[32,128]{1,0:T(8,128)S(1)}, u32[]{:S(2)}, u32[]{:S(2)}) collective-permute-start(f32[32,128]{1,0:T(8,128)S(1)} %dom.1.refs_0_), channel_id=1, source_target_pairs={{0,6},{1,7},{2,4},{3,5},{4,2},{5,3},{6,0},{7,1},{8,14},{9,15},{10,... | collective-permute-start | bytes 49160 | tf_op jit(solution)/shard_map/ppermute | solution.py:240
  46.0 3.0 %collective-permute-start.16 = (f32[32,128]{1,0:T(8,128)S(1)}, f32[32,128]{1,0:T(8,128)S(1)}, u32[]{:S(2)}, u32[]{:S(2)}) collective-permute-start(f32[32,128]{1,0:T(8,128)S(1)} %dom.1.refs_0_), channel_id=1, source_target_pairs={{0,4},{1,5},{2,6},{3,7},{4,0},{5,1},{6,2},{7,3},{8,12},{9,13},{10,... | collective-permute-start | bytes 49160 | tf_op jit(solution)/shard_map/ppermute | solution.py:240
  49.0 0.5 collective-permute-start.15
  49.5 1.3 %collective-permute-done.16.refs_2_ = f32[32,128]{1,0:T(8,128)S(1)} collective-permute-done((f32[32,128]{1,0:T(8,128)S(1)}, f32[32,128]{1,0:T(8,128)S(1)}, u32[]{:S(2)}, u32[]{:S(2)}) %collective-permute-start.16) | collective-permute-done | bytes 16416 | tf_op jit(solution)/shard_map/ppermute | solution.py:240
  50.8 1.9 %collective-permute-done.15.refs_1_ = f32[32,128]{1,0:T(8,128)S(1)} collective-permute-done((f32[32,128]{1,0:T(8,128)S(1)}, f32[32,128]{1,0:T(8,128)S(1)}, u32[]{:S(2)}, u32[]{:S(2)}) %collective-permute-start.15) | collective-permute-done | bytes 16416 | tf_op jit(solution)/shard_map/ppermute | solution.py:240
  53.0 1.6 %collective-permute-start.23 = (f32[16,16,128]{2,1,0:T(8,128)S(1)}, f32[16,16,128]{2,1,0:T(8,128)S(1)}, u32[]{:S(2)}, u32[]{:S(2)}) collective-permute-start(f32[16,16,128]{2,1,0:T(8,128)S(1)} %remove.1.refs_0_), channel_id=1, source_target_pairs={{0,4},{1,5},{2,6},{3,7},{4,0},{5,1},{6,2},{7,3},{8,12},{9,13},{10,... | collective-permute-start | bytes 393224 | tf_op jit(solution)/shard_map/ppermute | solution.py:240
  54.6 2.2 %collective-permute-start.21 = (f32[16,16,128]{2,1,0:T(8,128)S(1)}, f32[16,16,128]{2,1,0:T(8,128)S(1)}, u32[]{:S(2)}, u32[]{:S(2)}) collective-permute-start(f32[16,16,128]{2,1,0:T(8,128)S(1)} %remove.1.refs_0_), channel_id=1, source_target_pairs={{0,6},{1,7},{2,4},{3,5},{4,2},{5,3},{6,0},{7,1},{8,14},{9,15},{10,... | collective-permute-start | bytes 393224 | tf_op jit(solution)/shard_map/ppermute | solution.py:240
  56.8 6.5 %collective-permute-done.23.refs_7_ = f32[16,16,128]{2,1,0:T(8,128)S(1)} collective-permute-done((f32[16,16,128]{2,1,0:T(8,128)S(1)}, f32[16,16,128]{2,1,0:T(8,128)S(1)}, u32[]{:S(2)}, u32[]{:S(2)}) %collective-permute-start.23) | collective-permute-done | bytes 131104 | tf_op jit(solution)/shard_map/ppermute | solution.py:240
  63.3 0.5 collective-permute-start.22
  64.8 0.4 collective-permute-done.20.refs_3_
  65.3 1.8 %update.1 = (f32[16,128,128]{2,1,0:T(8,128)}, f32[16,128,128]{2,1,0:T(8,128)}) custom-call(bf16[128,128]{1,0:T(8,128)(2,1)S(1)} %get-tuple-element.33.wh_ref, bf16[128,128]{1,0:T(8,128)(2,1)S(1)} %get-tuple-element.34.wl_ref, f32[16,128,128]{2,1,0:T(8,128)S(1)} %bitcast.13, f32[16,16,128]{2,1,0:T(8,128)S(1)} %remove.1.refs_0_, ...), custom_call_target="tpu_custom_call" | custom-call | tf_op jit(solution)/shard_map/update/pallas_call | solution.py:372
  (42 shorter events, 2.2 us)
Async XLA Ops:
  2.3 17.8 %collective-permute-start.2 = (f32[2,16,16,128]{3,2,1,0:T(8,128)S(1)}, f32[2,16,16,128]{3,2,1,0:T(8,128)S(1)}, u32[]{:S(2)}, u32[]{:S(2)}) collective-permute-start(f32[2,16,16,128]{3,2,1,0:T(8,128)S(1)} %get-tuple-element.21), channel_id=1, source_target_pairs={{0,4},{1,5},{2,6},{3,7},{4,0},{5,1},{6,2},{7,3},{8,12},{9,13},{10,... | collective-permute-start | bytes 786440 | tf_op jit(solution)/shard_map/ppermute | solution.py:240
  6.4 19.0 %collective-permute-start.6 = (f32[16,16,128]{2,1,0:T(8,128)S(1)}, f32[16,16,128]{2,1,0:T(8,128)S(1)}, u32[]{:S(2)}, u32[]{:S(2)}) collective-permute-start(f32[16,16,128]{2,1,0:T(8,128)S(1)} %slice_bitcast_fusion.1), channel_id=1, source_target_pairs={{0,1},{1,0},{2,3},{3,2},{4,5},{5,4},{6,7},{7,6},{8,9},{9,8},{10,11... | collective-permute-start | bytes 393224 | tf_op jit(solution)/shard_map/ppermute | solution.py:240
  6.5 18.8 %collective-permute-start.4 = (f32[2,16,16,128]{3,2,1,0:T(8,128)S(1)}, f32[2,16,16,128]{3,2,1,0:T(8,128)S(1)}, u32[]{:S(2)}, u32[]{:S(2)}) collective-permute-start(f32[2,16,16,128]{3,2,1,0:T(8,128)S(1)} %get-tuple-element.22), channel_id=1, source_target_pairs={{0,2},{1,3},{2,0},{3,1},{4,6},{5,7},{6,4},{7,5},{8,10},{9,11},{10,... | collective-permute-start | bytes 786440 | tf_op jit(solution)/shard_map/ppermute | solution.py:240
  8.1 17.3 %collective-permute-start.1 = (f32[16,16,128]{2,1,0:T(8,128)S(1)}, f32[16,16,128]{2,1,0:T(8,128)S(1)}, u32[]{:S(2)}, u32[]{:S(2)}) collective-permute-start(f32[16,16,128]{2,1,0:T(8,128)S(1)} %get-tuple-element.38), channel_id=1, source_target_pairs={{0,6},{1,7},{2,4},{3,5},{4,2},{5,3},{6,0},{7,1},{8,14},{9,15},{10,... | collective-permute-start | bytes 393224 | tf_op jit(solution)/shard_map/ppermute | solution.py:240
  8.2 17.2 %collective-permute-start = (f32[16,16,128]{2,1,0:T(8,128)S(1)}, f32[16,16,128]{2,1,0:T(8,128)S(1)}, u32[]{:S(2)}, u32[]{:S(2)}) collective-permute-start(f32[16,16,128]{2,1,0:T(8,128)S(1)} %get-tuple-element.39), channel_id=1, source_target_pairs={{0,7},{1,6},{2,5},{3,4},{4,3},{5,2},{6,1},{7,0},{8,15},{9,14},{10,... | collective-permute-start | bytes 393224 | tf_op jit(solution)/shard_map/ppermute | solution.py:240
  20.1 5.4 %collective-permute-start.3 = (f32[16,16,128]{2,1,0:T(8,128)S(1)}, f32[16,16,128]{2,1,0:T(8,128)S(1)}, u32[]{:S(2)}, u32[]{:S(2)}) collective-permute-start(f32[16,16,128]{2,1,0:T(8,128)S(1)} %slice_bitcast_fusion), channel_id=1, source_target_pairs={{0,1},{1,0},{2,3},{3,2},{4,5},{5,4},{6,7},{7,6},{8,9},{9,8},{10,11... | collective-permute-start | bytes 393224 | tf_op jit(solution)/shard_map/ppermute | solution.py:240
  25.3 8.3 %copy-start.1 = (bf16[384,128]{1,0:T(8,128)(2,1)S(1)}, bf16[384,128]{1,0:T(8,128)(2,1)}, u32[]{:S(2)}) copy-start(bf16[384,128]{1,0:T(8,128)(2,1)} %constant.5.clone.wl_ref) | copy-start | bytes 294916
  25.3 8.3 %copy-start.2 = (bf16[384,128]{1,0:T(8,128)(2,1)S(1)}, bf16[384,128]{1,0:T(8,128)(2,1)}, u32[]{:S(2)}) copy-start(bf16[384,128]{1,0:T(8,128)(2,1)} %constant.4.clone.wh_ref) | copy-start | bytes 294916
  25.3 8.3 %copy-start.3 = (f32[8,16,128]{2,1,0:T(8,128)S(1)}, f32[8,16,128]{2,1,0:T(8,128)}, u32[]{:S(2)}) copy-start(f32[8,16,128]{2,1,0:T(8,128)} %param.8) | copy-start | bytes 196612
  25.3 1.4 %collective-permute-start.5 = (f32[16,16,128]{2,1,0:T(8,128)S(1)}, f32[16,16,128]{2,1,0:T(8,128)S(1)}, u32[]{:S(2)}, u32[]{:S(2)}) collective-permute-start(f32[16,16,128]{2,1,0:T(8,128)S(1)} %hand.1), channel_id=1, source_target_pairs={{0,1},{1,0},{2,3},{3,2},{4,5},{5,4},{6,7},{7,6},{8,9},{9,8},{10,11... | collective-permute-start | bytes 393224 | tf_op jit(solution)/shard_map/ppermute | solution.py:240
  26.9 8.3 %collective-permute-start.9 = (f32[192,128]{1,0:T(8,128)S(1)}, f32[192,128]{1,0:T(8,128)S(1)}, u32[]{:S(2)}, u32[]{:S(2)}) collective-permute-start(f32[192,128]{1,0:T(8,128)S(1)} %get-tuple-element.30), channel_id=1, source_target_pairs={{0,8},{8,16},{16,24},{24,0},{1,9},{9,17},{17,25},{25,1},{2,10},{10... | collective-permute-start | bytes 294920 | tf_op jit(solution)/shard_map/ppermute | solution.py:307
  28.6 6.6 %collective-permute-start.10 = (f32[192,128]{1,0:T(8,128)S(1)}, f32[192,128]{1,0:T(8,128)S(1)}, u32[]{:S(2)}, u32[]{:S(2)}) collective-permute-start(f32[192,128]{1,0:T(8,128)S(1)} %get-tuple-element.31), channel_id=1, source_target_pairs={{0,24},{8,0},{16,8},{24,16},{1,25},{9,1},{17,9},{25,17},{2,26},{10... | collective-permute-start | bytes 294920 | tf_op jit(solution)/shard_map/ppermute | solution.py:308
  29.9 5.3 %collective-permute-start.7 = (f32[6,16,128]{2,1,0:T(8,128)S(1)}, f32[6,16,128]{2,1,0:T(8,128)S(1)}, u32[]{:S(2)}, u32[]{:S(2)}) collective-permute-start(f32[6,16,128]{2,1,0:T(8,128)S(1)} %get-tuple-element.28), channel_id=1, source_target_pairs={{0,7},{1,2},{2,1},{3,4},{4,3},{5,6},{6,5},{7,0},{8,15},{9,10},{10,... | collective-permute-start | bytes 147464 | tf_op jit(solution)/shard_map/ppermute | solution.py:310
  31.6 3.6 %collective-permute-start.8 = (f32[6,16,128]{2,1,0:T(8,128)S(1)}, f32[6,16,128]{2,1,0:T(8,128)S(1)}, u32[]{:S(2)}, u32[]{:S(2)}) collective-permute-start(f32[6,16,128]{2,1,0:T(8,128)S(1)} %get-tuple-element.29), channel_id=1, source_target_pairs={{0,1},{1,0},{2,3},{3,2},{4,5},{5,4},{6,7},{7,6},{8,9},{9,8},{10,11... | collective-permute-start | bytes 147464 | tf_op jit(solution)/shard_map/ppermute | solution.py:240
  33.6 1.7 %copy-start.4 = (f32[16,128]{1,0:T(8,128)S(1)}, f32[16,128]{1,0:T(8,128)}, u32[]{:S(2)}) copy-start(f32[16,128]{1,0:T(8,128)} %rot_ref.1) | copy-start | bytes 24580
  36.1 29.2 %copy-start = (f32[16,8,16,128]{3,2,1,0:T(8,128)S(1)}, f32[16,8,16,128]{3,2,1,0:T(8,128)}, u32[]{:S(2)}) copy-start(f32[16,8,16,128]{3,2,1,0:T(8,128)} %param.7) | copy-start | bytes 3145732
  36.1 1.2 %collective-permute-start.11 = (f32[32,128]{1,0:T(8,128)S(1)}, f32[32,128]{1,0:T(8,128)S(1)}, u32[]{:S(2)}, u32[]{:S(2)}) collective-permute-start(f32[32,128]{1,0:T(8,128)S(1)} %get-tuple-element.32), channel_id=1, source_target_pairs={{0,1},{1,0},{2,3},{3,2},{4,5},{5,4},{6,7},{7,6},{8,9},{9,8},{10,11... | collective-permute-start | bytes 49160 | tf_op jit(solution)/shard_map/ppermute | solution.py:240
  37.3 4.5 %collective-permute-start.14 = (f32[16,128]{1,0:T(8,128)S(1)}, f32[16,128]{1,0:T(8,128)S(1)}, u32[]{:S(2)}, u32[]{:S(2)}) collective-permute-start(f32[16,128]{1,0:T(8,128)S(1)} %slice.23), channel_id=1, source_target_pairs={{0,24},{8,16},{16,8},{24,0},{1,25},{9,17},{17,9},{25,1},{2,26},{10... | collective-permute-start | bytes 24584 | tf_op jit(solution)/shard_map/ppermute | solution.py:240
  39.0 3.7 %collective-permute-start.13 = (f32[16,128]{1,0:T(8,128)S(1)}, f32[16,128]{1,0:T(8,128)S(1)}, u32[]{:S(2)}, u32[]{:S(2)}) collective-permute-start(f32[16,128]{1,0:T(8,128)S(1)} %slice.23), channel_id=1, source_target_pairs={{0,16},{8,24},{16,0},{24,8},{1,17},{9,25},{17,1},{25,9},{2,18},{10... | collective-permute-start | bytes 24584 | tf_op jit(solution)/shard_map/ppermute | solution.py:240
  40.2 3.7 %collective-permute-start.12 = (f32[16,128]{1,0:T(8,128)S(1)}, f32[16,128]{1,0:T(8,128)S(1)}, u32[]{:S(2)}, u32[]{:S(2)}) collective-permute-start(f32[16,128]{1,0:T(8,128)S(1)} %slice.23), channel_id=1, source_target_pairs={{0,8},{8,0},{16,24},{24,16},{1,9},{9,1},{17,25},{25,17},{2,10},{10... | collective-permute-start | bytes 24584 | tf_op jit(solution)/shard_map/ppermute | solution.py:240
  43.9 5.6 %collective-permute-start.17 = (f32[32,128]{1,0:T(8,128)S(1)}, f32[32,128]{1,0:T(8,128)S(1)}, u32[]{:S(2)}, u32[]{:S(2)}) collective-permute-start(f32[32,128]{1,0:T(8,128)S(1)} %dom.1.refs_0_), channel_id=1, source_target_pairs={{0,6},{1,7},{2,4},{3,5},{4,2},{5,3},{6,0},{7,1},{8,14},{9,15},{10,... | collective-permute-start | bytes 49160 | tf_op jit(solution)/shard_map/ppermute | solution.py:240
  46.0 4.8 %collective-permute-start.16 = (f32[32,128]{1,0:T(8,128)S(1)}, f32[32,128]{1,0:T(8,128)S(1)}, u32[]{:S(2)}, u32[]{:S(2)}) collective-permute-start(f32[32,128]{1,0:T(8,128)S(1)} %dom.1.refs_0_), channel_id=1, source_target_pairs={{0,4},{1,5},{2,6},{3,7},{4,0},{5,1},{6,2},{7,3},{8,12},{9,13},{10,... | collective-permute-start | bytes 49160 | tf_op jit(solution)/shard_map/ppermute | solution.py:240
  49.0 3.7 %collective-permute-start.15 = (f32[32,128]{1,0:T(8,128)S(1)}, f32[32,128]{1,0:T(8,128)S(1)}, u32[]{:S(2)}, u32[]{:S(2)}) collective-permute-start(f32[32,128]{1,0:T(8,128)S(1)} %dom.1.refs_0_), channel_id=1, source_target_pairs={{0,2},{1,3},{2,0},{3,1},{4,6},{5,7},{6,4},{7,5},{8,10},{9,11},{10,... | collective-permute-start | bytes 49160 | tf_op jit(solution)/shard_map/ppermute | solution.py:240
  53.0 10.3 %collective-permute-start.23 = (f32[16,16,128]{2,1,0:T(8,128)S(1)}, f32[16,16,128]{2,1,0:T(8,128)S(1)}, u32[]{:S(2)}, u32[]{:S(2)}) collective-permute-start(f32[16,16,128]{2,1,0:T(8,128)S(1)} %remove.1.refs_0_), channel_id=1, source_target_pairs={{0,4},{1,5},{2,6},{3,7},{4,0},{5,1},{6,2},{7,3},{8,12},{9,13},{10,... | collective-permute-start | bytes 393224 | tf_op jit(solution)/shard_map/ppermute | solution.py:240
  54.6 8.7 %collective-permute-start.21 = (f32[16,16,128]{2,1,0:T(8,128)S(1)}, f32[16,16,128]{2,1,0:T(8,128)S(1)}, u32[]{:S(2)}, u32[]{:S(2)}) collective-permute-start(f32[16,16,128]{2,1,0:T(8,128)S(1)} %remove.1.refs_0_), channel_id=1, source_target_pairs={{0,6},{1,7},{2,4},{3,5},{4,2},{5,3},{6,0},{7,1},{8,14},{9,15},{10,... | collective-permute-start | bytes 393224 | tf_op jit(solution)/shard_map/ppermute | solution.py:240
  56.8 7.1 %collective-permute-start.19 = (f32[16,16,128]{2,1,0:T(8,128)S(1)}, f32[16,16,128]{2,1,0:T(8,128)S(1)}, u32[]{:S(2)}, u32[]{:S(2)}) collective-permute-start(f32[16,16,128]{2,1,0:T(8,128)S(1)} %remove.1.refs_0_), channel_id=1, source_target_pairs={{0,2},{1,3},{2,0},{3,1},{4,6},{5,7},{6,4},{7,5},{8,10},{9,11},{10,... | collective-permute-start | bytes 393224 | tf_op jit(solution)/shard_map/ppermute | solution.py:240
  56.8 7.5 %collective-permute-start.18 = (f32[16,16,128]{2,1,0:T(8,128)S(1)}, f32[16,16,128]{2,1,0:T(8,128)S(1)}, u32[]{:S(2)}, u32[]{:S(2)}) collective-permute-start(f32[16,16,128]{2,1,0:T(8,128)S(1)} %remove.1.refs_0_), channel_id=1, source_target_pairs={{0,1},{1,0},{2,3},{3,2},{4,5},{5,4},{6,7},{7,6},{8,9},{9,8},{10,11... | collective-permute-start | bytes 393224 | tf_op jit(solution)/shard_map/ppermute | solution.py:240
  63.3 1.3 %collective-permute-start.24 = (f32[16,16,128]{2,1,0:T(8,128)S(1)}, f32[16,16,128]{2,1,0:T(8,128)S(1)}, u32[]{:S(2)}, u32[]{:S(2)}) collective-permute-start(f32[16,16,128]{2,1,0:T(8,128)S(1)} %collective-permute-done.23.refs_7_), channel_id=1, source_target_pairs={{0,1},{1,0},{2,3},{3,2},{4,5},{5,4},{6,7},{7,6},{8,9},{9,8},{10,11... | collective-permute-start | bytes 393224 | tf_op jit(solution)/shard_map/ppermute | solution.py:240
  63.3 1.5 %collective-permute-start.22 = (f32[16,16,128]{2,1,0:T(8,128)S(1)}, f32[16,16,128]{2,1,0:T(8,128)S(1)}, u32[]{:S(2)}, u32[]{:S(2)}) collective-permute-start(f32[16,16,128]{2,1,0:T(8,128)S(1)} %collective-permute-done.21.refs_5_), channel_id=1, source_target_pairs={{0,1},{1,0},{2,3},{3,2},{4,5},{5,4},{6,7},{7,6},{8,9},{9,8},{10,11... | collective-permute-start | bytes 393224 | tf_op jit(solution)/shard_map/ppermute | solution.py:240
  63.9 1.3 %collective-permute-start.20 = (f32[16,16,128]{2,1,0:T(8,128)S(1)}, f32[16,16,128]{2,1,0:T(8,128)S(1)}, u32[]{:S(2)}, u32[]{:S(2)}) collective-permute-start(f32[16,16,128]{2,1,0:T(8,128)S(1)} %collective-permute-done.19.refs_2_), channel_id=1, source_target_pairs={{0,1},{1,0},{2,3},{3,2},{4,5},{5,4},{6,7},{7,6},{8,9},{9,8},{10,11... | collective-permute-start | bytes 393224 | tf_op jit(solution)/shard_map/ppermute | solution.py:240

commit v2 on v1

--- a/solution.py
+++ b/solution.py
@@ -341,7 +341,7 @@
         compiler_params=params(),
         name="dom",
     )(part, *[swap(part[:nb], "dom", k) for k in range(1, doms)])
-    sums = [part] + [swap(part, "orb", k) for k in range(2, blocks, 2)]
+    sums = [part] + [swap(part, "orb", k) for k in sorted(range(2, blocks, 2), key=lambda k: (k != half, k))]
 
     own = pl.pallas_call(
         remove_kernel,

time: 67.2 us -> 68.1 us (1.013)
  waiting for transfers between devices: 29.6 us -> 30.8 us
    ppermute x22, waiting for transfers between devices: 28.4 us -> 29.6 us  [swap(): return lax.ppermute(value, axis, [(i, i ^ k) for i in range(count)])]
  transfers between devices with their start and end apart: 25 -> 25, of which waited for: 15 -> 14; matrix products, arithmetic and copies ran while one was open for 0% -> 0% of each run, Pallas kernels for 1% -> 1%
where the time goes in v2:
time: 68.1 us; the launch traced here: 67.9 us
  waiting for transfers between devices  30.8 us (45%)
  starting transfers between devices  29.5 us (43%)
  Pallas kernels  5.48 us (8%)
  between operations  2.1 us (3%)
    ppermute x22, waiting for transfers between devices, swap(): return lax.ppermute(value, axis, [(i, i ^ k) for i in range(count)])  29.6 us
    ppermute x22, starting transfers between devices, swap(): return lax.ppermute(value, axis, [(i, i ^ k) for i in range(count)])  24.9 us
    pallas_call x1, Pallas kernels, per_device(): pl.pallas_call(functools.partial(update_kernel, blocks, sequence), out_sh...  1.77 us
    ppermute x1, starting transfers between devices, per_device(): x_before = lax.ppermute(last, 'dom', up(doms))  1.71 us
    ppermute x1, starting transfers between devices, per_device(): lax.ppermute(far, 'orb', [(o, (o + 2 * (o % 2) - 1) % blocks) for o in ra...  1.68 us
    pallas_call x1, Pallas kernels, per_device(): pl.pallas_call(functools.partial(pack_kernel, blocks), out_shape=[shape(2...  1.65 us
  transfers between devices with their start and end apart: 25, of which 14 were waited for; matrix products, arithmetic and copies ran while one was open for 0% of the time, Pallas kernels for 1%

profile of v2, /device:TPU:0, one launch (start us, length us, event | category | flops | bytes accessed | tf_op | source)
XLA Modules:
  0.0 67.9 jit_solution(1987299801577920599)
XLA Ops:
  0.6 1.7 %pack.1 = (f32[2,16,16,128]{3,2,1,0:T(8,128)S(1)}, f32[2,16,16,128]{3,2,1,0:T(8,128)S(1)}, f32[2,16,16,128]{3,2,1,0:T(8,128)S(1)}, f32[2,16,16,128]{3,2,1,0:T(8,128)S(1)}) custom-call(f32[16,128,128]{2,1,0:T(8,128)} %bitcast.12), custom_call_target="tpu_custom_call" | custom-call | tf_op jit(solution)/shard_map/pack/pallas_call | solution.py:268
  2.3 4.1 %collective-permute-start.2 = (f32[2,16,16,128]{3,2,1,0:T(8,128)S(1)}, f32[2,16,16,128]{3,2,1,0:T(8,128)S(1)}, u32[]{:S(2)}, u32[]{:S(2)}) collective-permute-start(f32[2,16,16,128]{3,2,1,0:T(8,128)S(1)} %get-tuple-element.21), channel_id=1, source_target_pairs={{0,4},{1,5},{2,6},{3,7},{4,0},{5,1},{6,2},{7,3},{8,12},{9,13},{10,... | collective-permute-start | bytes 786440 | tf_op jit(solution)/shard_map/ppermute | solution.py:240
  6.5 1.6 %collective-permute-start.4 = (f32[2,16,16,128]{3,2,1,0:T(8,128)S(1)}, f32[2,16,16,128]{3,2,1,0:T(8,128)S(1)}, u32[]{:S(2)}, u32[]{:S(2)}) collective-permute-start(f32[2,16,16,128]{3,2,1,0:T(8,128)S(1)} %get-tuple-element.22), channel_id=1, source_target_pairs={{0,2},{1,3},{2,0},{3,1},{4,6},{5,7},{6,4},{7,5},{8,10},{9,11},{10,... | collective-permute-start | bytes 786440 | tf_op jit(solution)/shard_map/ppermute | solution.py:240
  8.2 3.3 %collective-permute-start = (f32[16,16,128]{2,1,0:T(8,128)S(1)}, f32[16,16,128]{2,1,0:T(8,128)S(1)}, u32[]{:S(2)}, u32[]{:S(2)}) collective-permute-start(f32[16,16,128]{2,1,0:T(8,128)S(1)} %get-tuple-element.39), channel_id=1, source_target_pairs={{0,7},{1,6},{2,5},{3,4},{4,3},{5,2},{6,1},{7,0},{8,15},{9,14},{10,... | collective-permute-start | bytes 393224 | tf_op jit(solution)/shard_map/ppermute | solution.py:240
  12.8 7.2 %collective-permute-done.2.refs_5_ = f32[2,16,16,128]{3,2,1,0:T(8,128)S(1)} collective-permute-done((f32[2,16,16,128]{3,2,1,0:T(8,128)S(1)}, f32[2,16,16,128]{3,2,1,0:T(8,128)S(1)}, u32[]{:S(2)}, u32[]{:S(2)}) %collective-permute-start.2) | collective-permute-done | bytes 262176 | tf_op jit(solution)/shard_map/ppermute | solution.py:240
  20.1 5.1 %collective-permute-done.4.pair_ref.refs_6_ = f32[2,16,16,128]{3,2,1,0:T(8,128)S(1)} collective-permute-done((f32[2,16,16,128]{3,2,1,0:T(8,128)S(1)}, f32[2,16,16,128]{3,2,1,0:T(8,128)S(1)}, u32[]{:S(2)}, u32[]{:S(2)}) %collective-permute-start.4) | collective-permute-done | bytes 262176 | tf_op jit(solution)/shard_map/ppermute | solution.py:240
  25.4 1.3 %collective-permute-done.5.refs_3_ = f32[16,16,128]{2,1,0:T(8,128)S(1)} collective-permute-done((f32[16,16,128]{2,1,0:T(8,128)S(1)}, f32[16,16,128]{2,1,0:T(8,128)S(1)}, u32[]{:S(2)}, u32[]{:S(2)}) %collective-permute-start.5) | collective-permute-done | bytes 131104 | tf_op jit(solution)/shard_map/ppermute | solution.py:240
  26.9 1.7 %collective-permute-start.9 = (f32[192,128]{1,0:T(8,128)S(1)}, f32[192,128]{1,0:T(8,128)S(1)}, u32[]{:S(2)}, u32[]{:S(2)}) collective-permute-start(f32[192,128]{1,0:T(8,128)S(1)} %get-tuple-element.30), channel_id=1, source_target_pairs={{0,8},{8,16},{16,24},{24,0},{1,9},{9,17},{17,25},{25,1},{2,10},{10... | collective-permute-start | bytes 294920 | tf_op jit(solution)/shard_map/ppermute | solution.py:307
  28.7 1.3 %collective-permute-start.10 = (f32[192,128]{1,0:T(8,128)S(1)}, f32[192,128]{1,0:T(8,128)S(1)}, u32[]{:S(2)}, u32[]{:S(2)}) collective-permute-start(f32[192,128]{1,0:T(8,128)S(1)} %get-tuple-element.31), channel_id=1, source_target_pairs={{0,24},{8,0},{16,8},{24,16},{1,25},{9,1},{17,9},{25,17},{2,26},{10... | collective-permute-start | bytes 294920 | tf_op jit(solution)/shard_map/ppermute | solution.py:308
  29.9 1.7 %collective-permute-start.7 = (f32[6,16,128]{2,1,0:T(8,128)S(1)}, f32[6,16,128]{2,1,0:T(8,128)S(1)}, u32[]{:S(2)}, u32[]{:S(2)}) collective-permute-start(f32[6,16,128]{2,1,0:T(8,128)S(1)} %get-tuple-element.28), channel_id=1, source_target_pairs={{0,7},{1,2},{2,1},{3,4},{4,3},{5,6},{6,5},{7,0},{8,15},{9,10},{10,... | collective-permute-start | bytes 147464 | tf_op jit(solution)/shard_map/ppermute | solution.py:310
  31.6 2.0 %collective-permute-start.8 = (f32[6,16,128]{2,1,0:T(8,128)S(1)}, f32[6,16,128]{2,1,0:T(8,128)S(1)}, u32[]{:S(2)}, u32[]{:S(2)}) collective-permute-start(f32[6,16,128]{2,1,0:T(8,128)S(1)} %get-tuple-element.29), channel_id=1, source_target_pairs={{0,1},{1,0},{2,3},{3,2},{4,5},{5,4},{6,7},{7,6},{8,9},{9,8},{10,11... | collective-permute-start | bytes 147464 | tf_op jit(solution)/shard_map/ppermute | solution.py:240
  33.7 0.4 split.1
  34.1 1.2 %collective-permute-done.7.far_ref = f32[6,16,128]{2,1,0:T(8,128)S(1)} collective-permute-done((f32[6,16,128]{2,1,0:T(8,128)S(1)}, f32[6,16,128]{2,1,0:T(8,128)S(1)}, u32[]{:S(2)}, u32[]{:S(2)}) %collective-permute-start.7) | collective-permute-done | bytes 49184 | tf_op jit(solution)/shard_map/ppermute | solution.py:310
  35.3 0.8 %project.1 = (f32[16,16,128]{2,1,0:T(8,128)S(1)}, f32[32,128]{1,0:T(8,128)S(1)}) custom-call(s32[1]{0:T(128)S(6)} %copy.10.owner_ref, f32[16,128]{1,0:T(8,128)S(1)} %copy-done.4, bf16[128,2048]{1,0:T(8,128)(2,1)S(1)} %get-tuple-element.25.xh_ref, bf16[128,2048]{1,0:T(8,128)(2,1)S(1)} %get-tuple-element.26.xl_ref, ...), custom_call_target="tpu_custom_call" | custom-call | tf_op jit(solution)/shard_map/project/pallas_call | solution.py:325
  36.4 0.9 %collective-permute-done.11 = f32[32,128]{1,0:T(8,128)S(1)} collective-permute-done((f32[32,128]{1,0:T(8,128)S(1)}, f32[32,128]{1,0:T(8,128)S(1)}, u32[]{:S(2)}, u32[]{:S(2)}) %collective-permute-start.11) | collective-permute-done | bytes 16416 | tf_op jit(solution)/shard_map/ppermute | solution.py:240
  37.3 1.7 %collective-permute-start.14 = (f32[16,128]{1,0:T(8,128)S(1)}, f32[16,128]{1,0:T(8,128)S(1)}, u32[]{:S(2)}, u32[]{:S(2)}) collective-permute-start(f32[16,128]{1,0:T(8,128)S(1)} %slice.23), channel_id=1, source_target_pairs={{0,24},{8,16},{16,8},{24,0},{1,25},{9,17},{17,9},{25,1},{2,26},{10... | collective-permute-start | bytes 24584 | tf_op jit(solution)/shard_map/ppermute | solution.py:240
  39.0 1.2 %collective-permute-start.13 = (f32[16,128]{1,0:T(8,128)S(1)}, f32[16,128]{1,0:T(8,128)S(1)}, u32[]{:S(2)}, u32[]{:S(2)}) collective-permute-start(f32[16,128]{1,0:T(8,128)S(1)} %slice.23), channel_id=1, source_target_pairs={{0,16},{8,24},{16,0},{24,8},{1,17},{9,25},{17,1},{25,9},{2,18},{10... | collective-permute-start | bytes 24584 | tf_op jit(solution)/shard_map/ppermute | solution.py:240
  40.3 0.5 collective-permute-start.12
  40.8 1.1 %collective-permute-done.14.refs_2_ = f32[16,128]{1,0:T(8,128)S(1)} collective-permute-done((f32[16,128]{1,0:T(8,128)S(1)}, f32[16,128]{1,0:T(8,128)S(1)}, u32[]{:S(2)}, u32[]{:S(2)}) %collective-permute-start.14) | collective-permute-done | bytes 8224 | tf_op jit(solution)/shard_map/ppermute | solution.py:240
  41.9 0.8 %collective-permute-done.13.refs_1_ = f32[16,128]{1,0:T(8,128)S(1)} collective-permute-done((f32[16,128]{1,0:T(8,128)S(1)}, f32[16,128]{1,0:T(8,128)S(1)}, u32[]{:S(2)}, u32[]{:S(2)}) %collective-permute-start.13) | collective-permute-done | bytes 8224 | tf_op jit(solution)/shard_map/ppermute | solution.py:240
  42.7 1.2 %collective-permute-done.12.refs_0_ = f32[16,128]{1,0:T(8,128)S(1)} collective-permute-done((f32[16,128]{1,0:T(8,128)S(1)}, f32[16,128]{1,0:T(8,128)S(1)}, u32[]{:S(2)}, u32[]{:S(2)}) %collective-permute-start.12) | collective-permute-done | bytes 8224 | tf_op jit(solution)/shard_map/ppermute | solution.py:240
  43.9 2.1 %collective-permute-start.17 = (f32[32,128]{1,0:T(8,128)S(1)}, f32[32,128]{1,0:T(8,128)S(1)}, u32[]{:S(2)}, u32[]{:S(2)}) collective-permute-start(f32[32,128]{1,0:T(8,128)S(1)} %dom.1.refs_0_), channel_id=1, source_target_pairs={{0,6},{1,7},{2,4},{3,5},{4,2},{5,3},{6,0},{7,1},{8,14},{9,15},{10,... | collective-permute-start | bytes 49160 | tf_op jit(solution)/shard_map/ppermute | solution.py:240
  46.0 3.4 %collective-permute-start.16 = (f32[32,128]{1,0:T(8,128)S(1)}, f32[32,128]{1,0:T(8,128)S(1)}, u32[]{:S(2)}, u32[]{:S(2)}) collective-permute-start(f32[32,128]{1,0:T(8,128)S(1)} %dom.1.refs_0_), channel_id=1, source_target_pairs={{0,2},{1,3},{2,0},{3,1},{4,6},{5,7},{6,4},{7,5},{8,10},{9,11},{10,... | collective-permute-start | bytes 49160 | tf_op jit(solution)/shard_map/ppermute | solution.py:240
  49.5 1.9 %collective-permute-done.16.refs_2_ = f32[32,128]{1,0:T(8,128)S(1)} collective-permute-done((f32[32,128]{1,0:T(8,128)S(1)}, f32[32,128]{1,0:T(8,128)S(1)}, u32[]{:S(2)}, u32[]{:S(2)}) %collective-permute-start.16) | collective-permute-done | bytes 16416 | tf_op jit(solution)/shard_map/ppermute | solution.py:240
  51.3 2.8 %collective-permute-done.15.refs_1_ = f32[32,128]{1,0:T(8,128)S(1)} collective-permute-done((f32[32,128]{1,0:T(8,128)S(1)}, f32[32,128]{1,0:T(8,128)S(1)}, u32[]{:S(2)}, u32[]{:S(2)}) %collective-permute-start.15) | collective-permute-done | bytes 16416 | tf_op jit(solution)/shard_map/ppermute | solution.py:240
  54.6 2.1 %collective-permute-start.21 = (f32[16,16,128]{2,1,0:T(8,128)S(1)}, f32[16,16,128]{2,1,0:T(8,128)S(1)}, u32[]{:S(2)}, u32[]{:S(2)}) collective-permute-start(f32[16,16,128]{2,1,0:T(8,128)S(1)} %remove.1.refs_0_), channel_id=1, source_target_pairs={{0,6},{1,7},{2,4},{3,5},{4,2},{5,3},{6,0},{7,1},{8,14},{9,15},{10,... | collective-permute-start | bytes 393224 | tf_op jit(solution)/shard_map/ppermute | solution.py:240
  56.8 1.1 %collective-permute-start.19 = (f32[16,16,128]{2,1,0:T(8,128)S(1)}, f32[16,16,128]{2,1,0:T(8,128)S(1)}, u32[]{:S(2)}, u32[]{:S(2)}) collective-permute-start(f32[16,16,128]{2,1,0:T(8,128)S(1)} %remove.1.refs_0_), channel_id=1, source_target_pairs={{0,2},{1,3},{2,0},{3,1},{4,6},{5,7},{6,4},{7,5},{8,10},{9,11},{10,... | collective-permute-start | bytes 393224 | tf_op jit(solution)/shard_map/ppermute | solution.py:240
  57.9 6.4 %collective-permute-done.23.refs_7_ = f32[16,16,128]{2,1,0:T(8,128)S(1)} collective-permute-done((f32[16,16,128]{2,1,0:T(8,128)S(1)}, f32[16,16,128]{2,1,0:T(8,128)S(1)}, u32[]{:S(2)}, u32[]{:S(2)}) %collective-permute-start.23) | collective-permute-done | bytes 131104 | tf_op jit(solution)/shard_map/ppermute | solution.py:240
  64.3 0.5 collective-permute-start.22
  64.9 0.4 mixing.1
  65.3 0.4 collective-permute-done.24.refs_6_
  66.2 1.8 %update.1 = (f32[16,128,128]{2,1,0:T(8,128)}, f32[16,128,128]{2,1,0:T(8,128)}) custom-call(bf16[128,128]{1,0:T(8,128)(2,1)S(1)} %get-tuple-element.33.wh_ref, bf16[128,128]{1,0:T(8,128)(2,1)S(1)} %get-tuple-element.34.wl_ref, f32[16,128,128]{2,1,0:T(8,128)S(1)} %bitcast.13, f32[16,16,128]{2,1,0:T(8,128)S(1)} %remove.1.refs_0_, ...), custom_call_target="tpu_custom_call" | custom-call | tf_op jit(solution)/shard_map/update/pallas_call | solution.py:372
  (42 shorter events, 2.1 us)
Async XLA Ops:
  2.3 17.8 %collective-permute-start.2 = (f32[2,16,16,128]{3,2,1,0:T(8,128)S(1)}, f32[2,16,16,128]{3,2,1,0:T(8,128)S(1)}, u32[]{:S(2)}, u32[]{:S(2)}) collective-permute-start(f32[2,16,16,128]{3,2,1,0:T(8,128)S(1)} %get-tuple-element.21), channel_id=1, source_target_pairs={{0,4},{1,5},{2,6},{3,7},{4,0},{5,1},{6,2},{7,3},{8,12},{9,13},{10,... | collective-permute-start | bytes 786440 | tf_op jit(solution)/shard_map/ppermute | solution.py:240
  6.4 19.0 %collective-permute-start.6 = (f32[16,16,128]{2,1,0:T(8,128)S(1)}, f32[16,16,128]{2,1,0:T(8,128)S(1)}, u32[]{:S(2)}, u32[]{:S(2)}) collective-permute-start(f32[16,16,128]{2,1,0:T(8,128)S(1)} %slice_bitcast_fusion.1), channel_id=1, source_target_pairs={{0,1},{1,0},{2,3},{3,2},{4,5},{5,4},{6,7},{7,6},{8,9},{9,8},{10,11... | collective-permute-start | bytes 393224 | tf_op jit(solution)/shard_map/ppermute | solution.py:240
  6.5 18.8 %collective-permute-start.4 = (f32[2,16,16,128]{3,2,1,0:T(8,128)S(1)}, f32[2,16,16,128]{3,2,1,0:T(8,128)S(1)}, u32[]{:S(2)}, u32[]{:S(2)}) collective-permute-start(f32[2,16,16,128]{3,2,1,0:T(8,128)S(1)} %get-tuple-element.22), channel_id=1, source_target_pairs={{0,2},{1,3},{2,0},{3,1},{4,6},{5,7},{6,4},{7,5},{8,10},{9,11},{10,... | collective-permute-start | bytes 786440 | tf_op jit(solution)/shard_map/ppermute | solution.py:240
  8.1 17.3 %collective-permute-start.1 = (f32[16,16,128]{2,1,0:T(8,128)S(1)}, f32[16,16,128]{2,1,0:T(8,128)S(1)}, u32[]{:S(2)}, u32[]{:S(2)}) collective-permute-start(f32[16,16,128]{2,1,0:T(8,128)S(1)} %get-tuple-element.38), channel_id=1, source_target_pairs={{0,6},{1,7},{2,4},{3,5},{4,2},{5,3},{6,0},{7,1},{8,14},{9,15},{10,... | collective-permute-start | bytes 393224 | tf_op jit(solution)/shard_map/ppermute | solution.py:240
  8.2 17.2 %collective-permute-start = (f32[16,16,128]{2,1,0:T(8,128)S(1)}, f32[16,16,128]{2,1,0:T(8,128)S(1)}, u32[]{:S(2)}, u32[]{:S(2)}) collective-permute-start(f32[16,16,128]{2,1,0:T(8,128)S(1)} %get-tuple-element.39), channel_id=1, source_target_pairs={{0,7},{1,6},{2,5},{3,4},{4,3},{5,2},{6,1},{7,0},{8,15},{9,14},{10,... | collective-permute-start | bytes 393224 | tf_op jit(solution)/shard_map/ppermute | solution.py:240
  20.1 5.4 %collective-permute-start.3 = (f32[16,16,128]{2,1,0:T(8,128)S(1)}, f32[16,16,128]{2,1,0:T(8,128)S(1)}, u32[]{:S(2)}, u32[]{:S(2)}) collective-permute-start(f32[16,16,128]{2,1,0:T(8,128)S(1)} %slice_bitcast_fusion), channel_id=1, source_target_pairs={{0,1},{1,0},{2,3},{3,2},{4,5},{5,4},{6,7},{7,6},{8,9},{9,8},{10,11... | collective-permute-start | bytes 393224 | tf_op jit(solution)/shard_map/ppermute | solution.py:240
  25.3 8.3 %copy-start.1 = (bf16[384,128]{1,0:T(8,128)(2,1)S(1)}, bf16[384,128]{1,0:T(8,128)(2,1)}, u32[]{:S(2)}) copy-start(bf16[384,128]{1,0:T(8,128)(2,1)} %constant.5.clone.wl_ref) | copy-start | bytes 294916
  25.3 8.3 %copy-start.2 = (bf16[384,128]{1,0:T(8,128)(2,1)S(1)}, bf16[384,128]{1,0:T(8,128)(2,1)}, u32[]{:S(2)}) copy-start(bf16[384,128]{1,0:T(8,128)(2,1)} %constant.4.clone.wh_ref) | copy-start | bytes 294916
  25.3 8.3 %copy-start.3 = (f32[8,16,128]{2,1,0:T(8,128)S(1)}, f32[8,16,128]{2,1,0:T(8,128)}, u32[]{:S(2)}) copy-start(f32[8,16,128]{2,1,0:T(8,128)} %param.8) | copy-start | bytes 196612
  25.3 1.4 %collective-permute-start.5 = (f32[16,16,128]{2,1,0:T(8,128)S(1)}, f32[16,16,128]{2,1,0:T(8,128)S(1)}, u32[]{:S(2)}, u32[]{:S(2)}) collective-permute-start(f32[16,16,128]{2,1,0:T(8,128)S(1)} %hand.1), channel_id=1, source_target_pairs={{0,1},{1,0},{2,3},{3,2},{4,5},{5,4},{6,7},{7,6},{8,9},{9,8},{10,11... | collective-permute-start | bytes 393224 | tf_op jit(solution)/shard_map/ppermute | solution.py:240
  26.9 8.3 %collective-permute-start.9 = (f32[192,128]{1,0:T(8,128)S(1)}, f32[192,128]{1,0:T(8,128)S(1)}, u32[]{:S(2)}, u32[]{:S(2)}) collective-permute-start(f32[192,128]{1,0:T(8,128)S(1)} %get-tuple-element.30), channel_id=1, source_target_pairs={{0,8},{8,16},{16,24},{24,0},{1,9},{9,17},{17,25},{25,1},{2,10},{10... | collective-permute-start | bytes 294920 | tf_op jit(solution)/shard_map/ppermute | solution.py:307
  28.7 6.6 %collective-permute-start.10 = (f32[192,128]{1,0:T(8,128)S(1)}, f32[192,128]{1,0:T(8,128)S(1)}, u32[]{:S(2)}, u32[]{:S(2)}) collective-permute-start(f32[192,128]{1,0:T(8,128)S(1)} %get-tuple-element.31), channel_id=1, source_target_pairs={{0,24},{8,0},{16,8},{24,16},{1,25},{9,1},{17,9},{25,17},{2,26},{10... | collective-permute-start | bytes 294920 | tf_op jit(solution)/shard_map/ppermute | solution.py:308
  29.9 5.3 %collective-permute-start.7 = (f32[6,16,128]{2,1,0:T(8,128)S(1)}, f32[6,16,128]{2,1,0:T(8,128)S(1)}, u32[]{:S(2)}, u32[]{:S(2)}) collective-permute-start(f32[6,16,128]{2,1,0:T(8,128)S(1)} %get-tuple-element.28), channel_id=1, source_target_pairs={{0,7},{1,2},{2,1},{3,4},{4,3},{5,6},{6,5},{7,0},{8,15},{9,10},{10,... | collective-permute-start | bytes 147464 | tf_op jit(solution)/shard_map/ppermute | solution.py:310
  31.6 3.7 %collective-permute-start.8 = (f32[6,16,128]{2,1,0:T(8,128)S(1)}, f32[6,16,128]{2,1,0:T(8,128)S(1)}, u32[]{:S(2)}, u32[]{:S(2)}) collective-permute-start(f32[6,16,128]{2,1,0:T(8,128)S(1)} %get-tuple-element.29), channel_id=1, source_target_pairs={{0,1},{1,0},{2,3},{3,2},{4,5},{5,4},{6,7},{7,6},{8,9},{9,8},{10,11... | collective-permute-start | bytes 147464 | tf_op jit(solution)/shard_map/ppermute | solution.py:240
  33.6 1.6 %copy-start.4 = (f32[16,128]{1,0:T(8,128)S(1)}, f32[16,128]{1,0:T(8,128)}, u32[]{:S(2)}) copy-start(f32[16,128]{1,0:T(8,128)} %rot_ref.1) | copy-start | bytes 24580
  36.1 30.1 %copy-start = (f32[16,8,16,128]{3,2,1,0:T(8,128)S(1)}, f32[16,8,16,128]{3,2,1,0:T(8,128)}, u32[]{:S(2)}) copy-start(f32[16,8,16,128]{3,2,1,0:T(8,128)} %param.7) | copy-start | bytes 3145732
  36.1 1.2 %collective-permute-start.11 = (f32[32,128]{1,0:T(8,128)S(1)}, f32[32,128]{1,0:T(8,128)S(1)}, u32[]{:S(2)}, u32[]{:S(2)}) collective-permute-start(f32[32,128]{1,0:T(8,128)S(1)} %get-tuple-element.32), channel_id=1, source_target_pairs={{0,1},{1,0},{2,3},{3,2},{4,5},{5,4},{6,7},{7,6},{8,9},{9,8},{10,11... | collective-permute-start | bytes 49160 | tf_op jit(solution)/shard_map/ppermute | solution.py:240
  37.3 4.5 %collective-permute-start.14 = (f32[16,128]{1,0:T(8,128)S(1)}, f32[16,128]{1,0:T(8,128)S(1)}, u32[]{:S(2)}, u32[]{:S(2)}) collective-permute-start(f32[16,128]{1,0:T(8,128)S(1)} %slice.23), channel_id=1, source_target_pairs={{0,24},{8,16},{16,8},{24,0},{1,25},{9,17},{17,9},{25,1},{2,26},{10... | collective-permute-start | bytes 24584 | tf_op jit(solution)/shard_map/ppermute | solution.py:240
  39.0 3.7 %collective-permute-start.13 = (f32[16,128]{1,0:T(8,128)S(1)}, f32[16,128]{1,0:T(8,128)S(1)}, u32[]{:S(2)}, u32[]{:S(2)}) collective-permute-start(f32[16,128]{1,0:T(8,128)S(1)} %slice.23), channel_id=1, source_target_pairs={{0,16},{8,24},{16,0},{24,8},{1,17},{9,25},{17,1},{25,9},{2,18},{10... | collective-permute-start | bytes 24584 | tf_op jit(solution)/shard_map/ppermute | solution.py:240
  40.3 3.7 %collective-permute-start.12 = (f32[16,128]{1,0:T(8,128)S(1)}, f32[16,128]{1,0:T(8,128)S(1)}, u32[]{:S(2)}, u32[]{:S(2)}) collective-permute-start(f32[16,128]{1,0:T(8,128)S(1)} %slice.23), channel_id=1, source_target_pairs={{0,8},{8,0},{16,24},{24,16},{1,9},{9,1},{17,25},{25,17},{2,10},{10... | collective-permute-start | bytes 24584 | tf_op jit(solution)/shard_map/ppermute | solution.py:240
  43.9 5.5 %collective-permute-start.17 = (f32[32,128]{1,0:T(8,128)S(1)}, f32[32,128]{1,0:T(8,128)S(1)}, u32[]{:S(2)}, u32[]{:S(2)}) collective-permute-start(f32[32,128]{1,0:T(8,128)S(1)} %dom.1.refs_0_), channel_id=1, source_target_pairs={{0,6},{1,7},{2,4},{3,5},{4,2},{5,3},{6,0},{7,1},{8,14},{9,15},{10,... | collective-permute-start | bytes 49160 | tf_op jit(solution)/shard_map/ppermute | solution.py:240
  46.0 5.3 %collective-permute-start.16 = (f32[32,128]{1,0:T(8,128)S(1)}, f32[32,128]{1,0:T(8,128)S(1)}, u32[]{:S(2)}, u32[]{:S(2)}) collective-permute-start(f32[32,128]{1,0:T(8,128)S(1)} %dom.1.refs_0_), channel_id=1, source_target_pairs={{0,2},{1,3},{2,0},{3,1},{4,6},{5,7},{6,4},{7,5},{8,10},{9,11},{10,... | collective-permute-start | bytes 49160 | tf_op jit(solution)/shard_map/ppermute | solution.py:240
  49.5 4.6 %collective-permute-start.15 = (f32[32,128]{1,0:T(8,128)S(1)}, f32[32,128]{1,0:T(8,128)S(1)}, u32[]{:S(2)}, u32[]{:S(2)}) collective-permute-start(f32[32,128]{1,0:T(8,128)S(1)} %dom.1.refs_0_), channel_id=1, source_target_pairs={{0,4},{1,5},{2,6},{3,7},{4,0},{5,1},{6,2},{7,3},{8,12},{9,13},{10,... | collective-permute-start | bytes 49160 | tf_op jit(solution)/shard_map/ppermute | solution.py:240
  54.3 9.9 %collective-permute-start.23 = (f32[16,16,128]{2,1,0:T(8,128)S(1)}, f32[16,16,128]{2,1,0:T(8,128)S(1)}, u32[]{:S(2)}, u32[]{:S(2)}) collective-permute-start(f32[16,16,128]{2,1,0:T(8,128)S(1)} %remove.1.refs_0_), channel_id=1, source_target_pairs={{0,4},{1,5},{2,6},{3,7},{4,0},{5,1},{6,2},{7,3},{8,12},{9,13},{10,... | collective-permute-start | bytes 393224 | tf_op jit(solution)/shard_map/ppermute | solution.py:240
  54.6 9.7 %collective-permute-start.21 = (f32[16,16,128]{2,1,0:T(8,128)S(1)}, f32[16,16,128]{2,1,0:T(8,128)S(1)}, u32[]{:S(2)}, u32[]{:S(2)}) collective-permute-start(f32[16,16,128]{2,1,0:T(8,128)S(1)} %remove.1.refs_0_), channel_id=1, source_target_pairs={{0,6},{1,7},{2,4},{3,5},{4,2},{5,3},{6,0},{7,1},{8,14},{9,15},{10,... | collective-permute-start | bytes 393224 | tf_op jit(solution)/shard_map/ppermute | solution.py:240
  56.8 8.0 %collective-permute-start.19 = (f32[16,16,128]{2,1,0:T(8,128)S(1)}, f32[16,16,128]{2,1,0:T(8,128)S(1)}, u32[]{:S(2)}, u32[]{:S(2)}) collective-permute-start(f32[16,16,128]{2,1,0:T(8,128)S(1)} %remove.1.refs_0_), channel_id=1, source_target_pairs={{0,2},{1,3},{2,0},{3,1},{4,6},{5,7},{6,4},{7,5},{8,10},{9,11},{10,... | collective-permute-start | bytes 393224 | tf_op jit(solution)/shard_map/ppermute | solution.py:240
  57.9 7.4 %collective-permute-start.18 = (f32[16,16,128]{2,1,0:T(8,128)S(1)}, f32[16,16,128]{2,1,0:T(8,128)S(1)}, u32[]{:S(2)}, u32[]{:S(2)}) collective-permute-start(f32[16,16,128]{2,1,0:T(8,128)S(1)} %remove.1.refs_0_), channel_id=1, source_target_pairs={{0,1},{1,0},{2,3},{3,2},{4,5},{5,4},{6,7},{7,6},{8,9},{9,8},{10,11... | collective-permute-start | bytes 393224 | tf_op jit(solution)/shard_map/ppermute | solution.py:240
  64.3 1.3 %collective-permute-start.24 = (f32[16,16,128]{2,1,0:T(8,128)S(1)}, f32[16,16,128]{2,1,0:T(8,128)S(1)}, u32[]{:S(2)}, u32[]{:S(2)}) collective-permute-start(f32[16,16,128]{2,1,0:T(8,128)S(1)} %collective-permute-done.23.refs_7_), channel_id=1, source_target_pairs={{0,1},{1,0},{2,3},{3,2},{4,5},{5,4},{6,7},{7,6},{8,9},{9,8},{10,11... | collective-permute-start | bytes 393224 | tf_op jit(solution)/shard_map/ppermute | solution.py:240
  64.3 1.5 %collective-permute-start.22 = (f32[16,16,128]{2,1,0:T(8,128)S(1)}, f32[16,16,128]{2,1,0:T(8,128)S(1)}, u32[]{:S(2)}, u32[]{:S(2)}) collective-permute-start(f32[16,16,128]{2,1,0:T(8,128)S(1)} %collective-permute-done.21.refs_5_), channel_id=1, source_target_pairs={{0,1},{1,0},{2,3},{3,2},{4,5},{5,4},{6,7},{7,6},{8,9},{9,8},{10,11... | collective-permute-start | bytes 393224 | tf_op jit(solution)/shard_map/ppermute | solution.py:240
  64.8 1.3 %collective-permute-start.20 = (f32[16,16,128]{2,1,0:T(8,128)S(1)}, f32[16,16,128]{2,1,0:T(8,128)S(1)}, u32[]{:S(2)}, u32[]{:S(2)}) collective-permute-start(f32[16,16,128]{2,1,0:T(8,128)S(1)} %collective-permute-done.19.refs_2_), channel_id=1, source_target_pairs={{0,1},{1,0},{2,3},{3,2},{4,5},{5,4},{6,7},{7,6},{8,9},{9,8},{10,11... | collective-permute-start | bytes 393224 | tf_op jit(solution)/shard_map/ppermute | solution.py:240

commit v3 on v1

--- a/solution.py
+++ b/solution.py
@@ -340,7 +340,7 @@
         out_specs=VMEM,
         compiler_params=params(),
         name="dom",
-    )(part, *[swap(part[:nb], "dom", k) for k in range(1, doms)])
+    )(part, *[swap(part[:nb], "dom", k) for k in sorted(range(1, doms), key=lambda k: (k.bit_count() > 1, -k))])
     sums = [part] + [swap(part, "orb", k) for k in range(2, blocks, 2)]
 
     own = pl.pallas_call(

time: 67.2 us -> 66.2 us (0.985)
  starting transfers between devices: 29.8 us -> 28.6 us
    ppermute x22, starting transfers between devices: 25.1 us -> 23.9 us  [swap(): return lax.ppermute(value, axis, [(i, i ^ k) for i in range(count)])]
  transfers between devices with their start and end apart: 25 -> 25, of which waited for: 15 -> 16; matrix products, arithmetic and copies ran while one was open for 0% -> 0% of each run, Pallas kernels for 1% -> 1%
where the time goes in v3:
time: 66.2 us; the launch traced here: 66 us
  waiting for transfers between devices  29.8 us (45%)
  starting transfers between devices  28.6 us (43%)
  Pallas kernels  5.47 us (8%)
  between operations  2.1 us (3%)
    ppermute x22, waiting for transfers between devices, swap(): return lax.ppermute(value, axis, [(i, i ^ k) for i in range(count)])  28.6 us
    ppermute x22, starting transfers between devices, swap(): return lax.ppermute(value, axis, [(i, i ^ k) for i in range(count)])  23.9 us
    pallas_call x1, Pallas kernels, per_device(): pl.pallas_call(functools.partial(update_kernel, blocks, sequence), out_sh...  1.77 us
    ppermute x1, starting transfers between devices, per_device(): x_before = lax.ppermute(last, 'dom', up(doms))  1.71 us
    ppermute x1, starting transfers between devices, per_device(): lax.ppermute(far, 'orb', [(o, (o + 2 * (o % 2) - 1) % blocks) for o in ra...  1.68 us
    pallas_call x1, Pallas kernels, per_device(): pl.pallas_call(functools.partial(pack_kernel, blocks), out_shape=[shape(2...  1.65 us
  transfers between devices with their start and end apart: 25, of which 16 were waited for; matrix products, arithmetic and copies ran while one was open for 0% of the time, Pallas kernels for 1%

profile of v3, /device:TPU:0, one launch (start us, length us, event | category | flops | bytes accessed | tf_op | source)
XLA Modules:
  0.0 66.0 jit_solution(10371246981779953689)
XLA Ops:
  0.6 1.7 %pack.1 = (f32[2,16,16,128]{3,2,1,0:T(8,128)S(1)}, f32[2,16,16,128]{3,2,1,0:T(8,128)S(1)}, f32[2,16,16,128]{3,2,1,0:T(8,128)S(1)}, f32[2,16,16,128]{3,2,1,0:T(8,128)S(1)}) custom-call(f32[16,128,128]{2,1,0:T(8,128)} %bitcast.12), custom_call_target="tpu_custom_call" | custom-call | tf_op jit(solution)/shard_map/pack/pallas_call | solution.py:268
  2.3 4.1 %collective-permute-start.2 = (f32[2,16,16,128]{3,2,1,0:T(8,128)S(1)}, f32[2,16,16,128]{3,2,1,0:T(8,128)S(1)}, u32[]{:S(2)}, u32[]{:S(2)}) collective-permute-start(f32[2,16,16,128]{3,2,1,0:T(8,128)S(1)} %get-tuple-element.21), channel_id=1, source_target_pairs={{0,4},{1,5},{2,6},{3,7},{4,0},{5,1},{6,2},{7,3},{8,12},{9,13},{10,... | collective-permute-start | bytes 786440 | tf_op jit(solution)/shard_map/ppermute | solution.py:240
  6.5 1.6 %collective-permute-start.4 = (f32[2,16,16,128]{3,2,1,0:T(8,128)S(1)}, f32[2,16,16,128]{3,2,1,0:T(8,128)S(1)}, u32[]{:S(2)}, u32[]{:S(2)}) collective-permute-start(f32[2,16,16,128]{3,2,1,0:T(8,128)S(1)} %get-tuple-element.22), channel_id=1, source_target_pairs={{0,2},{1,3},{2,0},{3,1},{4,6},{5,7},{6,4},{7,5},{8,10},{9,11},{10,... | collective-permute-start | bytes 786440 | tf_op jit(solution)/shard_map/ppermute | solution.py:240
  8.2 3.3 %collective-permute-start = (f32[16,16,128]{2,1,0:T(8,128)S(1)}, f32[16,16,128]{2,1,0:T(8,128)S(1)}, u32[]{:S(2)}, u32[]{:S(2)}) collective-permute-start(f32[16,16,128]{2,1,0:T(8,128)S(1)} %get-tuple-element.39), channel_id=1, source_target_pairs={{0,7},{1,6},{2,5},{3,4},{4,3},{5,2},{6,1},{7,0},{8,15},{9,14},{10,... | collective-permute-start | bytes 393224 | tf_op jit(solution)/shard_map/ppermute | solution.py:240
  12.8 7.2 %collective-permute-done.2.refs_5_ = f32[2,16,16,128]{3,2,1,0:T(8,128)S(1)} collective-permute-done((f32[2,16,16,128]{3,2,1,0:T(8,128)S(1)}, f32[2,16,16,128]{3,2,1,0:T(8,128)S(1)}, u32[]{:S(2)}, u32[]{:S(2)}) %collective-permute-start.2) | collective-permute-done | bytes 262176 | tf_op jit(solution)/shard_map/ppermute | solution.py:240
  20.1 5.1 %collective-permute-done.4.pair_ref.refs_6_ = f32[2,16,16,128]{3,2,1,0:T(8,128)S(1)} collective-permute-done((f32[2,16,16,128]{3,2,1,0:T(8,128)S(1)}, f32[2,16,16,128]{3,2,1,0:T(8,128)S(1)}, u32[]{:S(2)}, u32[]{:S(2)}) %collective-permute-start.4) | collective-permute-done | bytes 262176 | tf_op jit(solution)/shard_map/ppermute | solution.py:240
  25.4 1.3 %collective-permute-done.5.refs_3_ = f32[16,16,128]{2,1,0:T(8,128)S(1)} collective-permute-done((f32[16,16,128]{2,1,0:T(8,128)S(1)}, f32[16,16,128]{2,1,0:T(8,128)S(1)}, u32[]{:S(2)}, u32[]{:S(2)}) %collective-permute-start.5) | collective-permute-done | bytes 131104 | tf_op jit(solution)/shard_map/ppermute | solution.py:240
  26.9 1.7 %collective-permute-start.9 = (f32[192,128]{1,0:T(8,128)S(1)}, f32[192,128]{1,0:T(8,128)S(1)}, u32[]{:S(2)}, u32[]{:S(2)}) collective-permute-start(f32[192,128]{1,0:T(8,128)S(1)} %get-tuple-element.30), channel_id=1, source_target_pairs={{0,8},{8,16},{16,24},{24,0},{1,9},{9,17},{17,25},{25,1},{2,10},{10... | collective-permute-start | bytes 294920 | tf_op jit(solution)/shard_map/ppermute | solution.py:307
  28.7 1.3 %collective-permute-start.10 = (f32[192,128]{1,0:T(8,128)S(1)}, f32[192,128]{1,0:T(8,128)S(1)}, u32[]{:S(2)}, u32[]{:S(2)}) collective-permute-start(f32[192,128]{1,0:T(8,128)S(1)} %get-tuple-element.31), channel_id=1, source_target_pairs={{0,24},{8,0},{16,8},{24,16},{1,25},{9,1},{17,9},{25,17},{2,26},{10... | collective-permute-start | bytes 294920 | tf_op jit(solution)/shard_map/ppermute | solution.py:308
  29.9 1.7 %collective-permute-start.7 = (f32[6,16,128]{2,1,0:T(8,128)S(1)}, f32[6,16,128]{2,1,0:T(8,128)S(1)}, u32[]{:S(2)}, u32[]{:S(2)}) collective-permute-start(f32[6,16,128]{2,1,0:T(8,128)S(1)} %get-tuple-element.28), channel_id=1, source_target_pairs={{0,7},{1,2},{2,1},{3,4},{4,3},{5,6},{6,5},{7,0},{8,15},{9,10},{10,... | collective-permute-start | bytes 147464 | tf_op jit(solution)/shard_map/ppermute | solution.py:310
  31.6 2.0 %collective-permute-start.8 = (f32[6,16,128]{2,1,0:T(8,128)S(1)}, f32[6,16,128]{2,1,0:T(8,128)S(1)}, u32[]{:S(2)}, u32[]{:S(2)}) collective-permute-start(f32[6,16,128]{2,1,0:T(8,128)S(1)} %get-tuple-element.29), channel_id=1, source_target_pairs={{0,1},{1,0},{2,3},{3,2},{4,5},{5,4},{6,7},{7,6},{8,9},{9,8},{10,11... | collective-permute-start | bytes 147464 | tf_op jit(solution)/shard_map/ppermute | solution.py:240
  33.7 0.4 split.1
  34.1 1.2 %collective-permute-done.7.far_ref = f32[6,16,128]{2,1,0:T(8,128)S(1)} collective-permute-done((f32[6,16,128]{2,1,0:T(8,128)S(1)}, f32[6,16,128]{2,1,0:T(8,128)S(1)}, u32[]{:S(2)}, u32[]{:S(2)}) %collective-permute-start.7) | collective-permute-done | bytes 49184 | tf_op jit(solution)/shard_map/ppermute | solution.py:310
  35.3 0.8 %project.1 = (f32[16,16,128]{2,1,0:T(8,128)S(1)}, f32[32,128]{1,0:T(8,128)S(1)}) custom-call(s32[1]{0:T(128)S(6)} %copy.10.owner_ref, f32[16,128]{1,0:T(8,128)S(1)} %copy-done.4, bf16[128,2048]{1,0:T(8,128)(2,1)S(1)} %get-tuple-element.25.xh_ref, bf16[128,2048]{1,0:T(8,128)(2,1)S(1)} %get-tuple-element.26.xl_ref, ...), custom_call_target="tpu_custom_call" | custom-call | tf_op jit(solution)/shard_map/project/pallas_call | solution.py:325
  36.4 0.9 %collective-permute-done.11 = f32[32,128]{1,0:T(8,128)S(1)} collective-permute-done((f32[32,128]{1,0:T(8,128)S(1)}, f32[32,128]{1,0:T(8,128)S(1)}, u32[]{:S(2)}, u32[]{:S(2)}) %collective-permute-start.11) | collective-permute-done | bytes 16416 | tf_op jit(solution)/shard_map/ppermute | solution.py:240
  37.3 1.7 %collective-permute-start.14 = (f32[16,128]{1,0:T(8,128)S(1)}, f32[16,128]{1,0:T(8,128)S(1)}, u32[]{:S(2)}, u32[]{:S(2)}) collective-permute-start(f32[16,128]{1,0:T(8,128)S(1)} %slice.23), channel_id=1, source_target_pairs={{0,24},{8,16},{16,8},{24,0},{1,25},{9,17},{17,9},{25,1},{2,26},{10... | collective-permute-start | bytes 24584 | tf_op jit(solution)/shard_map/ppermute | solution.py:240
  39.0 1.4 %collective-permute-start.13 = (f32[16,128]{1,0:T(8,128)S(1)}, f32[16,128]{1,0:T(8,128)S(1)}, u32[]{:S(2)}, u32[]{:S(2)}) collective-permute-start(f32[16,128]{1,0:T(8,128)S(1)} %slice.23), channel_id=1, source_target_pairs={{0,8},{8,0},{16,24},{24,16},{1,9},{9,1},{17,25},{25,17},{2,10},{10... | collective-permute-start | bytes 24584 | tf_op jit(solution)/shard_map/ppermute | solution.py:240
  40.8 1.1 %collective-permute-done.14.refs_2_ = f32[16,128]{1,0:T(8,128)S(1)} collective-permute-done((f32[16,128]{1,0:T(8,128)S(1)}, f32[16,128]{1,0:T(8,128)S(1)}, u32[]{:S(2)}, u32[]{:S(2)}) %collective-permute-start.14) | collective-permute-done | bytes 8224 | tf_op jit(solution)/shard_map/ppermute | solution.py:240
  41.9 0.8 %collective-permute-done.13.refs_1_ = f32[16,128]{1,0:T(8,128)S(1)} collective-permute-done((f32[16,128]{1,0:T(8,128)S(1)}, f32[16,128]{1,0:T(8,128)S(1)}, u32[]{:S(2)}, u32[]{:S(2)}) %collective-permute-start.13) | collective-permute-done | bytes 8224 | tf_op jit(solution)/shard_map/ppermute | solution.py:240
  42.7 1.4 %collective-permute-done.12.refs_0_ = f32[16,128]{1,0:T(8,128)S(1)} collective-permute-done((f32[16,128]{1,0:T(8,128)S(1)}, f32[16,128]{1,0:T(8,128)S(1)}, u32[]{:S(2)}, u32[]{:S(2)}) %collective-permute-start.12) | collective-permute-done | bytes 8224 | tf_op jit(solution)/shard_map/ppermute | solution.py:240
  44.1 2.6 %collective-permute-start.17 = (f32[32,128]{1,0:T(8,128)S(1)}, f32[32,128]{1,0:T(8,128)S(1)}, u32[]{:S(2)}, u32[]{:S(2)}) collective-permute-start(f32[32,128]{1,0:T(8,128)S(1)} %dom.1.refs_0_), channel_id=1, source_target_pairs={{0,6},{1,7},{2,4},{3,5},{4,2},{5,3},{6,0},{7,1},{8,14},{9,15},{10,... | collective-permute-start | bytes 49160 | tf_op jit(solution)/shard_map/ppermute | solution.py:240
  46.7 1.3 %collective-permute-start.16 = (f32[32,128]{1,0:T(8,128)S(1)}, f32[32,128]{1,0:T(8,128)S(1)}, u32[]{:S(2)}, u32[]{:S(2)}) collective-permute-start(f32[32,128]{1,0:T(8,128)S(1)} %dom.1.refs_0_), channel_id=1, source_target_pairs={{0,4},{1,5},{2,6},{3,7},{4,0},{5,1},{6,2},{7,3},{8,12},{9,13},{10,... | collective-permute-start | bytes 49160 | tf_op jit(solution)/shard_map/ppermute | solution.py:240
  48.0 0.5 collective-permute-start.15
  48.5 1.3 %collective-permute-done.17.refs_3_ = f32[32,128]{1,0:T(8,128)S(1)} collective-permute-done((f32[32,128]{1,0:T(8,128)S(1)}, f32[32,128]{1,0:T(8,128)S(1)}, u32[]{:S(2)}, u32[]{:S(2)}) %collective-permute-start.17) | collective-permute-done | bytes 16416 | tf_op jit(solution)/shard_map/ppermute | solution.py:240
  49.8 1.6 %collective-permute-done.16.refs_2_ = f32[32,128]{1,0:T(8,128)S(1)} collective-permute-done((f32[32,128]{1,0:T(8,128)S(1)}, f32[32,128]{1,0:T(8,128)S(1)}, u32[]{:S(2)}, u32[]{:S(2)}) %collective-permute-start.16) | collective-permute-done | bytes 16416 | tf_op jit(solution)/shard_map/ppermute | solution.py:240
  52.0 1.7 %collective-permute-start.23 = (f32[16,16,128]{2,1,0:T(8,128)S(1)}, f32[16,16,128]{2,1,0:T(8,128)S(1)}, u32[]{:S(2)}, u32[]{:S(2)}) collective-permute-start(f32[16,16,128]{2,1,0:T(8,128)S(1)} %remove.1.refs_0_), channel_id=1, source_target_pairs={{0,4},{1,5},{2,6},{3,7},{4,0},{5,1},{6,2},{7,3},{8,12},{9,13},{10,... | collective-permute-start | bytes 393224 | tf_op jit(solution)/shard_map/ppermute | solution.py:240
  53.7 2.1 %collective-permute-start.21 = (f32[16,16,128]{2,1,0:T(8,128)S(1)}, f32[16,16,128]{2,1,0:T(8,128)S(1)}, u32[]{:S(2)}, u32[]{:S(2)}) collective-permute-start(f32[16,16,128]{2,1,0:T(8,128)S(1)} %remove.1.refs_0_), channel_id=1, source_target_pairs={{0,6},{1,7},{2,4},{3,5},{4,2},{5,3},{6,0},{7,1},{8,14},{9,15},{10,... | collective-permute-start | bytes 393224 | tf_op jit(solution)/shard_map/ppermute | solution.py:240
  55.8 6.6 %collective-permute-done.23.refs_7_ = f32[16,16,128]{2,1,0:T(8,128)S(1)} collective-permute-done((f32[16,16,128]{2,1,0:T(8,128)S(1)}, f32[16,16,128]{2,1,0:T(8,128)S(1)}, u32[]{:S(2)}, u32[]{:S(2)}) %collective-permute-start.23) | collective-permute-done | bytes 131104 | tf_op jit(solution)/shard_map/ppermute | solution.py:240
  62.4 0.5 collective-permute-start.22
  62.9 0.4 mixing.1
  63.9 0.4 collective-permute-done.20.refs_3_
  64.3 1.8 %update.1 = (f32[16,128,128]{2,1,0:T(8,128)}, f32[16,128,128]{2,1,0:T(8,128)}) custom-call(bf16[128,128]{1,0:T(8,128)(2,1)S(1)} %get-tuple-element.33.wh_ref, bf16[128,128]{1,0:T(8,128)(2,1)S(1)} %get-tuple-element.34.wl_ref, f32[16,128,128]{2,1,0:T(8,128)S(1)} %bitcast.13, f32[16,16,128]{2,1,0:T(8,128)S(1)} %remove.1.refs_0_, ...), custom_call_target="tpu_custom_call" | custom-call | tf_op jit(solution)/shard_map/update/pallas_call | solution.py:372
  (42 shorter events, 2.5 us)
Async XLA Ops:
  2.3 17.8 %collective-permute-start.2 = (f32[2,16,16,128]{3,2,1,0:T(8,128)S(1)}, f32[2,16,16,128]{3,2,1,0:T(8,128)S(1)}, u32[]{:S(2)}, u32[]{:S(2)}) collective-permute-start(f32[2,16,16,128]{3,2,1,0:T(8,128)S(1)} %get-tuple-element.21), channel_id=1, source_target_pairs={{0,4},{1,5},{2,6},{3,7},{4,0},{5,1},{6,2},{7,3},{8,12},{9,13},{10,... | collective-permute-start | bytes 786440 | tf_op jit(solution)/shard_map/ppermute | solution.py:240
  6.4 19.0 %collective-permute-start.6 = (f32[16,16,128]{2,1,0:T(8,128)S(1)}, f32[16,16,128]{2,1,0:T(8,128)S(1)}, u32[]{:S(2)}, u32[]{:S(2)}) collective-permute-start(f32[16,16,128]{2,1,0:T(8,128)S(1)} %slice_bitcast_fusion.1), channel_id=1, source_target_pairs={{0,1},{1,0},{2,3},{3,2},{4,5},{5,4},{6,7},{7,6},{8,9},{9,8},{10,11... | collective-permute-start | bytes 393224 | tf_op jit(solution)/shard_map/ppermute | solution.py:240
  6.5 18.8 %collective-permute-start.4 = (f32[2,16,16,128]{3,2,1,0:T(8,128)S(1)}, f32[2,16,16,128]{3,2,1,0:T(8,128)S(1)}, u32[]{:S(2)}, u32[]{:S(2)}) collective-permute-start(f32[2,16,16,128]{3,2,1,0:T(8,128)S(1)} %get-tuple-element.22), channel_id=1, source_target_pairs={{0,2},{1,3},{2,0},{3,1},{4,6},{5,7},{6,4},{7,5},{8,10},{9,11},{10,... | collective-permute-start | bytes 786440 | tf_op jit(solution)/shard_map/ppermute | solution.py:240
  8.1 17.3 %collective-permute-start.1 = (f32[16,16,128]{2,1,0:T(8,128)S(1)}, f32[16,16,128]{2,1,0:T(8,128)S(1)}, u32[]{:S(2)}, u32[]{:S(2)}) collective-permute-start(f32[16,16,128]{2,1,0:T(8,128)S(1)} %get-tuple-element.38), channel_id=1, source_target_pairs={{0,6},{1,7},{2,4},{3,5},{4,2},{5,3},{6,0},{7,1},{8,14},{9,15},{10,... | collective-permute-start | bytes 393224 | tf_op jit(solution)/shard_map/ppermute | solution.py:240
  8.2 17.2 %collective-permute-start = (f32[16,16,128]{2,1,0:T(8,128)S(1)}, f32[16,16,128]{2,1,0:T(8,128)S(1)}, u32[]{:S(2)}, u32[]{:S(2)}) collective-permute-start(f32[16,16,128]{2,1,0:T(8,128)S(1)} %get-tuple-element.39), channel_id=1, source_target_pairs={{0,7},{1,6},{2,5},{3,4},{4,3},{5,2},{6,1},{7,0},{8,15},{9,14},{10,... | collective-permute-start | bytes 393224 | tf_op jit(solution)/shard_map/ppermute | solution.py:240
  20.1 5.4 %collective-permute-start.3 = (f32[16,16,128]{2,1,0:T(8,128)S(1)}, f32[16,16,128]{2,1,0:T(8,128)S(1)}, u32[]{:S(2)}, u32[]{:S(2)}) collective-permute-start(f32[16,16,128]{2,1,0:T(8,128)S(1)} %slice_bitcast_fusion), channel_id=1, source_target_pairs={{0,1},{1,0},{2,3},{3,2},{4,5},{5,4},{6,7},{7,6},{8,9},{9,8},{10,11... | collective-permute-start | bytes 393224 | tf_op jit(solution)/shard_map/ppermute | solution.py:240
  25.3 8.3 %copy-start.1 = (bf16[384,128]{1,0:T(8,128)(2,1)S(1)}, bf16[384,128]{1,0:T(8,128)(2,1)}, u32[]{:S(2)}) copy-start(bf16[384,128]{1,0:T(8,128)(2,1)} %constant.5.clone.wl_ref) | copy-start | bytes 294916
  25.3 8.3 %copy-start.2 = (bf16[384,128]{1,0:T(8,128)(2,1)S(1)}, bf16[384,128]{1,0:T(8,128)(2,1)}, u32[]{:S(2)}) copy-start(bf16[384,128]{1,0:T(8,128)(2,1)} %constant.4.clone.wh_ref) | copy-start | bytes 294916
  25.3 8.3 %copy-start.3 = (f32[8,16,128]{2,1,0:T(8,128)S(1)}, f32[8,16,128]{2,1,0:T(8,128)}, u32[]{:S(2)}) copy-start(f32[8,16,128]{2,1,0:T(8,128)} %param.8) | copy-start | bytes 196612
  25.3 1.4 %collective-permute-start.5 = (f32[16,16,128]{2,1,0:T(8,128)S(1)}, f32[16,16,128]{2,1,0:T(8,128)S(1)}, u32[]{:S(2)}, u32[]{:S(2)}) collective-permute-start(f32[16,16,128]{2,1,0:T(8,128)S(1)} %hand.1), channel_id=1, source_target_pairs={{0,1},{1,0},{2,3},{3,2},{4,5},{5,4},{6,7},{7,6},{8,9},{9,8},{10,11... | collective-permute-start | bytes 393224 | tf_op jit(solution)/shard_map/ppermute | solution.py:240
  26.9 8.3 %collective-permute-start.9 = (f32[192,128]{1,0:T(8,128)S(1)}, f32[192,128]{1,0:T(8,128)S(1)}, u32[]{:S(2)}, u32[]{:S(2)}) collective-permute-start(f32[192,128]{1,0:T(8,128)S(1)} %get-tuple-element.30), channel_id=1, source_target_pairs={{0,8},{8,16},{16,24},{24,0},{1,9},{9,17},{17,25},{25,1},{2,10},{10... | collective-permute-start | bytes 294920 | tf_op jit(solution)/shard_map/ppermute | solution.py:307
  28.7 6.6 %collective-permute-start.10 = (f32[192,128]{1,0:T(8,128)S(1)}, f32[192,128]{1,0:T(8,128)S(1)}, u32[]{:S(2)}, u32[]{:S(2)}) collective-permute-start(f32[192,128]{1,0:T(8,128)S(1)} %get-tuple-element.31), channel_id=1, source_target_pairs={{0,24},{8,0},{16,8},{24,16},{1,25},{9,1},{17,9},{25,17},{2,26},{10... | collective-permute-start | bytes 294920 | tf_op jit(solution)/shard_map/ppermute | solution.py:308
  29.9 5.3 %collective-permute-start.7 = (f32[6,16,128]{2,1,0:T(8,128)S(1)}, f32[6,16,128]{2,1,0:T(8,128)S(1)}, u32[]{:S(2)}, u32[]{:S(2)}) collective-permute-start(f32[6,16,128]{2,1,0:T(8,128)S(1)} %get-tuple-element.28), channel_id=1, source_target_pairs={{0,7},{1,2},{2,1},{3,4},{4,3},{5,6},{6,5},{7,0},{8,15},{9,10},{10,... | collective-permute-start | bytes 147464 | tf_op jit(solution)/shard_map/ppermute | solution.py:310
  31.6 3.7 %collective-permute-start.8 = (f32[6,16,128]{2,1,0:T(8,128)S(1)}, f32[6,16,128]{2,1,0:T(8,128)S(1)}, u32[]{:S(2)}, u32[]{:S(2)}) collective-permute-start(f32[6,16,128]{2,1,0:T(8,128)S(1)} %get-tuple-element.29), channel_id=1, source_target_pairs={{0,1},{1,0},{2,3},{3,2},{4,5},{5,4},{6,7},{7,6},{8,9},{9,8},{10,11... | collective-permute-start | bytes 147464 | tf_op jit(solution)/shard_map/ppermute | solution.py:240
  33.6 1.6 %copy-start.4 = (f32[16,128]{1,0:T(8,128)S(1)}, f32[16,128]{1,0:T(8,128)}, u32[]{:S(2)}) copy-start(f32[16,128]{1,0:T(8,128)} %rot_ref.1) | copy-start | bytes 24580
  36.1 28.2 %copy-start = (f32[16,8,16,128]{3,2,1,0:T(8,128)S(1)}, f32[16,8,16,128]{3,2,1,0:T(8,128)}, u32[]{:S(2)}) copy-start(f32[16,8,16,128]{3,2,1,0:T(8,128)} %param.7) | copy-start | bytes 3145732
  36.1 1.2 %collective-permute-start.11 = (f32[32,128]{1,0:T(8,128)S(1)}, f32[32,128]{1,0:T(8,128)S(1)}, u32[]{:S(2)}, u32[]{:S(2)}) collective-permute-start(f32[32,128]{1,0:T(8,128)S(1)} %get-tuple-element.32), channel_id=1, source_target_pairs={{0,1},{1,0},{2,3},{3,2},{4,5},{5,4},{6,7},{7,6},{8,9},{9,8},{10,11... | collective-permute-start | bytes 49160 | tf_op jit(solution)/shard_map/ppermute | solution.py:240
  37.3 4.5 %collective-permute-start.14 = (f32[16,128]{1,0:T(8,128)S(1)}, f32[16,128]{1,0:T(8,128)S(1)}, u32[]{:S(2)}, u32[]{:S(2)}) collective-permute-start(f32[16,128]{1,0:T(8,128)S(1)} %slice.23), channel_id=1, source_target_pairs={{0,24},{8,16},{16,8},{24,0},{1,25},{9,17},{17,9},{25,1},{2,26},{10... | collective-permute-start | bytes 24584 | tf_op jit(solution)/shard_map/ppermute | solution.py:240
  39.0 3.7 %collective-permute-start.13 = (f32[16,128]{1,0:T(8,128)S(1)}, f32[16,128]{1,0:T(8,128)S(1)}, u32[]{:S(2)}, u32[]{:S(2)}) collective-permute-start(f32[16,128]{1,0:T(8,128)S(1)} %slice.23), channel_id=1, source_target_pairs={{0,8},{8,0},{16,24},{24,16},{1,9},{9,1},{17,25},{25,17},{2,10},{10... | collective-permute-start | bytes 24584 | tf_op jit(solution)/shard_map/ppermute | solution.py:240
  40.5 3.7 %collective-permute-start.12 = (f32[16,128]{1,0:T(8,128)S(1)}, f32[16,128]{1,0:T(8,128)S(1)}, u32[]{:S(2)}, u32[]{:S(2)}) collective-permute-start(f32[16,128]{1,0:T(8,128)S(1)} %slice.23), channel_id=1, source_target_pairs={{0,16},{8,24},{16,0},{24,8},{1,17},{9,25},{17,1},{25,9},{2,18},{10... | collective-permute-start | bytes 24584 | tf_op jit(solution)/shard_map/ppermute | solution.py:240
  44.1 5.6 %collective-permute-start.17 = (f32[32,128]{1,0:T(8,128)S(1)}, f32[32,128]{1,0:T(8,128)S(1)}, u32[]{:S(2)}, u32[]{:S(2)}) collective-permute-start(f32[32,128]{1,0:T(8,128)S(1)} %dom.1.refs_0_), channel_id=1, source_target_pairs={{0,6},{1,7},{2,4},{3,5},{4,2},{5,3},{6,0},{7,1},{8,14},{9,15},{10,... | collective-permute-start | bytes 49160 | tf_op jit(solution)/shard_map/ppermute | solution.py:240
  46.7 4.6 %collective-permute-start.16 = (f32[32,128]{1,0:T(8,128)S(1)}, f32[32,128]{1,0:T(8,128)S(1)}, u32[]{:S(2)}, u32[]{:S(2)}) collective-permute-start(f32[32,128]{1,0:T(8,128)S(1)} %dom.1.refs_0_), channel_id=1, source_target_pairs={{0,4},{1,5},{2,6},{3,7},{4,0},{5,1},{6,2},{7,3},{8,12},{9,13},{10,... | collective-permute-start | bytes 49160 | tf_op jit(solution)/shard_map/ppermute | solution.py:240
  48.0 3.7 %collective-permute-start.15 = (f32[32,128]{1,0:T(8,128)S(1)}, f32[32,128]{1,0:T(8,128)S(1)}, u32[]{:S(2)}, u32[]{:S(2)}) collective-permute-start(f32[32,128]{1,0:T(8,128)S(1)} %dom.1.refs_0_), channel_id=1, source_target_pairs={{0,2},{1,3},{2,0},{3,1},{4,6},{5,7},{6,4},{7,5},{8,10},{9,11},{10,... | collective-permute-start | bytes 49160 | tf_op jit(solution)/shard_map/ppermute | solution.py:240
  52.0 10.4 %collective-permute-start.23 = (f32[16,16,128]{2,1,0:T(8,128)S(1)}, f32[16,16,128]{2,1,0:T(8,128)S(1)}, u32[]{:S(2)}, u32[]{:S(2)}) collective-permute-start(f32[16,16,128]{2,1,0:T(8,128)S(1)} %remove.1.refs_0_), channel_id=1, source_target_pairs={{0,4},{1,5},{2,6},{3,7},{4,0},{5,1},{6,2},{7,3},{8,12},{9,13},{10,... | collective-permute-start | bytes 393224 | tf_op jit(solution)/shard_map/ppermute | solution.py:240
  53.7 8.7 %collective-permute-start.21 = (f32[16,16,128]{2,1,0:T(8,128)S(1)}, f32[16,16,128]{2,1,0:T(8,128)S(1)}, u32[]{:S(2)}, u32[]{:S(2)}) collective-permute-start(f32[16,16,128]{2,1,0:T(8,128)S(1)} %remove.1.refs_0_), channel_id=1, source_target_pairs={{0,6},{1,7},{2,4},{3,5},{4,2},{5,3},{6,0},{7,1},{8,14},{9,15},{10,... | collective-permute-start | bytes 393224 | tf_op jit(solution)/shard_map/ppermute | solution.py:240
  55.8 7.1 %collective-permute-start.19 = (f32[16,16,128]{2,1,0:T(8,128)S(1)}, f32[16,16,128]{2,1,0:T(8,128)S(1)}, u32[]{:S(2)}, u32[]{:S(2)}) collective-permute-start(f32[16,16,128]{2,1,0:T(8,128)S(1)} %remove.1.refs_0_), channel_id=1, source_target_pairs={{0,2},{1,3},{2,0},{3,1},{4,6},{5,7},{6,4},{7,5},{8,10},{9,11},{10,... | collective-permute-start | bytes 393224 | tf_op jit(solution)/shard_map/ppermute | solution.py:240
  55.8 7.5 %collective-permute-start.18 = (f32[16,16,128]{2,1,0:T(8,128)S(1)}, f32[16,16,128]{2,1,0:T(8,128)S(1)}, u32[]{:S(2)}, u32[]{:S(2)}) collective-permute-start(f32[16,16,128]{2,1,0:T(8,128)S(1)} %remove.1.refs_0_), channel_id=1, source_target_pairs={{0,1},{1,0},{2,3},{3,2},{4,5},{5,4},{6,7},{7,6},{8,9},{9,8},{10,11... | collective-permute-start | bytes 393224 | tf_op jit(solution)/shard_map/ppermute | solution.py:240
  62.3 1.3 %collective-permute-start.24 = (f32[16,16,128]{2,1,0:T(8,128)S(1)}, f32[16,16,128]{2,1,0:T(8,128)S(1)}, u32[]{:S(2)}, u32[]{:S(2)}) collective-permute-start(f32[16,16,128]{2,1,0:T(8,128)S(1)} %collective-permute-done.23.refs_7_), channel_id=1, source_target_pairs={{0,1},{1,0},{2,3},{3,2},{4,5},{5,4},{6,7},{7,6},{8,9},{9,8},{10,11... | collective-permute-start | bytes 393224 | tf_op jit(solution)/shard_map/ppermute | solution.py:240
  62.4 1.5 %collective-permute-start.22 = (f32[16,16,128]{2,1,0:T(8,128)S(1)}, f32[16,16,128]{2,1,0:T(8,128)S(1)}, u32[]{:S(2)}, u32[]{:S(2)}) collective-permute-start(f32[16,16,128]{2,1,0:T(8,128)S(1)} %collective-permute-done.21.refs_5_), channel_id=1, source_target_pairs={{0,1},{1,0},{2,3},{3,2},{4,5},{5,4},{6,7},{7,6},{8,9},{9,8},{10,11... | collective-permute-start | bytes 393224 | tf_op jit(solution)/shard_map/ppermute | solution.py:240
  62.9 1.3 %collective-permute-start.20 = (f32[16,16,128]{2,1,0:T(8,128)S(1)}, f32[16,16,128]{2,1,0:T(8,128)S(1)}, u32[]{:S(2)}, u32[]{:S(2)}) collective-permute-start(f32[16,16,128]{2,1,0:T(8,128)S(1)} %collective-permute-done.19.refs_2_), channel_id=1, source_target_pairs={{0,1},{1,0},{2,3},{3,2},{4,5},{5,4},{6,7},{7,6},{8,9},{9,8},{10,11... | collective-permute-start | bytes 393224 | tf_op jit(solution)/shard_map/ppermute | solution.py:240

commit v4 on v3

--- a/solution.py
+++ b/solution.py
@@ -340,7 +340,7 @@
         out_specs=VMEM,
         compiler_params=params(),
         name="dom",
-    )(part, *[swap(part[:nb], "dom", k) for k in sorted(range(1, doms), key=lambda k: (k.bit_count() > 1, -k))])
+    )(part, *[swap(part[:nb], "dom", k) for k in sorted(range(1, doms), key=lambda k: (k == 1, k))])
     sums = [part] + [swap(part, "orb", k) for k in range(2, blocks, 2)]
 
     own = pl.pallas_call(

time: 66.2 us -> 66.7 us (level)
  transfers between devices with their start and end apart: 25 -> 25, of which waited for: 16 -> 15; matrix products, arithmetic and copies ran while one was open for 0% -> 0% of each run, Pallas kernels for 1% -> 1%
where the time goes in v4:
time: 66.7 us; the launch traced here: 66.5 us
  waiting for transfers between devices  29.8 us (45%)
  starting transfers between devices  29 us (43%)
  Pallas kernels  5.5 us (8%)
  between operations  2.11 us (3%)
    ppermute x22, waiting for transfers between devices, swap(): return lax.ppermute(value, axis, [(i, i ^ k) for i in range(count)])  28.6 us
    ppermute x22, starting transfers between devices, swap(): return lax.ppermute(value, axis, [(i, i ^ k) for i in range(count)])  24.4 us
    pallas_call x1, Pallas kernels, per_device(): pl.pallas_call(functools.partial(update_kernel, blocks, sequence), out_sh...  1.77 us
    ppermute x1, starting transfers between devices, per_device(): x_before = lax.ppermute(last, 'dom', up(doms))  1.7 us
    pallas_call x1, Pallas kernels, per_device(): pl.pallas_call(functools.partial(pack_kernel, blocks), out_shape=[shape(2...  1.65 us
    ppermute x1, starting transfers between devices, per_device(): lax.ppermute(far, 'orb', [(o, (o + 2 * (o % 2) - 1) % blocks) for o in ra...  1.64 us
  transfers between devices with their start and end apart: 25, of which 15 were waited for; matrix products, arithmetic and copies ran while one was open for 0% of the time, Pallas kernels for 1%

profile of v4, /device:TPU:0, one launch (start us, length us, event | category | flops | bytes accessed | tf_op | source)
XLA Modules:
  0.0 66.5 jit_solution(12633096486404907487)
XLA Ops:
  0.6 1.7 %pack.1 = (f32[2,16,16,128]{3,2,1,0:T(8,128)S(1)}, f32[2,16,16,128]{3,2,1,0:T(8,128)S(1)}, f32[2,16,16,128]{3,2,1,0:T(8,128)S(1)}, f32[2,16,16,128]{3,2,1,0:T(8,128)S(1)}) custom-call(f32[16,128,128]{2,1,0:T(8,128)} %bitcast.12), custom_call_target="tpu_custom_call" | custom-call | tf_op jit(solution)/shard_map/pack/pallas_call | solution.py:268
  2.3 4.1 %collective-permute-start.2 = (f32[2,16,16,128]{3,2,1,0:T(8,128)S(1)}, f32[2,16,16,128]{3,2,1,0:T(8,128)S(1)}, u32[]{:S(2)}, u32[]{:S(2)}) collective-permute-start(f32[2,16,16,128]{3,2,1,0:T(8,128)S(1)} %get-tuple-element.21), channel_id=1, source_target_pairs={{0,4},{1,5},{2,6},{3,7},{4,0},{5,1},{6,2},{7,3},{8,12},{9,13},{10,... | collective-permute-start | bytes 786440 | tf_op jit(solution)/shard_map/ppermute | solution.py:240
  6.5 1.6 %collective-permute-start.4 = (f32[2,16,16,128]{3,2,1,0:T(8,128)S(1)}, f32[2,16,16,128]{3,2,1,0:T(8,128)S(1)}, u32[]{:S(2)}, u32[]{:S(2)}) collective-permute-start(f32[2,16,16,128]{3,2,1,0:T(8,128)S(1)} %get-tuple-element.22), channel_id=1, source_target_pairs={{0,2},{1,3},{2,0},{3,1},{4,6},{5,7},{6,4},{7,5},{8,10},{9,11},{10,... | collective-permute-start | bytes 786440 | tf_op jit(solution)/shard_map/ppermute | solution.py:240
  8.2 3.3 %collective-permute-start = (f32[16,16,128]{2,1,0:T(8,128)S(1)}, f32[16,16,128]{2,1,0:T(8,128)S(1)}, u32[]{:S(2)}, u32[]{:S(2)}) collective-permute-start(f32[16,16,128]{2,1,0:T(8,128)S(1)} %get-tuple-element.39), channel_id=1, source_target_pairs={{0,7},{1,6},{2,5},{3,4},{4,3},{5,2},{6,1},{7,0},{8,15},{9,14},{10,... | collective-permute-start | bytes 393224 | tf_op jit(solution)/shard_map/ppermute | solution.py:240
  12.8 7.2 %collective-permute-done.2.refs_5_ = f32[2,16,16,128]{3,2,1,0:T(8,128)S(1)} collective-permute-done((f32[2,16,16,128]{3,2,1,0:T(8,128)S(1)}, f32[2,16,16,128]{3,2,1,0:T(8,128)S(1)}, u32[]{:S(2)}, u32[]{:S(2)}) %collective-permute-start.2) | collective-permute-done | bytes 262176 | tf_op jit(solution)/shard_map/ppermute | solution.py:240
  20.1 5.1 %collective-permute-done.4.pair_ref.refs_6_ = f32[2,16,16,128]{3,2,1,0:T(8,128)S(1)} collective-permute-done((f32[2,16,16,128]{3,2,1,0:T(8,128)S(1)}, f32[2,16,16,128]{3,2,1,0:T(8,128)S(1)}, u32[]{:S(2)}, u32[]{:S(2)}) %collective-permute-start.4) | collective-permute-done | bytes 262176 | tf_op jit(solution)/shard_map/ppermute | solution.py:240
  25.4 1.3 %collective-permute-done.5.refs_3_ = f32[16,16,128]{2,1,0:T(8,128)S(1)} collective-permute-done((f32[16,16,128]{2,1,0:T(8,128)S(1)}, f32[16,16,128]{2,1,0:T(8,128)S(1)}, u32[]{:S(2)}, u32[]{:S(2)}) %collective-permute-start.5) | collective-permute-done | bytes 131104 | tf_op jit(solution)/shard_map/ppermute | solution.py:240
  27.0 1.7 %collective-permute-start.9 = (f32[192,128]{1,0:T(8,128)S(1)}, f32[192,128]{1,0:T(8,128)S(1)}, u32[]{:S(2)}, u32[]{:S(2)}) collective-permute-start(f32[192,128]{1,0:T(8,128)S(1)} %get-tuple-element.30), channel_id=1, source_target_pairs={{0,8},{8,16},{16,24},{24,0},{1,9},{9,17},{17,25},{25,1},{2,10},{10... | collective-permute-start | bytes 294920 | tf_op jit(solution)/shard_map/ppermute | solution.py:307
  28.7 1.3 %collective-permute-start.10 = (f32[192,128]{1,0:T(8,128)S(1)}, f32[192,128]{1,0:T(8,128)S(1)}, u32[]{:S(2)}, u32[]{:S(2)}) collective-permute-start(f32[192,128]{1,0:T(8,128)S(1)} %get-tuple-element.31), channel_id=1, source_target_pairs={{0,24},{8,0},{16,8},{24,16},{1,25},{9,1},{17,9},{25,17},{2,26},{10... | collective-permute-start | bytes 294920 | tf_op jit(solution)/shard_map/ppermute | solution.py:308
  29.9 1.6 %collective-permute-start.7 = (f32[6,16,128]{2,1,0:T(8,128)S(1)}, f32[6,16,128]{2,1,0:T(8,128)S(1)}, u32[]{:S(2)}, u32[]{:S(2)}) collective-permute-start(f32[6,16,128]{2,1,0:T(8,128)S(1)} %get-tuple-element.28), channel_id=1, source_target_pairs={{0,7},{1,2},{2,1},{3,4},{4,3},{5,6},{6,5},{7,0},{8,15},{9,10},{10,... | collective-permute-start | bytes 147464 | tf_op jit(solution)/shard_map/ppermute | solution.py:310
  31.6 2.0 %collective-permute-start.8 = (f32[6,16,128]{2,1,0:T(8,128)S(1)}, f32[6,16,128]{2,1,0:T(8,128)S(1)}, u32[]{:S(2)}, u32[]{:S(2)}) collective-permute-start(f32[6,16,128]{2,1,0:T(8,128)S(1)} %get-tuple-element.29), channel_id=1, source_target_pairs={{0,1},{1,0},{2,3},{3,2},{4,5},{5,4},{6,7},{7,6},{8,9},{9,8},{10,11... | collective-permute-start | bytes 147464 | tf_op jit(solution)/shard_map/ppermute | solution.py:240
  33.6 0.4 split.1
  34.1 1.2 %collective-permute-done.7.far_ref = f32[6,16,128]{2,1,0:T(8,128)S(1)} collective-permute-done((f32[6,16,128]{2,1,0:T(8,128)S(1)}, f32[6,16,128]{2,1,0:T(8,128)S(1)}, u32[]{:S(2)}, u32[]{:S(2)}) %collective-permute-start.7) | collective-permute-done | bytes 49184 | tf_op jit(solution)/shard_map/ppermute | solution.py:310
  35.3 0.8 %project.1 = (f32[16,16,128]{2,1,0:T(8,128)S(1)}, f32[32,128]{1,0:T(8,128)S(1)}) custom-call(s32[1]{0:T(128)S(6)} %copy.10.owner_ref, f32[16,128]{1,0:T(8,128)S(1)} %copy-done.4, bf16[128,2048]{1,0:T(8,128)(2,1)S(1)} %get-tuple-element.25.xh_ref, bf16[128,2048]{1,0:T(8,128)(2,1)S(1)} %get-tuple-element.26.xl_ref, ...), custom_call_target="tpu_custom_call" | custom-call | tf_op jit(solution)/shard_map/project/pallas_call | solution.py:325
  36.5 0.9 %collective-permute-done.11 = f32[32,128]{1,0:T(8,128)S(1)} collective-permute-done((f32[32,128]{1,0:T(8,128)S(1)}, f32[32,128]{1,0:T(8,128)S(1)}, u32[]{:S(2)}, u32[]{:S(2)}) %collective-permute-start.11) | collective-permute-done | bytes 16416 | tf_op jit(solution)/shard_map/ppermute | solution.py:240
  37.3 1.5 %collective-permute-start.14 = (f32[16,128]{1,0:T(8,128)S(1)}, f32[16,128]{1,0:T(8,128)S(1)}, u32[]{:S(2)}, u32[]{:S(2)}) collective-permute-start(f32[16,128]{1,0:T(8,128)S(1)} %slice.23), channel_id=1, source_target_pairs={{0,8},{8,0},{16,24},{24,16},{1,9},{9,1},{17,25},{25,17},{2,10},{10... | collective-permute-start | bytes 24584 | tf_op jit(solution)/shard_map/ppermute | solution.py:240
  38.8 1.7 %collective-permute-start.13 = (f32[16,128]{1,0:T(8,128)S(1)}, f32[16,128]{1,0:T(8,128)S(1)}, u32[]{:S(2)}, u32[]{:S(2)}) collective-permute-start(f32[16,128]{1,0:T(8,128)S(1)} %slice.23), channel_id=1, source_target_pairs={{0,24},{8,16},{16,8},{24,0},{1,25},{9,17},{17,9},{25,1},{2,26},{10... | collective-permute-start | bytes 24584 | tf_op jit(solution)/shard_map/ppermute | solution.py:240
  41.0 2.4 %collective-permute-done.13.refs_1_ = f32[16,128]{1,0:T(8,128)S(1)} collective-permute-done((f32[16,128]{1,0:T(8,128)S(1)}, f32[16,128]{1,0:T(8,128)S(1)}, u32[]{:S(2)}, u32[]{:S(2)}) %collective-permute-start.13) | collective-permute-done | bytes 8224 | tf_op jit(solution)/shard_map/ppermute | solution.py:240
  43.4 0.8 %collective-permute-done.12.refs_0_ = f32[16,128]{1,0:T(8,128)S(1)} collective-permute-done((f32[16,128]{1,0:T(8,128)S(1)}, f32[16,128]{1,0:T(8,128)S(1)}, u32[]{:S(2)}, u32[]{:S(2)}) %collective-permute-start.12) | collective-permute-done | bytes 8224 | tf_op jit(solution)/shard_map/ppermute | solution.py:240
  44.1 2.5 %collective-permute-start.17 = (f32[32,128]{1,0:T(8,128)S(1)}, f32[32,128]{1,0:T(8,128)S(1)}, u32[]{:S(2)}, u32[]{:S(2)}) collective-permute-start(f32[32,128]{1,0:T(8,128)S(1)} %dom.1.refs_0_), channel_id=1, source_target_pairs={{0,6},{1,7},{2,4},{3,5},{4,2},{5,3},{6,0},{7,1},{8,14},{9,15},{10,... | collective-permute-start | bytes 49160 | tf_op jit(solution)/shard_map/ppermute | solution.py:240
  46.7 1.8 %collective-permute-start.16 = (f32[32,128]{1,0:T(8,128)S(1)}, f32[32,128]{1,0:T(8,128)S(1)}, u32[]{:S(2)}, u32[]{:S(2)}) collective-permute-start(f32[32,128]{1,0:T(8,128)S(1)} %dom.1.refs_0_), channel_id=1, source_target_pairs={{0,4},{1,5},{2,6},{3,7},{4,0},{5,1},{6,2},{7,3},{8,12},{9,13},{10,... | collective-permute-start | bytes 49160 | tf_op jit(solution)/shard_map/ppermute | solution.py:240
  48.5 0.5 collective-permute-start.15
  49.0 0.7 %collective-permute-done.17.refs_3_ = f32[32,128]{1,0:T(8,128)S(1)} collective-permute-done((f32[32,128]{1,0:T(8,128)S(1)}, f32[32,128]{1,0:T(8,128)S(1)}, u32[]{:S(2)}, u32[]{:S(2)}) %collective-permute-start.17) | collective-permute-done | bytes 16416 | tf_op jit(solution)/shard_map/ppermute | solution.py:240
  49.7 1.6 %collective-permute-done.16.refs_2_ = f32[32,128]{1,0:T(8,128)S(1)} collective-permute-done((f32[32,128]{1,0:T(8,128)S(1)}, f32[32,128]{1,0:T(8,128)S(1)}, u32[]{:S(2)}, u32[]{:S(2)}) %collective-permute-start.16) | collective-permute-done | bytes 16416 | tf_op jit(solution)/shard_map/ppermute | solution.py:240
  51.3 0.9 %collective-permute-done.15.refs_1_ = f32[32,128]{1,0:T(8,128)S(1)} collective-permute-done((f32[32,128]{1,0:T(8,128)S(1)}, f32[32,128]{1,0:T(8,128)S(1)}, u32[]{:S(2)}, u32[]{:S(2)}) %collective-permute-start.15) | collective-permute-done | bytes 16416 | tf_op jit(solution)/shard_map/ppermute | solution.py:240
  52.5 1.6 %collective-permute-start.23 = (f32[16,16,128]{2,1,0:T(8,128)S(1)}, f32[16,16,128]{2,1,0:T(8,128)S(1)}, u32[]{:S(2)}, u32[]{:S(2)}) collective-permute-start(f32[16,16,128]{2,1,0:T(8,128)S(1)} %remove.1.refs_0_), channel_id=1, source_target_pairs={{0,4},{1,5},{2,6},{3,7},{4,0},{5,1},{6,2},{7,3},{8,12},{9,13},{10,... | collective-permute-start | bytes 393224 | tf_op jit(solution)/shard_map/ppermute | solution.py:240
  54.1 2.2 %collective-permute-start.21 = (f32[16,16,128]{2,1,0:T(8,128)S(1)}, f32[16,16,128]{2,1,0:T(8,128)S(1)}, u32[]{:S(2)}, u32[]{:S(2)}) collective-permute-start(f32[16,16,128]{2,1,0:T(8,128)S(1)} %remove.1.refs_0_), channel_id=1, source_target_pairs={{0,6},{1,7},{2,4},{3,5},{4,2},{5,3},{6,0},{7,1},{8,14},{9,15},{10,... | collective-permute-start | bytes 393224 | tf_op jit(solution)/shard_map/ppermute | solution.py:240
  56.3 6.5 %collective-permute-done.23.refs_7_ = f32[16,16,128]{2,1,0:T(8,128)S(1)} collective-permute-done((f32[16,16,128]{2,1,0:T(8,128)S(1)}, f32[16,16,128]{2,1,0:T(8,128)S(1)}, u32[]{:S(2)}, u32[]{:S(2)}) %collective-permute-start.23) | collective-permute-done | bytes 131104 | tf_op jit(solution)/shard_map/ppermute | solution.py:240
  62.8 0.5 collective-permute-start.22
  63.4 0.4 mixing.1
  64.4 0.4 collective-permute-done.20.refs_3_
  64.7 1.8 %update.1 = (f32[16,128,128]{2,1,0:T(8,128)}, f32[16,128,128]{2,1,0:T(8,128)}) custom-call(bf16[128,128]{1,0:T(8,128)(2,1)S(1)} %get-tuple-element.33.wh_ref, bf16[128,128]{1,0:T(8,128)(2,1)S(1)} %get-tuple-element.34.wl_ref, f32[16,128,128]{2,1,0:T(8,128)S(1)} %bitcast.13, f32[16,16,128]{2,1,0:T(8,128)S(1)} %remove.1.refs_0_, ...), custom_call_target="tpu_custom_call" | custom-call | tf_op jit(solution)/shard_map/update/pallas_call | solution.py:372
  (42 shorter events, 2.3 us)
Async XLA Ops:
  2.3 17.8 %collective-permute-start.2 = (f32[2,16,16,128]{3,2,1,0:T(8,128)S(1)}, f32[2,16,16,128]{3,2,1,0:T(8,128)S(1)}, u32[]{:S(2)}, u32[]{:S(2)}) collective-permute-start(f32[2,16,16,128]{3,2,1,0:T(8,128)S(1)} %get-tuple-element.21), channel_id=1, source_target_pairs={{0,4},{1,5},{2,6},{3,7},{4,0},{5,1},{6,2},{7,3},{8,12},{9,13},{10,... | collective-permute-start | bytes 786440 | tf_op jit(solution)/shard_map/ppermute | solution.py:240
  6.4 19.0 %collective-permute-start.6 = (f32[16,16,128]{2,1,0:T(8,128)S(1)}, f32[16,16,128]{2,1,0:T(8,128)S(1)}, u32[]{:S(2)}, u32[]{:S(2)}) collective-permute-start(f32[16,16,128]{2,1,0:T(8,128)S(1)} %slice_bitcast_fusion.1), channel_id=1, source_target_pairs={{0,1},{1,0},{2,3},{3,2},{4,5},{5,4},{6,7},{7,6},{8,9},{9,8},{10,11... | collective-permute-start | bytes 393224 | tf_op jit(solution)/shard_map/ppermute | solution.py:240
  6.5 18.8 %collective-permute-start.4 = (f32[2,16,16,128]{3,2,1,0:T(8,128)S(1)}, f32[2,16,16,128]{3,2,1,0:T(8,128)S(1)}, u32[]{:S(2)}, u32[]{:S(2)}) collective-permute-start(f32[2,16,16,128]{3,2,1,0:T(8,128)S(1)} %get-tuple-element.22), channel_id=1, source_target_pairs={{0,2},{1,3},{2,0},{3,1},{4,6},{5,7},{6,4},{7,5},{8,10},{9,11},{10,... | collective-permute-start | bytes 786440 | tf_op jit(solution)/shard_map/ppermute | solution.py:240
  8.1 17.3 %collective-permute-start.1 = (f32[16,16,128]{2,1,0:T(8,128)S(1)}, f32[16,16,128]{2,1,0:T(8,128)S(1)}, u32[]{:S(2)}, u32[]{:S(2)}) collective-permute-start(f32[16,16,128]{2,1,0:T(8,128)S(1)} %get-tuple-element.38), channel_id=1, source_target_pairs={{0,6},{1,7},{2,4},{3,5},{4,2},{5,3},{6,0},{7,1},{8,14},{9,15},{10,... | collective-permute-start | bytes 393224 | tf_op jit(solution)/shard_map/ppermute | solution.py:240
  8.2 17.2 %collective-permute-start = (f32[16,16,128]{2,1,0:T(8,128)S(1)}, f32[16,16,128]{2,1,0:T(8,128)S(1)}, u32[]{:S(2)}, u32[]{:S(2)}) collective-permute-start(f32[16,16,128]{2,1,0:T(8,128)S(1)} %get-tuple-element.39), channel_id=1, source_target_pairs={{0,7},{1,6},{2,5},{3,4},{4,3},{5,2},{6,1},{7,0},{8,15},{9,14},{10,... | collective-permute-start | bytes 393224 | tf_op jit(solution)/shard_map/ppermute | solution.py:240
  20.1 5.4 %collective-permute-start.3 = (f32[16,16,128]{2,1,0:T(8,128)S(1)}, f32[16,16,128]{2,1,0:T(8,128)S(1)}, u32[]{:S(2)}, u32[]{:S(2)}) collective-permute-start(f32[16,16,128]{2,1,0:T(8,128)S(1)} %slice_bitcast_fusion), channel_id=1, source_target_pairs={{0,1},{1,0},{2,3},{3,2},{4,5},{5,4},{6,7},{7,6},{8,9},{9,8},{10,11... | collective-permute-start | bytes 393224 | tf_op jit(solution)/shard_map/ppermute | solution.py:240
  25.3 8.3 %copy-start.1 = (bf16[384,128]{1,0:T(8,128)(2,1)S(1)}, bf16[384,128]{1,0:T(8,128)(2,1)}, u32[]{:S(2)}) copy-start(bf16[384,128]{1,0:T(8,128)(2,1)} %constant.5.clone.wl_ref) | copy-start | bytes 294916
  25.3 8.3 %copy-start.2 = (bf16[384,128]{1,0:T(8,128)(2,1)S(1)}, bf16[384,128]{1,0:T(8,128)(2,1)}, u32[]{:S(2)}) copy-start(bf16[384,128]{1,0:T(8,128)(2,1)} %constant.4.clone.wh_ref) | copy-start | bytes 294916
  25.3 8.3 %copy-start.3 = (f32[8,16,128]{2,1,0:T(8,128)S(1)}, f32[8,16,128]{2,1,0:T(8,128)}, u32[]{:S(2)}) copy-start(f32[8,16,128]{2,1,0:T(8,128)} %param.8) | copy-start | bytes 196612
  25.3 1.4 %collective-permute-start.5 = (f32[16,16,128]{2,1,0:T(8,128)S(1)}, f32[16,16,128]{2,1,0:T(8,128)S(1)}, u32[]{:S(2)}, u32[]{:S(2)}) collective-permute-start(f32[16,16,128]{2,1,0:T(8,128)S(1)} %hand.1), channel_id=1, source_target_pairs={{0,1},{1,0},{2,3},{3,2},{4,5},{5,4},{6,7},{7,6},{8,9},{9,8},{10,11... | collective-permute-start | bytes 393224 | tf_op jit(solution)/shard_map/ppermute | solution.py:240
  27.0 8.3 %collective-permute-start.9 = (f32[192,128]{1,0:T(8,128)S(1)}, f32[192,128]{1,0:T(8,128)S(1)}, u32[]{:S(2)}, u32[]{:S(2)}) collective-permute-start(f32[192,128]{1,0:T(8,128)S(1)} %get-tuple-element.30), channel_id=1, source_target_pairs={{0,8},{8,16},{16,24},{24,0},{1,9},{9,17},{17,25},{25,1},{2,10},{10... | collective-permute-start | bytes 294920 | tf_op jit(solution)/shard_map/ppermute | solution.py:307
  28.7 6.6 %collective-permute-start.10 = (f32[192,128]{1,0:T(8,128)S(1)}, f32[192,128]{1,0:T(8,128)S(1)}, u32[]{:S(2)}, u32[]{:S(2)}) collective-permute-start(f32[192,128]{1,0:T(8,128)S(1)} %get-tuple-element.31), channel_id=1, source_target_pairs={{0,24},{8,0},{16,8},{24,16},{1,25},{9,1},{17,9},{25,17},{2,26},{10... | collective-permute-start | bytes 294920 | tf_op jit(solution)/shard_map/ppermute | solution.py:308
  29.9 5.3 %collective-permute-start.7 = (f32[6,16,128]{2,1,0:T(8,128)S(1)}, f32[6,16,128]{2,1,0:T(8,128)S(1)}, u32[]{:S(2)}, u32[]{:S(2)}) collective-permute-start(f32[6,16,128]{2,1,0:T(8,128)S(1)} %get-tuple-element.28), channel_id=1, source_target_pairs={{0,7},{1,2},{2,1},{3,4},{4,3},{5,6},{6,5},{7,0},{8,15},{9,10},{10,... | collective-permute-start | bytes 147464 | tf_op jit(solution)/shard_map/ppermute | solution.py:310
  31.6 3.7 %collective-permute-start.8 = (f32[6,16,128]{2,1,0:T(8,128)S(1)}, f32[6,16,128]{2,1,0:T(8,128)S(1)}, u32[]{:S(2)}, u32[]{:S(2)}) collective-permute-start(f32[6,16,128]{2,1,0:T(8,128)S(1)} %get-tuple-element.29), channel_id=1, source_target_pairs={{0,1},{1,0},{2,3},{3,2},{4,5},{5,4},{6,7},{7,6},{8,9},{9,8},{10,11... | collective-permute-start | bytes 147464 | tf_op jit(solution)/shard_map/ppermute | solution.py:240
  33.6 1.7 %copy-start.4 = (f32[16,128]{1,0:T(8,128)S(1)}, f32[16,128]{1,0:T(8,128)}, u32[]{:S(2)}) copy-start(f32[16,128]{1,0:T(8,128)} %rot_ref.1) | copy-start | bytes 24580
  36.1 28.6 %copy-start = (f32[16,8,16,128]{3,2,1,0:T(8,128)S(1)}, f32[16,8,16,128]{3,2,1,0:T(8,128)}, u32[]{:S(2)}) copy-start(f32[16,8,16,128]{3,2,1,0:T(8,128)} %param.7) | copy-start | bytes 3145732
  36.1 1.2 %collective-permute-start.11 = (f32[32,128]{1,0:T(8,128)S(1)}, f32[32,128]{1,0:T(8,128)S(1)}, u32[]{:S(2)}, u32[]{:S(2)}) collective-permute-start(f32[32,128]{1,0:T(8,128)S(1)} %get-tuple-element.32), channel_id=1, source_target_pairs={{0,1},{1,0},{2,3},{3,2},{4,5},{5,4},{6,7},{7,6},{8,9},{9,8},{10,11... | collective-permute-start | bytes 49160 | tf_op jit(solution)/shard_map/ppermute | solution.py:240
  37.3 3.7 %collective-permute-start.14 = (f32[16,128]{1,0:T(8,128)S(1)}, f32[16,128]{1,0:T(8,128)S(1)}, u32[]{:S(2)}, u32[]{:S(2)}) collective-permute-start(f32[16,128]{1,0:T(8,128)S(1)} %slice.23), channel_id=1, source_target_pairs={{0,8},{8,0},{16,24},{24,16},{1,9},{9,1},{17,25},{25,17},{2,10},{10... | collective-permute-start | bytes 24584 | tf_op jit(solution)/shard_map/ppermute | solution.py:240
  38.8 4.5 %collective-permute-start.13 = (f32[16,128]{1,0:T(8,128)S(1)}, f32[16,128]{1,0:T(8,128)S(1)}, u32[]{:S(2)}, u32[]{:S(2)}) collective-permute-start(f32[16,128]{1,0:T(8,128)S(1)} %slice.23), channel_id=1, source_target_pairs={{0,24},{8,16},{16,8},{24,0},{1,25},{9,17},{17,9},{25,1},{2,26},{10... | collective-permute-start | bytes 24584 | tf_op jit(solution)/shard_map/ppermute | solution.py:240
  40.5 3.7 %collective-permute-start.12 = (f32[16,128]{1,0:T(8,128)S(1)}, f32[16,128]{1,0:T(8,128)S(1)}, u32[]{:S(2)}, u32[]{:S(2)}) collective-permute-start(f32[16,128]{1,0:T(8,128)S(1)} %slice.23), channel_id=1, source_target_pairs={{0,16},{8,24},{16,0},{24,8},{1,17},{9,25},{17,1},{25,9},{2,18},{10... | collective-permute-start | bytes 24584 | tf_op jit(solution)/shard_map/ppermute | solution.py:240
  44.1 5.5 %collective-permute-start.17 = (f32[32,128]{1,0:T(8,128)S(1)}, f32[32,128]{1,0:T(8,128)S(1)}, u32[]{:S(2)}, u32[]{:S(2)}) collective-permute-start(f32[32,128]{1,0:T(8,128)S(1)} %dom.1.refs_0_), channel_id=1, source_target_pairs={{0,6},{1,7},{2,4},{3,5},{4,2},{5,3},{6,0},{7,1},{8,14},{9,15},{10,... | collective-permute-start | bytes 49160 | tf_op jit(solution)/shard_map/ppermute | solution.py:240
  46.7 4.6 %collective-permute-start.16 = (f32[32,128]{1,0:T(8,128)S(1)}, f32[32,128]{1,0:T(8,128)S(1)}, u32[]{:S(2)}, u32[]{:S(2)}) collective-permute-start(f32[32,128]{1,0:T(8,128)S(1)} %dom.1.refs_0_), channel_id=1, source_target_pairs={{0,4},{1,5},{2,6},{3,7},{4,0},{5,1},{6,2},{7,3},{8,12},{9,13},{10,... | collective-permute-start | bytes 49160 | tf_op jit(solution)/shard_map/ppermute | solution.py:240
  48.5 3.7 %collective-permute-start.15 = (f32[32,128]{1,0:T(8,128)S(1)}, f32[32,128]{1,0:T(8,128)S(1)}, u32[]{:S(2)}, u32[]{:S(2)}) collective-permute-start(f32[32,128]{1,0:T(8,128)S(1)} %dom.1.refs_0_), channel_id=1, source_target_pairs={{0,2},{1,3},{2,0},{3,1},{4,6},{5,7},{6,4},{7,5},{8,10},{9,11},{10,... | collective-permute-start | bytes 49160 | tf_op jit(solution)/shard_map/ppermute | solution.py:240
  52.5 10.4 %collective-permute-start.23 = (f32[16,16,128]{2,1,0:T(8,128)S(1)}, f32[16,16,128]{2,1,0:T(8,128)S(1)}, u32[]{:S(2)}, u32[]{:S(2)}) collective-permute-start(f32[16,16,128]{2,1,0:T(8,128)S(1)} %remove.1.refs_0_), channel_id=1, source_target_pairs={{0,4},{1,5},{2,6},{3,7},{4,0},{5,1},{6,2},{7,3},{8,12},{9,13},{10,... | collective-permute-start | bytes 393224 | tf_op jit(solution)/shard_map/ppermute | solution.py:240
  54.1 8.7 %collective-permute-start.21 = (f32[16,16,128]{2,1,0:T(8,128)S(1)}, f32[16,16,128]{2,1,0:T(8,128)S(1)}, u32[]{:S(2)}, u32[]{:S(2)}) collective-permute-start(f32[16,16,128]{2,1,0:T(8,128)S(1)} %remove.1.refs_0_), channel_id=1, source_target_pairs={{0,6},{1,7},{2,4},{3,5},{4,2},{5,3},{6,0},{7,1},{8,14},{9,15},{10,... | collective-permute-start | bytes 393224 | tf_op jit(solution)/shard_map/ppermute | solution.py:240
  56.3 7.1 %collective-permute-start.19 = (f32[16,16,128]{2,1,0:T(8,128)S(1)}, f32[16,16,128]{2,1,0:T(8,128)S(1)}, u32[]{:S(2)}, u32[]{:S(2)}) collective-permute-start(f32[16,16,128]{2,1,0:T(8,128)S(1)} %remove.1.refs_0_), channel_id=1, source_target_pairs={{0,2},{1,3},{2,0},{3,1},{4,6},{5,7},{6,4},{7,5},{8,10},{9,11},{10,... | collective-permute-start | bytes 393224 | tf_op jit(solution)/shard_map/ppermute | solution.py:240
  56.3 7.5 %collective-permute-start.18 = (f32[16,16,128]{2,1,0:T(8,128)S(1)}, f32[16,16,128]{2,1,0:T(8,128)S(1)}, u32[]{:S(2)}, u32[]{:S(2)}) collective-permute-start(f32[16,16,128]{2,1,0:T(8,128)S(1)} %remove.1.refs_0_), channel_id=1, source_target_pairs={{0,1},{1,0},{2,3},{3,2},{4,5},{5,4},{6,7},{7,6},{8,9},{9,8},{10,11... | collective-permute-start | bytes 393224 | tf_op jit(solution)/shard_map/ppermute | solution.py:240
  62.8 1.3 %collective-permute-start.24 = (f32[16,16,128]{2,1,0:T(8,128)S(1)}, f32[16,16,128]{2,1,0:T(8,128)S(1)}, u32[]{:S(2)}, u32[]{:S(2)}) collective-permute-start(f32[16,16,128]{2,1,0:T(8,128)S(1)} %collective-permute-done.23.refs_7_), channel_id=1, source_target_pairs={{0,1},{1,0},{2,3},{3,2},{4,5},{5,4},{6,7},{7,6},{8,9},{9,8},{10,11... | collective-permute-start | bytes 393224 | tf_op jit(solution)/shard_map/ppermute | solution.py:240
  62.8 1.5 %collective-permute-start.22 = (f32[16,16,128]{2,1,0:T(8,128)S(1)}, f32[16,16,128]{2,1,0:T(8,128)S(1)}, u32[]{:S(2)}, u32[]{:S(2)}) collective-permute-start(f32[16,16,128]{2,1,0:T(8,128)S(1)} %collective-permute-done.21.refs_5_), channel_id=1, source_target_pairs={{0,1},{1,0},{2,3},{3,2},{4,5},{5,4},{6,7},{7,6},{8,9},{9,8},{10,11... | collective-permute-start | bytes 393224 | tf_op jit(solution)/shard_map/ppermute | solution.py:240
  63.4 1.3 %collective-permute-start.20 = (f32[16,16,128]{2,1,0:T(8,128)S(1)}, f32[16,16,128]{2,1,0:T(8,128)S(1)}, u32[]{:S(2)}, u32[]{:S(2)}) collective-permute-start(f32[16,16,128]{2,1,0:T(8,128)S(1)} %collective-permute-done.19.refs_2_), channel_id=1, source_target_pairs={{0,1},{1,0},{2,3},{3,2},{4,5},{5,4},{6,7},{7,6},{8,9},{9,8},{10,11... | collective-permute-start | bytes 393224 | tf_op jit(solution)/shard_map/ppermute | solution.py:240

commit v5 on v3

--- a/solution.py
+++ b/solution.py
@@ -368,7 +368,7 @@
         name="mixing",
     )(*sums)
 
-    sequence = sorted(range(blocks), key=lambda k: (k >= half, -k if k >= half else k))
+    sequence = sorted(range(blocks), key=lambda k: (k > 1, k < half + 2, k >= half, -k if k >= half else k))
     gradient, updated = pl.pallas_call(
         functools.partial(update_kernel, blocks, sequence),
         out_shape=(shape(nb, cells, rows_z), shape(nb, cells, rows_z)),

time: 66.2 us -> 66.8 us (level)
  starting transfers between devices: 28.6 us -> 29.3 us
    ppermute x22, starting transfers between devices: 23.9 us -> 24.6 us  [swap(): return lax.ppermute(value, axis, [(i, i ^ k) for i in range(count)])]
  transfers between devices with their start and end apart: 25 -> 25, of which waited for: 16 -> 15; matrix products, arithmetic and copies ran while one was open for 0% -> 0% of each run, Pallas kernels for 1% -> 1%
where the time goes in v5:
time: 66.8 us; the launch traced here: 66.6 us
  waiting for transfers between devices  29.7 us (44%)
  starting transfers between devices  29.3 us (44%)
  Pallas kernels  5.49 us (8%)
  between operations  2.11 us (3%)
    ppermute x22, waiting for transfers between devices, swap(): return lax.ppermute(value, axis, [(i, i ^ k) for i in range(count)])  28.5 us
    ppermute x22, starting transfers between devices, swap(): return lax.ppermute(value, axis, [(i, i ^ k) for i in range(count)])  24.6 us
    pallas_call x1, Pallas kernels, per_device(): pl.pallas_call(functools.partial(update_kernel, blocks, sequence), out_sh...  1.77 us
    ppermute x1, starting transfers between devices, per_device(): x_before = lax.ppermute(last, 'dom', up(doms))  1.7 us
    ppermute x1, starting transfers between devices, per_device(): lax.ppermute(far, 'orb', [(o, (o + 2 * (o % 2) - 1) % blocks) for o in ra...  1.66 us
    pallas_call x1, Pallas kernels, per_device(): pl.pallas_call(functools.partial(pack_kernel, blocks), out_shape=[shape(2...  1.65 us
  transfers between devices with their start and end apart: 25, of which 15 were waited for; matrix products, arithmetic and copies ran while one was open for 0% of the time, Pallas kernels for 1%

profile of v5, /device:TPU:0, one launch (start us, length us, event | category | flops | bytes accessed | tf_op | source)
XLA Modules:
  0.0 66.6 jit_solution(4016766193438805905)
XLA Ops:
  0.6 1.7 %pack.1 = (f32[2,16,16,128]{3,2,1,0:T(8,128)S(1)}, f32[2,16,16,128]{3,2,1,0:T(8,128)S(1)}, f32[2,16,16,128]{3,2,1,0:T(8,128)S(1)}, f32[2,16,16,128]{3,2,1,0:T(8,128)S(1)}) custom-call(f32[16,128,128]{2,1,0:T(8,128)} %bitcast.12), custom_call_target="tpu_custom_call" | custom-call | tf_op jit(solution)/shard_map/pack/pallas_call | solution.py:268
  2.3 4.1 %collective-permute-start.2 = (f32[2,16,16,128]{3,2,1,0:T(8,128)S(1)}, f32[2,16,16,128]{3,2,1,0:T(8,128)S(1)}, u32[]{:S(2)}, u32[]{:S(2)}) collective-permute-start(f32[2,16,16,128]{3,2,1,0:T(8,128)S(1)} %get-tuple-element.21), channel_id=1, source_target_pairs={{0,4},{1,5},{2,6},{3,7},{4,0},{5,1},{6,2},{7,3},{8,12},{9,13},{10,... | collective-permute-start | bytes 786440 | tf_op jit(solution)/shard_map/ppermute | solution.py:240
  6.5 1.6 %collective-permute-start.4 = (f32[2,16,16,128]{3,2,1,0:T(8,128)S(1)}, f32[2,16,16,128]{3,2,1,0:T(8,128)S(1)}, u32[]{:S(2)}, u32[]{:S(2)}) collective-permute-start(f32[2,16,16,128]{3,2,1,0:T(8,128)S(1)} %get-tuple-element.22), channel_id=1, source_target_pairs={{0,2},{1,3},{2,0},{3,1},{4,6},{5,7},{6,4},{7,5},{8,10},{9,11},{10,... | collective-permute-start | bytes 786440 | tf_op jit(solution)/shard_map/ppermute | solution.py:240
  8.2 3.3 %collective-permute-start = (f32[16,16,128]{2,1,0:T(8,128)S(1)}, f32[16,16,128]{2,1,0:T(8,128)S(1)}, u32[]{:S(2)}, u32[]{:S(2)}) collective-permute-start(f32[16,16,128]{2,1,0:T(8,128)S(1)} %get-tuple-element.39), channel_id=1, source_target_pairs={{0,7},{1,6},{2,5},{3,4},{4,3},{5,2},{6,1},{7,0},{8,15},{9,14},{10,... | collective-permute-start | bytes 393224 | tf_op jit(solution)/shard_map/ppermute | solution.py:240
  12.8 7.2 %collective-permute-done.2.refs_5_ = f32[2,16,16,128]{3,2,1,0:T(8,128)S(1)} collective-permute-done((f32[2,16,16,128]{3,2,1,0:T(8,128)S(1)}, f32[2,16,16,128]{3,2,1,0:T(8,128)S(1)}, u32[]{:S(2)}, u32[]{:S(2)}) %collective-permute-start.2) | collective-permute-done | bytes 262176 | tf_op jit(solution)/shard_map/ppermute | solution.py:240
  20.1 5.1 %collective-permute-done.4.pair_ref.refs_6_ = f32[2,16,16,128]{3,2,1,0:T(8,128)S(1)} collective-permute-done((f32[2,16,16,128]{3,2,1,0:T(8,128)S(1)}, f32[2,16,16,128]{3,2,1,0:T(8,128)S(1)}, u32[]{:S(2)}, u32[]{:S(2)}) %collective-permute-start.4) | collective-permute-done | bytes 262176 | tf_op jit(solution)/shard_map/ppermute | solution.py:240
  25.4 1.3 %collective-permute-done.5.refs_3_ = f32[16,16,128]{2,1,0:T(8,128)S(1)} collective-permute-done((f32[16,16,128]{2,1,0:T(8,128)S(1)}, f32[16,16,128]{2,1,0:T(8,128)S(1)}, u32[]{:S(2)}, u32[]{:S(2)}) %collective-permute-start.5) | collective-permute-done | bytes 131104 | tf_op jit(solution)/shard_map/ppermute | solution.py:240
  27.0 1.7 %collective-permute-start.9 = (f32[192,128]{1,0:T(8,128)S(1)}, f32[192,128]{1,0:T(8,128)S(1)}, u32[]{:S(2)}, u32[]{:S(2)}) collective-permute-start(f32[192,128]{1,0:T(8,128)S(1)} %get-tuple-element.30), channel_id=1, source_target_pairs={{0,8},{8,16},{16,24},{24,0},{1,9},{9,17},{17,25},{25,1},{2,10},{10... | collective-permute-start | bytes 294920 | tf_op jit(solution)/shard_map/ppermute | solution.py:307
  28.7 1.3 %collective-permute-start.10 = (f32[192,128]{1,0:T(8,128)S(1)}, f32[192,128]{1,0:T(8,128)S(1)}, u32[]{:S(2)}, u32[]{:S(2)}) collective-permute-start(f32[192,128]{1,0:T(8,128)S(1)} %get-tuple-element.31), channel_id=1, source_target_pairs={{0,24},{8,0},{16,8},{24,16},{1,25},{9,1},{17,9},{25,17},{2,26},{10... | collective-permute-start | bytes 294920 | tf_op jit(solution)/shard_map/ppermute | solution.py:308
  29.9 1.7 %collective-permute-start.7 = (f32[6,16,128]{2,1,0:T(8,128)S(1)}, f32[6,16,128]{2,1,0:T(8,128)S(1)}, u32[]{:S(2)}, u32[]{:S(2)}) collective-permute-start(f32[6,16,128]{2,1,0:T(8,128)S(1)} %get-tuple-element.28), channel_id=1, source_target_pairs={{0,7},{1,2},{2,1},{3,4},{4,3},{5,6},{6,5},{7,0},{8,15},{9,10},{10,... | collective-permute-start | bytes 147464 | tf_op jit(solution)/shard_map/ppermute | solution.py:310
  31.6 2.0 %collective-permute-start.8 = (f32[6,16,128]{2,1,0:T(8,128)S(1)}, f32[6,16,128]{2,1,0:T(8,128)S(1)}, u32[]{:S(2)}, u32[]{:S(2)}) collective-permute-start(f32[6,16,128]{2,1,0:T(8,128)S(1)} %get-tuple-element.29), channel_id=1, source_target_pairs={{0,1},{1,0},{2,3},{3,2},{4,5},{5,4},{6,7},{7,6},{8,9},{9,8},{10,11... | collective-permute-start | bytes 147464 | tf_op jit(solution)/shard_map/ppermute | solution.py:240
  33.7 0.4 split.1
  34.1 1.2 %collective-permute-done.7.far_ref = f32[6,16,128]{2,1,0:T(8,128)S(1)} collective-permute-done((f32[6,16,128]{2,1,0:T(8,128)S(1)}, f32[6,16,128]{2,1,0:T(8,128)S(1)}, u32[]{:S(2)}, u32[]{:S(2)}) %collective-permute-start.7) | collective-permute-done | bytes 49184 | tf_op jit(solution)/shard_map/ppermute | solution.py:310
  35.3 0.8 %project.1 = (f32[16,16,128]{2,1,0:T(8,128)S(1)}, f32[32,128]{1,0:T(8,128)S(1)}) custom-call(s32[1]{0:T(128)S(6)} %copy.10.owner_ref, f32[16,128]{1,0:T(8,128)S(1)} %copy-done.4, bf16[128,2048]{1,0:T(8,128)(2,1)S(1)} %get-tuple-element.25.xh_ref, bf16[128,2048]{1,0:T(8,128)(2,1)S(1)} %get-tuple-element.26.xl_ref, ...), custom_call_target="tpu_custom_call" | custom-call | tf_op jit(solution)/shard_map/project/pallas_call | solution.py:325
  36.4 0.9 %collective-permute-done.11 = f32[32,128]{1,0:T(8,128)S(1)} collective-permute-done((f32[32,128]{1,0:T(8,128)S(1)}, f32[32,128]{1,0:T(8,128)S(1)}, u32[]{:S(2)}, u32[]{:S(2)}) %collective-permute-start.11) | collective-permute-done | bytes 16416 | tf_op jit(solution)/shard_map/ppermute | solution.py:240
  37.3 1.7 %collective-permute-start.14 = (f32[16,128]{1,0:T(8,128)S(1)}, f32[16,128]{1,0:T(8,128)S(1)}, u32[]{:S(2)}, u32[]{:S(2)}) collective-permute-start(f32[16,128]{1,0:T(8,128)S(1)} %slice.23), channel_id=1, source_target_pairs={{0,24},{8,16},{16,8},{24,0},{1,25},{9,17},{17,9},{25,1},{2,26},{10... | collective-permute-start | bytes 24584 | tf_op jit(solution)/shard_map/ppermute | solution.py:240
  39.0 1.4 %collective-permute-start.13 = (f32[16,128]{1,0:T(8,128)S(1)}, f32[16,128]{1,0:T(8,128)S(1)}, u32[]{:S(2)}, u32[]{:S(2)}) collective-permute-start(f32[16,128]{1,0:T(8,128)S(1)} %slice.23), channel_id=1, source_target_pairs={{0,8},{8,0},{16,24},{24,16},{1,9},{9,1},{17,25},{25,17},{2,10},{10... | collective-permute-start | bytes 24584 | tf_op jit(solution)/shard_map/ppermute | solution.py:240
  40.8 1.1 %collective-permute-done.14.refs_2_ = f32[16,128]{1,0:T(8,128)S(1)} collective-permute-done((f32[16,128]{1,0:T(8,128)S(1)}, f32[16,128]{1,0:T(8,128)S(1)}, u32[]{:S(2)}, u32[]{:S(2)}) %collective-permute-start.14) | collective-permute-done | bytes 8224 | tf_op jit(solution)/shard_map/ppermute | solution.py:240
  41.9 0.8 %collective-permute-done.13.refs_1_ = f32[16,128]{1,0:T(8,128)S(1)} collective-permute-done((f32[16,128]{1,0:T(8,128)S(1)}, f32[16,128]{1,0:T(8,128)S(1)}, u32[]{:S(2)}, u32[]{:S(2)}) %collective-permute-start.13) | collective-permute-done | bytes 8224 | tf_op jit(solution)/shard_map/ppermute | solution.py:240
  42.7 1.4 %collective-permute-done.12.refs_0_ = f32[16,128]{1,0:T(8,128)S(1)} collective-permute-done((f32[16,128]{1,0:T(8,128)S(1)}, f32[16,128]{1,0:T(8,128)S(1)}, u32[]{:S(2)}, u32[]{:S(2)}) %collective-permute-start.12) | collective-permute-done | bytes 8224 | tf_op jit(solution)/shard_map/ppermute | solution.py:240
  44.1 2.6 %collective-permute-start.17 = (f32[32,128]{1,0:T(8,128)S(1)}, f32[32,128]{1,0:T(8,128)S(1)}, u32[]{:S(2)}, u32[]{:S(2)}) collective-permute-start(f32[32,128]{1,0:T(8,128)S(1)} %dom.1.refs_0_), channel_id=1, source_target_pairs={{0,6},{1,7},{2,4},{3,5},{4,2},{5,3},{6,0},{7,1},{8,14},{9,15},{10,... | collective-permute-start | bytes 49160 | tf_op jit(solution)/shard_map/ppermute | solution.py:240
  46.7 1.3 %collective-permute-start.16 = (f32[32,128]{1,0:T(8,128)S(1)}, f32[32,128]{1,0:T(8,128)S(1)}, u32[]{:S(2)}, u32[]{:S(2)}) collective-permute-start(f32[32,128]{1,0:T(8,128)S(1)} %dom.1.refs_0_), channel_id=1, source_target_pairs={{0,4},{1,5},{2,6},{3,7},{4,0},{5,1},{6,2},{7,3},{8,12},{9,13},{10,... | collective-permute-start | bytes 49160 | tf_op jit(solution)/shard_map/ppermute | solution.py:240
  48.0 0.5 collective-permute-start.15
  48.5 1.3 %collective-permute-done.17.refs_3_ = f32[32,128]{1,0:T(8,128)S(1)} collective-permute-done((f32[32,128]{1,0:T(8,128)S(1)}, f32[32,128]{1,0:T(8,128)S(1)}, u32[]{:S(2)}, u32[]{:S(2)}) %collective-permute-start.17) | collective-permute-done | bytes 16416 | tf_op jit(solution)/shard_map/ppermute | solution.py:240
  49.8 1.6 %collective-permute-done.16.refs_2_ = f32[32,128]{1,0:T(8,128)S(1)} collective-permute-done((f32[32,128]{1,0:T(8,128)S(1)}, f32[32,128]{1,0:T(8,128)S(1)}, u32[]{:S(2)}, u32[]{:S(2)}) %collective-permute-start.16) | collective-permute-done | bytes 16416 | tf_op jit(solution)/shard_map/ppermute | solution.py:240
  52.0 1.7 %collective-permute-start.23 = (f32[16,16,128]{2,1,0:T(8,128)S(1)}, f32[16,16,128]{2,1,0:T(8,128)S(1)}, u32[]{:S(2)}, u32[]{:S(2)}) collective-permute-start(f32[16,16,128]{2,1,0:T(8,128)S(1)} %remove.1.refs_0_), channel_id=1, source_target_pairs={{0,4},{1,5},{2,6},{3,7},{4,0},{5,1},{6,2},{7,3},{8,12},{9,13},{10,... | collective-permute-start | bytes 393224 | tf_op jit(solution)/shard_map/ppermute | solution.py:240
  53.7 1.8 %collective-permute-start.21 = (f32[16,16,128]{2,1,0:T(8,128)S(1)}, f32[16,16,128]{2,1,0:T(8,128)S(1)}, u32[]{:S(2)}, u32[]{:S(2)}) collective-permute-start(f32[16,16,128]{2,1,0:T(8,128)S(1)} %remove.1.refs_0_), channel_id=1, source_target_pairs={{0,2},{1,3},{2,0},{3,1},{4,6},{5,7},{6,4},{7,5},{8,10},{9,11},{10,... | collective-permute-start | bytes 393224 | tf_op jit(solution)/shard_map/ppermute | solution.py:240
  55.4 1.0 %collective-permute-start.19 = (f32[16,16,128]{2,1,0:T(8,128)S(1)}, f32[16,16,128]{2,1,0:T(8,128)S(1)}, u32[]{:S(2)}, u32[]{:S(2)}) collective-permute-start(f32[16,16,128]{2,1,0:T(8,128)S(1)} %remove.1.refs_0_), channel_id=1, source_target_pairs={{0,6},{1,7},{2,4},{3,5},{4,2},{5,3},{6,0},{7,1},{8,14},{9,15},{10,... | collective-permute-start | bytes 393224 | tf_op jit(solution)/shard_map/ppermute | solution.py:240
  56.4 6.5 %collective-permute-done.23.refs_7_ = f32[16,16,128]{2,1,0:T(8,128)S(1)} collective-permute-done((f32[16,16,128]{2,1,0:T(8,128)S(1)}, f32[16,16,128]{2,1,0:T(8,128)S(1)}, u32[]{:S(2)}, u32[]{:S(2)}) %collective-permute-start.23) | collective-permute-done | bytes 131104 | tf_op jit(solution)/shard_map/ppermute | solution.py:240
  63.0 0.5 collective-permute-start.22
  63.5 0.4 mixing.1
  64.8 1.8 %update.1 = (f32[16,128,128]{2,1,0:T(8,128)}, f32[16,128,128]{2,1,0:T(8,128)}) custom-call(bf16[128,128]{1,0:T(8,128)(2,1)S(1)} %get-tuple-element.33.wh_ref, bf16[128,128]{1,0:T(8,128)(2,1)S(1)} %get-tuple-element.34.wl_ref, f32[16,128,128]{2,1,0:T(8,128)S(1)} %bitcast.13, f32[16,16,128]{2,1,0:T(8,128)S(1)} %remove.1.refs_0_, ...), custom_call_target="tpu_custom_call" | custom-call | tf_op jit(solution)/shard_map/update/pallas_call | solution.py:372
  (42 shorter events, 2.9 us)
Async XLA Ops:
  2.3 17.8 %collective-permute-start.2 = (f32[2,16,16,128]{3,2,1,0:T(8,128)S(1)}, f32[2,16,16,128]{3,2,1,0:T(8,128)S(1)}, u32[]{:S(2)}, u32[]{:S(2)}) collective-permute-start(f32[2,16,16,128]{3,2,1,0:T(8,128)S(1)} %get-tuple-element.21), channel_id=1, source_target_pairs={{0,4},{1,5},{2,6},{3,7},{4,0},{5,1},{6,2},{7,3},{8,12},{9,13},{10,... | collective-permute-start | bytes 786440 | tf_op jit(solution)/shard_map/ppermute | solution.py:240
  6.4 19.0 %collective-permute-start.6 = (f32[16,16,128]{2,1,0:T(8,128)S(1)}, f32[16,16,128]{2,1,0:T(8,128)S(1)}, u32[]{:S(2)}, u32[]{:S(2)}) collective-permute-start(f32[16,16,128]{2,1,0:T(8,128)S(1)} %slice_bitcast_fusion.1), channel_id=1, source_target_pairs={{0,1},{1,0},{2,3},{3,2},{4,5},{5,4},{6,7},{7,6},{8,9},{9,8},{10,11... | collective-permute-start | bytes 393224 | tf_op jit(solution)/shard_map/ppermute | solution.py:240
  6.5 18.8 %collective-permute-start.4 = (f32[2,16,16,128]{3,2,1,0:T(8,128)S(1)}, f32[2,16,16,128]{3,2,1,0:T(8,128)S(1)}, u32[]{:S(2)}, u32[]{:S(2)}) collective-permute-start(f32[2,16,16,128]{3,2,1,0:T(8,128)S(1)} %get-tuple-element.22), channel_id=1, source_target_pairs={{0,2},{1,3},{2,0},{3,1},{4,6},{5,7},{6,4},{7,5},{8,10},{9,11},{10,... | collective-permute-start | bytes 786440 | tf_op jit(solution)/shard_map/ppermute | solution.py:240
  8.1 17.3 %collective-permute-start.1 = (f32[16,16,128]{2,1,0:T(8,128)S(1)}, f32[16,16,128]{2,1,0:T(8,128)S(1)}, u32[]{:S(2)}, u32[]{:S(2)}) collective-permute-start(f32[16,16,128]{2,1,0:T(8,128)S(1)} %get-tuple-element.38), channel_id=1, source_target_pairs={{0,6},{1,7},{2,4},{3,5},{4,2},{5,3},{6,0},{7,1},{8,14},{9,15},{10,... | collective-permute-start | bytes 393224 | tf_op jit(solution)/shard_map/ppermute | solution.py:240
  8.2 17.2 %collective-permute-start = (f32[16,16,128]{2,1,0:T(8,128)S(1)}, f32[16,16,128]{2,1,0:T(8,128)S(1)}, u32[]{:S(2)}, u32[]{:S(2)}) collective-permute-start(f32[16,16,128]{2,1,0:T(8,128)S(1)} %get-tuple-element.39), channel_id=1, source_target_pairs={{0,7},{1,6},{2,5},{3,4},{4,3},{5,2},{6,1},{7,0},{8,15},{9,14},{10,... | collective-permute-start | bytes 393224 | tf_op jit(solution)/shard_map/ppermute | solution.py:240
  20.1 5.4 %collective-permute-start.3 = (f32[16,16,128]{2,1,0:T(8,128)S(1)}, f32[16,16,128]{2,1,0:T(8,128)S(1)}, u32[]{:S(2)}, u32[]{:S(2)}) collective-permute-start(f32[16,16,128]{2,1,0:T(8,128)S(1)} %slice_bitcast_fusion), channel_id=1, source_target_pairs={{0,1},{1,0},{2,3},{3,2},{4,5},{5,4},{6,7},{7,6},{8,9},{9,8},{10,11... | collective-permute-start | bytes 393224 | tf_op jit(solution)/shard_map/ppermute | solution.py:240
  25.3 8.4 %copy-start.1 = (bf16[384,128]{1,0:T(8,128)(2,1)S(1)}, bf16[384,128]{1,0:T(8,128)(2,1)}, u32[]{:S(2)}) copy-start(bf16[384,128]{1,0:T(8,128)(2,1)} %constant.5.clone.wl_ref) | copy-start | bytes 294916
  25.3 8.3 %copy-start.2 = (bf16[384,128]{1,0:T(8,128)(2,1)S(1)}, bf16[384,128]{1,0:T(8,128)(2,1)}, u32[]{:S(2)}) copy-start(bf16[384,128]{1,0:T(8,128)(2,1)} %constant.4.clone.wh_ref) | copy-start | bytes 294916
  25.3 8.3 %copy-start.3 = (f32[8,16,128]{2,1,0:T(8,128)S(1)}, f32[8,16,128]{2,1,0:T(8,128)}, u32[]{:S(2)}) copy-start(f32[8,16,128]{2,1,0:T(8,128)} %param.8) | copy-start | bytes 196612
  25.3 1.4 %collective-permute-start.5 = (f32[16,16,128]{2,1,0:T(8,128)S(1)}, f32[16,16,128]{2,1,0:T(8,128)S(1)}, u32[]{:S(2)}, u32[]{:S(2)}) collective-permute-start(f32[16,16,128]{2,1,0:T(8,128)S(1)} %hand.1), channel_id=1, source_target_pairs={{0,1},{1,0},{2,3},{3,2},{4,5},{5,4},{6,7},{7,6},{8,9},{9,8},{10,11... | collective-permute-start | bytes 393224 | tf_op jit(solution)/shard_map/ppermute | solution.py:240
  27.0 8.3 %collective-permute-start.9 = (f32[192,128]{1,0:T(8,128)S(1)}, f32[192,128]{1,0:T(8,128)S(1)}, u32[]{:S(2)}, u32[]{:S(2)}) collective-permute-start(f32[192,128]{1,0:T(8,128)S(1)} %get-tuple-element.30), channel_id=1, source_target_pairs={{0,8},{8,16},{16,24},{24,0},{1,9},{9,17},{17,25},{25,1},{2,10},{10... | collective-permute-start | bytes 294920 | tf_op jit(solution)/shard_map/ppermute | solution.py:307
  28.7 6.6 %collective-permute-start.10 = (f32[192,128]{1,0:T(8,128)S(1)}, f32[192,128]{1,0:T(8,128)S(1)}, u32[]{:S(2)}, u32[]{:S(2)}) collective-permute-start(f32[192,128]{1,0:T(8,128)S(1)} %get-tuple-element.31), channel_id=1, source_target_pairs={{0,24},{8,0},{16,8},{24,16},{1,25},{9,1},{17,9},{25,17},{2,26},{10... | collective-permute-start | bytes 294920 | tf_op jit(solution)/shard_map/ppermute | solution.py:308
  29.9 5.3 %collective-permute-start.7 = (f32[6,16,128]{2,1,0:T(8,128)S(1)}, f32[6,16,128]{2,1,0:T(8,128)S(1)}, u32[]{:S(2)}, u32[]{:S(2)}) collective-permute-start(f32[6,16,128]{2,1,0:T(8,128)S(1)} %get-tuple-element.28), channel_id=1, source_target_pairs={{0,7},{1,2},{2,1},{3,4},{4,3},{5,6},{6,5},{7,0},{8,15},{9,10},{10,... | collective-permute-start | bytes 147464 | tf_op jit(solution)/shard_map/ppermute | solution.py:310
  31.6 3.7 %collective-permute-start.8 = (f32[6,16,128]{2,1,0:T(8,128)S(1)}, f32[6,16,128]{2,1,0:T(8,128)S(1)}, u32[]{:S(2)}, u32[]{:S(2)}) collective-permute-start(f32[6,16,128]{2,1,0:T(8,128)S(1)} %get-tuple-element.29), channel_id=1, source_target_pairs={{0,1},{1,0},{2,3},{3,2},{4,5},{5,4},{6,7},{7,6},{8,9},{9,8},{10,11... | collective-permute-start | bytes 147464 | tf_op jit(solution)/shard_map/ppermute | solution.py:240
  33.7 1.6 %copy-start.4 = (f32[16,128]{1,0:T(8,128)S(1)}, f32[16,128]{1,0:T(8,128)}, u32[]{:S(2)}) copy-start(f32[16,128]{1,0:T(8,128)} %rot_ref.1) | copy-start | bytes 24580
  36.1 28.7 %copy-start = (f32[16,8,16,128]{3,2,1,0:T(8,128)S(1)}, f32[16,8,16,128]{3,2,1,0:T(8,128)}, u32[]{:S(2)}) copy-start(f32[16,8,16,128]{3,2,1,0:T(8,128)} %param.7) | copy-start | bytes 3145732
  36.1 1.2 %collective-permute-start.11 = (f32[32,128]{1,0:T(8,128)S(1)}, f32[32,128]{1,0:T(8,128)S(1)}, u32[]{:S(2)}, u32[]{:S(2)}) collective-permute-start(f32[32,128]{1,0:T(8,128)S(1)} %get-tuple-element.32), channel_id=1, source_target_pairs={{0,1},{1,0},{2,3},{3,2},{4,5},{5,4},{6,7},{7,6},{8,9},{9,8},{10,11... | collective-permute-start | bytes 49160 | tf_op jit(solution)/shard_map/ppermute | solution.py:240
  37.3 4.5 %collective-permute-start.14 = (f32[16,128]{1,0:T(8,128)S(1)}, f32[16,128]{1,0:T(8,128)S(1)}, u32[]{:S(2)}, u32[]{:S(2)}) collective-permute-start(f32[16,128]{1,0:T(8,128)S(1)} %slice.23), channel_id=1, source_target_pairs={{0,24},{8,16},{16,8},{24,0},{1,25},{9,17},{17,9},{25,1},{2,26},{10... | collective-permute-start | bytes 24584 | tf_op jit(solution)/shard_map/ppermute | solution.py:240
  39.0 3.7 %collective-permute-start.13 = (f32[16,128]{1,0:T(8,128)S(1)}, f32[16,128]{1,0:T(8,128)S(1)}, u32[]{:S(2)}, u32[]{:S(2)}) collective-permute-start(f32[16,128]{1,0:T(8,128)S(1)} %slice.23), channel_id=1, source_target_pairs={{0,8},{8,0},{16,24},{24,16},{1,9},{9,1},{17,25},{25,17},{2,10},{10... | collective-permute-start | bytes 24584 | tf_op jit(solution)/shard_map/ppermute | solution.py:240
  40.5 3.7 %collective-permute-start.12 = (f32[16,128]{1,0:T(8,128)S(1)}, f32[16,128]{1,0:T(8,128)S(1)}, u32[]{:S(2)}, u32[]{:S(2)}) collective-permute-start(f32[16,128]{1,0:T(8,128)S(1)} %slice.23), channel_id=1, source_target_pairs={{0,16},{8,24},{16,0},{24,8},{1,17},{9,25},{17,1},{25,9},{2,18},{10... | collective-permute-start | bytes 24584 | tf_op jit(solution)/shard_map/ppermute | solution.py:240
  44.1 5.6 %collective-permute-start.17 = (f32[32,128]{1,0:T(8,128)S(1)}, f32[32,128]{1,0:T(8,128)S(1)}, u32[]{:S(2)}, u32[]{:S(2)}) collective-permute-start(f32[32,128]{1,0:T(8,128)S(1)} %dom.1.refs_0_), channel_id=1, source_target_pairs={{0,6},{1,7},{2,4},{3,5},{4,2},{5,3},{6,0},{7,1},{8,14},{9,15},{10,... | collective-permute-start | bytes 49160 | tf_op jit(solution)/shard_map/ppermute | solution.py:240
  46.7 4.6 %collective-permute-start.16 = (f32[32,128]{1,0:T(8,128)S(1)}, f32[32,128]{1,0:T(8,128)S(1)}, u32[]{:S(2)}, u32[]{:S(2)}) collective-permute-start(f32[32,128]{1,0:T(8,128)S(1)} %dom.1.refs_0_), channel_id=1, source_target_pairs={{0,4},{1,5},{2,6},{3,7},{4,0},{5,1},{6,2},{7,3},{8,12},{9,13},{10,... | collective-permute-start | bytes 49160 | tf_op jit(solution)/shard_map/ppermute | solution.py:240
  48.0 3.7 %collective-permute-start.15 = (f32[32,128]{1,0:T(8,128)S(1)}, f32[32,128]{1,0:T(8,128)S(1)}, u32[]{:S(2)}, u32[]{:S(2)}) collective-permute-start(f32[32,128]{1,0:T(8,128)S(1)} %dom.1.refs_0_), channel_id=1, source_target_pairs={{0,2},{1,3},{2,0},{3,1},{4,6},{5,7},{6,4},{7,5},{8,10},{9,11},{10,... | collective-permute-start | bytes 49160 | tf_op jit(solution)/shard_map/ppermute | solution.py:240
  52.0 11.0 %collective-permute-start.23 = (f32[16,16,128]{2,1,0:T(8,128)S(1)}, f32[16,16,128]{2,1,0:T(8,128)S(1)}, u32[]{:S(2)}, u32[]{:S(2)}) collective-permute-start(f32[16,16,128]{2,1,0:T(8,128)S(1)} %remove.1.refs_0_), channel_id=1, source_target_pairs={{0,4},{1,5},{2,6},{3,7},{4,0},{5,1},{6,2},{7,3},{8,12},{9,13},{10,... | collective-permute-start | bytes 393224 | tf_op jit(solution)/shard_map/ppermute | solution.py:240
  53.7 9.3 %collective-permute-start.21 = (f32[16,16,128]{2,1,0:T(8,128)S(1)}, f32[16,16,128]{2,1,0:T(8,128)S(1)}, u32[]{:S(2)}, u32[]{:S(2)}) collective-permute-start(f32[16,16,128]{2,1,0:T(8,128)S(1)} %remove.1.refs_0_), channel_id=1, source_target_pairs={{0,2},{1,3},{2,0},{3,1},{4,6},{5,7},{6,4},{7,5},{8,10},{9,11},{10,... | collective-permute-start | bytes 393224 | tf_op jit(solution)/shard_map/ppermute | solution.py:240
  55.4 8.0 %collective-permute-start.19 = (f32[16,16,128]{2,1,0:T(8,128)S(1)}, f32[16,16,128]{2,1,0:T(8,128)S(1)}, u32[]{:S(2)}, u32[]{:S(2)}) collective-permute-start(f32[16,16,128]{2,1,0:T(8,128)S(1)} %remove.1.refs_0_), channel_id=1, source_target_pairs={{0,6},{1,7},{2,4},{3,5},{4,2},{5,3},{6,0},{7,1},{8,14},{9,15},{10,... | collective-permute-start | bytes 393224 | tf_op jit(solution)/shard_map/ppermute | solution.py:240
  56.4 7.5 %collective-permute-start.18 = (f32[16,16,128]{2,1,0:T(8,128)S(1)}, f32[16,16,128]{2,1,0:T(8,128)S(1)}, u32[]{:S(2)}, u32[]{:S(2)}) collective-permute-start(f32[16,16,128]{2,1,0:T(8,128)S(1)} %remove.1.refs_0_), channel_id=1, source_target_pairs={{0,1},{1,0},{2,3},{3,2},{4,5},{5,4},{6,7},{7,6},{8,9},{9,8},{10,11... | collective-permute-start | bytes 393224 | tf_op jit(solution)/shard_map/ppermute | solution.py:240
  63.0 1.3 %collective-permute-start.24 = (f32[16,16,128]{2,1,0:T(8,128)S(1)}, f32[16,16,128]{2,1,0:T(8,128)S(1)}, u32[]{:S(2)}, u32[]{:S(2)}) collective-permute-start(f32[16,16,128]{2,1,0:T(8,128)S(1)} %collective-permute-done.23.refs_7_), channel_id=1, source_target_pairs={{0,1},{1,0},{2,3},{3,2},{4,5},{5,4},{6,7},{7,6},{8,9},{9,8},{10,11... | collective-permute-start | bytes 393224 | tf_op jit(solution)/shard_map/ppermute | solution.py:240
  63.0 1.5 %collective-permute-start.22 = (f32[16,16,128]{2,1,0:T(8,128)S(1)}, f32[16,16,128]{2,1,0:T(8,128)S(1)}, u32[]{:S(2)}, u32[]{:S(2)}) collective-permute-start(f32[16,16,128]{2,1,0:T(8,128)S(1)} %collective-permute-done.21.refs_4_), channel_id=1, source_target_pairs={{0,1},{1,0},{2,3},{3,2},{4,5},{5,4},{6,7},{7,6},{8,9},{9,8},{10,11... | collective-permute-start | bytes 393224 | tf_op jit(solution)/shard_map/ppermute | solution.py:240
  63.5 1.3 %collective-permute-start.20 = (f32[16,16,128]{2,1,0:T(8,128)S(1)}, f32[16,16,128]{2,1,0:T(8,128)S(1)}, u32[]{:S(2)}, u32[]{:S(2)}) collective-permute-start(f32[16,16,128]{2,1,0:T(8,128)S(1)} %collective-permute-done.19.refs_3_), channel_id=1, source_target_pairs={{0,1},{1,0},{2,3},{3,2},{4,5},{5,4},{6,7},{7,6},{8,9},{9,8},{10,11... | collective-permute-start | bytes 393224 | tf_op jit(solution)/shard_map/ppermute | solution.py:240
